TPU v7x, 32 devices: a whole 2x2x4 slice. The times are simulated.
32 devices in a mesh: dp: 4 (over y, core), seq: 8 (over z, x).
Axes of the slice: x: 2, y: 2, z: 4, core: 2. Of those that a mesh axis runs over, the one named last changes fastest.
Arguments:
- hidden_in: float32 [8, 2048, 1024], P('dp', 'seq'), may hold values from -6 to 6
- lengths: int32 [8], P('dp'), may hold values from 512 to 2048, as said below
- norm_gain: float32 [1024], replicated, may hold values from 0.1 to 1.9
- in_weight: float32 [4489216], P(('dp', 'seq')), may hold values from -0.1875 to 0.1875
- conv_weight: float32 [9216], P(('dp', 'seq')), may hold values from -3 to 3
- conv_bias: float32 [2304], P(('dp', 'seq')), may hold values from -3 to 3
- dt_bias: float32 [32], replicated, may hold values from -9 to -1
- a_log: float32 [32], replicated, may hold values from -6 to -1
- skip_gain: float32 [32], replicated, may hold values from 0.5 to 2
- gated_gain: float32 [2048], replicated, may hold values from 0.1 to 1.9
- out_weight: float32 [2097152], P(('dp', 'seq')), may hold values from -0.125 to 0.125
- cotangent: float32 [8, 2048, 1024], P('dp', 'seq'), may hold values from -6 to 6
Outputs:
- output: float32 [8, 2048, 1024], P('dp', 'seq')
- grad_input: float32 [8, 2048, 1024], P('dp', 'seq')
- grad_norm_gain: float32 [1024], replicated
- grad_in_weight: float32 [4489216], P(('dp', 'seq'))
- grad_conv_weight: float32 [9216], P(('dp', 'seq'))
- grad_conv_bias: float32 [2304], P(('dp', 'seq'))
- grad_dt_bias: float32 [32], replicated
- grad_a_log: float32 [32], replicated
- grad_skip_gain: float32 [32], replicated
- grad_gated_gain: float32 [2048], replicated
- grad_out_weight: float32 [2097152], P(('dp', 'seq'))
Inputs may be any that keep to these rules, and one draw needn't show every extreme that they name: `lengths`: of the 2 sequences of each index of dp, one, drawn from the seed, fills all 2048 slots; the others are drawn evenly.
All inputs are finite; a program needn't handle non-finite values.
Results may differ from a plain program's by a relative error of at most 0.0003.
Values sent between devices are 32-bit elements; how exact they have to be, the bound alone decides.
No kernel may reach another device: no remote copies, remote signals or barrier semaphores. Data moves between devices by JAX's collectives and lax.ppermute only.
A program may use at most 256 MiB of HBM per device.

v0:
```python
import jax
import jax.numpy as jnp
from jax import lax
from jax.sharding import PartitionSpec as P

DI = 2048
HEADS = 32
HDIM = 64
STATE = 128
CONV = 4


epsilon = 1e-05
highest = lax.Precision.HIGHEST


def from_behind(block, axis, distance):
    devices = range(lax.axis_size(axis))
    route = [(i - distance, i) for i in devices if i - distance in devices]
    return lax.ppermute(block, axis, route)


def carried_in(value, axis, combine, identity, reverse):
    count, index = (lax.axis_size(axis), lax.axis_index(axis))
    everything = jax.tree.map(lambda part: lax.all_gather(part, axis), value)
    start = jax.tree.map(
        lambda part, zero: jnp.broadcast_to(jnp.asarray(zero, part.dtype), part.shape),
        value,
        identity,
    )

    def step(k, before):
        at = count - 1 - k if reverse else k
        reached = at > index if reverse else at < index
        new = combine(before, jax.tree.map(lambda part: part[at], everything))
        return jax.tree.map(lambda a, b: jnp.where(reached, a, b), new, before)

    return lax.fori_loop(0, count, step, start)


def rms_scale(values, gain):
    return values * lax.rsqrt(jnp.mean(values * values, axis=-1, keepdims=True) + epsilon) * gain


def prepare(conv_in, edge_rows, rate_in, taps, conv_bias, dt_bias, a_log):
    seq_count, piece_rows, mixed_width = conv_in.shape
    padded = jnp.concatenate([edge_rows, conv_in], axis=1)
    conv_out = conv_bias + taps[0] * padded[:, 0:piece_rows]
    for offset in range(1, taps.shape[0]):
        conv_out = conv_out + taps[offset] * padded[:, offset : offset + piece_rows]
    active = jax.nn.silu(conv_out)
    heads_in = active[:, :, :DI].reshape(seq_count, piece_rows, HEADS, HDIM)
    b_state = active[:, :, DI : DI + STATE]
    c_state = active[:, :, DI + STATE :]
    step_size = jax.nn.softplus(rate_in + dt_bias)
    log_decay = jnp.cumsum(-jnp.exp(a_log) * step_size, axis=1)
    return (heads_in, b_state, c_state, step_size, log_decay)


def local_states(heads_in, b_state, step_size, log_decay):
    tail = jnp.exp(log_decay[:, -1:, :] - log_decay) * step_size
    weighted = tail[..., None] * heads_in
    leaving = jnp.einsum("bshp,bsn->bhpn", weighted, b_state, precision=highest)
    return (jnp.exp(log_decay[:, -1, :]), leaving)


def local_out(heads_in, b_state, c_state, step_size, log_decay, skip_gain, entering):
    piece_rows = log_decay.shape[1]
    by_head = jnp.swapaxes(log_decay, 1, 2)
    lower = lax.iota(jnp.int32, piece_rows)[:, None] >= lax.iota(jnp.int32, piece_rows)[None, :]
    spread = by_head[:, :, :, None] - by_head[:, :, None, :]
    weights = jnp.where(lower, jnp.exp(jnp.where(lower, spread, 0.0)), 0.0)
    scores = jnp.einsum("btn,bsn->bts", c_state, b_state, precision=highest)
    mixing = scores[:, None] * weights * jnp.swapaxes(step_size, 1, 2)[:, :, None, :]
    inner = jnp.einsum("bhts,bshp->bthp", mixing, heads_in, precision=highest)
    carried = jnp.exp(log_decay)[..., None] * jnp.einsum(
        "btn,bhpn->bthp", c_state, entering, precision=highest
    )
    return inner + carried + skip_gain[:, None] * heads_in


def gate_norm(ssd_out, gate_in, gated_gain):
    gated = ssd_out.reshape(gate_in.shape) * jax.nn.silu(gate_in)
    return rms_scale(gated, gated_gain)


def chain_pair(earlier, later):
    return (earlier[0] * later[0], later[0][..., None, None] * earlier[1] + later[1])


def per_device(
    hidden_in,
    lengths,
    norm_gain,
    in_weight,
    conv_weight,
    conv_bias,
    dt_bias,
    a_log,
    skip_gain,
    gated_gain,
    out_weight,
    cotangent,
):
    seq_count, piece_rows, model_width = hidden_in.shape
    mixed_width = DI + 2 * STATE
    edge_count = CONV - 1
    positions = lax.axis_index("seq") * piece_rows + lax.iota(jnp.int32, piece_rows)
    valid = (positions[None, :] < lengths[:, None]).astype(jnp.float32)[:, :, None]
    gathered = (
        lax.all_gather(in_weight, ("dp", "seq"), axis=0, tiled=True),
        lax.all_gather(conv_weight, ("dp", "seq"), axis=0, tiled=True),
        lax.all_gather(conv_bias, ("dp", "seq"), axis=0, tiled=True),
        lax.all_gather(out_weight, ("dp", "seq"), axis=0, tiled=True),
    )
    w_in = gathered[0].reshape(model_width, -1)
    w_out = gathered[3].reshape(DI, model_width)
    normed, norm_back = jax.vjp(rms_scale, hidden_in, norm_gain)
    flat_normed = normed.reshape(-1, model_width)
    projected = jnp.dot(flat_normed, w_in, precision=highest).reshape(seq_count, piece_rows, -1)
    gate_in = projected[:, :, :DI]
    conv_in = projected[:, :, DI : DI + mixed_width]
    rate_in = projected[:, :, DI + mixed_width :]
    edge_rows = from_behind(conv_in[:, piece_rows - edge_count :, :], "seq", 1)
    prepared, prepare_back = jax.vjp(
        prepare,
        conv_in,
        edge_rows,
        rate_in,
        gathered[1].reshape(CONV, mixed_width),
        gathered[2],
        dt_bias,
        a_log,
    )
    heads_in, b_state, c_state, step_size, log_decay = prepared
    (decay, leaving), states_back = jax.vjp(local_states, heads_in, b_state, step_size, log_decay)
    unit_decay = jnp.ones_like(decay)
    empty_state = jnp.zeros_like(leaving)
    entering = carried_in((decay, leaving), "seq", chain_pair, (unit_decay, empty_state), False)[1]
    ssd_out, out_back = jax.vjp(
        jax.checkpoint(local_out),
        heads_in,
        b_state,
        c_state,
        step_size,
        log_decay,
        skip_gain,
        entering,
    )
    normed_gate, gate_back = jax.vjp(gate_norm, ssd_out, gate_in, gated_gain)
    flat_gate = normed_gate.reshape(-1, DI)
    branch = jnp.dot(flat_gate, w_out, precision=highest).reshape(
        seq_count, piece_rows, model_width
    )
    output = (hidden_in + branch) * valid
    grad_out = cotangent * valid
    flat_grad = grad_out.reshape(-1, model_width)
    again = (
        lax.all_gather(in_weight, ("dp", "seq"), axis=0, tiled=True),
        lax.all_gather(out_weight, ("dp", "seq"), axis=0, tiled=True),
    )
    back_in = again[0].reshape(model_width, -1)
    back_out = again[1].reshape(DI, model_width)
    grad_wout = jnp.dot(flat_gate.T, flat_grad, precision=highest)
    grad_gate = jnp.dot(flat_grad, back_out.T, precision=highest).reshape(seq_count, piece_rows, DI)
    grad_ssd, grad_gate_in, grad_ggain = gate_back(grad_gate)
    grad_heads, grad_bstate, grad_cstate, grad_step, grad_logd, grad_skip, grad_entering = out_back(
        grad_ssd
    )
    grad_leaving = carried_in(
        (decay, grad_entering), "seq", chain_pair, (unit_decay, empty_state), True
    )[1]
    grad_decay = jnp.sum(grad_leaving * entering, axis=(2, 3))
    more_heads, more_bstate, more_step, more_logd = states_back((grad_decay, grad_leaving))
    grad_conv_in, grad_edges, grad_rate, grad_taps, grad_convb, grad_dtb, grad_alog = prepare_back(
        (
            grad_heads + more_heads,
            grad_bstate + more_bstate,
            grad_cstate,
            grad_step + more_step,
            grad_logd + more_logd,
        )
    )
    returned = from_behind(grad_edges, "seq", -1)
    grad_conv_in = grad_conv_in + jnp.pad(returned, ((0, 0), (piece_rows - edge_count, 0), (0, 0)))
    grad_proj = jnp.concatenate([grad_gate_in, grad_conv_in, grad_rate], axis=2).reshape(
        seq_count * piece_rows, -1
    )
    grad_win = jnp.dot(flat_normed.T, grad_proj, precision=highest)
    grad_normed = jnp.dot(grad_proj, back_in.T, precision=highest).reshape(
        seq_count, piece_rows, model_width
    )
    grad_hidden, grad_ngain = norm_back(grad_normed)
    grad_input = grad_hidden + grad_out
    shares = (
        lax.psum_scatter(grad_win.reshape(-1), ("dp", "seq"), scatter_dimension=0, tiled=True),
        lax.psum_scatter(grad_taps.reshape(-1), ("dp", "seq"), scatter_dimension=0, tiled=True),
        lax.psum_scatter(grad_convb, ("dp", "seq"), scatter_dimension=0, tiled=True),
        lax.psum_scatter(grad_wout.reshape(-1), ("dp", "seq"), scatter_dimension=0, tiled=True),
    )
    summed = lax.psum((grad_ngain, grad_dtb, grad_alog, grad_skip, grad_ggain), ("dp", "seq"))
    return (
        output,
        grad_input,
        summed[0],
        shares[0],
        shares[1],
        shares[2],
        summed[1],
        summed[2],
        summed[3],
        summed[4],
        shares[3],
    )


def solution(mesh):
    in_specs = (
        P("dp", "seq", None),
        P("dp"),
        P(),
        P(("dp", "seq")),
        P(("dp", "seq")),
        P(("dp", "seq")),
        P(),
        P(),
        P(),
        P(),
        P(("dp", "seq")),
        P("dp", "seq", None),
    )
    out_specs = (
        P("dp", "seq", None),
        P("dp", "seq", None),
        P(),
        P(("dp", "seq")),
        P(("dp", "seq")),
        P(("dp", "seq")),
        P(),
        P(),
        P(),
        P(),
        P(("dp", "seq")),
    )
    return jax.shard_map(
        per_device, mesh=mesh, in_specs=in_specs, out_specs=out_specs, check_vma=False
    )
```

profile of v0, /device:TPU:8, one launch (start us, length us, event | category | flops | bytes accessed | tf_op | source)
XLA Modules:
  0.0 1377.3 jit_solution(2329556406140851384)
XLA Ops:
  10.5 41.9 %all-reduce.21 = (f32[9216]{0:T(1024)S(1)}, f32[2304]{0:T(1024)S(1)}) all-reduce(f32[9216]{0:T(1024)S(1)} %dynamic-update-slice.1, f32[2304]{0:T(1024)S(1)} %dynamic-update-slice), channel_id=1, replica_groups=mesh['dp'=4,'seq'=8] {'dp','seq'}, use_global_device_ids=true, to_apply=%add.15 | all-reduce | flops 11520 | bytes 92160
  55.0 77.4 %all-gather.8.cloned.1.call-done = f32[4489216]{0:T(1024)} async-done(((f32[140288]{0:T(1024)}), f32[4489216]{0:T(1024)}) %all-gather.8.cloned.1.call-update) | async-done | bytes 17956880 | tf_op jit(solution)/shard_map/all_gather | solution.py:111
  132.4 21.3 %reshape.274 = f32[1024,4384]{1,0:T(8,128)} reshape(f32[4489216]{0:T(1024)} %all-gather.8.cloned.1.call-done) | data formatting | bytes 35913728 | tf_op jit(solution)/shard_map/reshape | solution.py:116
  153.7 34.0 %fusion.4 = f32[2,256,4384]{1,2,0:T(8,128)S(1)} fusion(f32[1024,4384]{1,0:T(8,128)} %reshape.274, f32[2,256,1024]{2,1,0:T(8,128)S(1)} %copy-done.9, f32[1024]{0:T(1024)S(1)} %copy-done.20, f32[2,256]{1,0:T(2,128)S(1)} %fusion.113), kind=kOutput, calls=%fused_computation.8 | convolution fusion | flops 27582791680 | bytes 29038592 | tf_op jit(solution)/shard_map/dot_general | solution.py:120
  204.1 13.5 fusion.36
  221.2 5.1 fusion.55
  226.5 9.4 reshape.298
  236.2 15.4 %all-gather = f32[16,1,32]{2,1,0:T(1,128)S(1)} all-gather(f32[2,1,32]{2,1,0:T(1,128)S(1)} %bitcast.185), channel_id=2, replica_groups=mesh['dp'=4,'seq'=8] {'seq'}, dimensions={0}, use_global_device_ids=true | all-gather | bytes 2304 | tf_op jit(solution)/shard_map/all_gather | solution.py:25
  255.2 196.5 %all-gather.12.cloned.1.call-done = f32[16,32,64,128]{3,2,1,0:T(8,128)} async-done(((f32[2,32,64,128]{3,2,1,0:T(8,128)}), f32[16,32,64,128]{3,2,1,0:T(8,128)}) %all-gather.12.cloned.1.call-update) | async-done | bytes 16777232 | tf_op jit(solution)/shard_map/all_gather | solution.py:25
  451.7 17.0 %while.30 = (s32[]{:T(128)}, f32[2,32,64,128]{3,2,1,0:T(8,128)S(1)}, s32[]{:T(128)}, f32[8,2,32]{2,1,0:T(2,128)S(1)}, f32[8,2,32,64,128]{4,3,2,1,0:T(8,128)}, /*index=5*/s32[]{:T(128)}, s32[]{:T(128)}) while((s32[]{:T(128)}, f32[2,32,64,128]{3,2,1,0:T(8,128)S(1)}, s32[]{:T(128)}, f32[8,2,32]{2,1,0:T(2,128)S(1)}, ...), condition=%wide.region_4.5_spmd.clone, body=%wide.region_3.4_spmd.clone.sunk | while | flops 2097156 | bytes 6292337 | solution.py:38
  473.5 19.9 %fusion.43 = f32[2,256,32,64]{1,3,2,0:T(8,128)S(1)} fusion(f32[2,256,32,64]{1,3,2,0:T(8,128)S(1)} %bitcast.166, f32[2,256,32,64]{1,3,2,0:T(8,128)S(1)} %fusion.102, f32[2,32,256]{2,1,0:T(8,128)S(1)} %copy.157, f32[2,32,256]{2,1,0:T(8,128)S(1)} %copy.155, f32[2,256,256]{2,1,0:T(8,128)S(1)} %copy-done.26, pred[256,256]{1,0:T(8,128)(4,1)S(1)} %iota_compare_fusion, ...), kind=kOutput, calls=%fused_computation.72 | convolution fusion | flops 3246391296 | bytes 13369472 | tf_op jit(solution)/shard_map/jvp(bhts,bshp->bthp)/dot_general | solution.py:75
  495.2 18.8 %multiply_reduce_fusion.6 = (f32[2048]{0:T(1024)}, f32[2,256]{1,0:T(2,128)S(1)}, f32[2,256,2048]{1,2,0:T(8,128)}) fusion(f32[2,256,2048]{1,2,0:T(8,128)S(1)} %get-tuple-element.341, f32[2,256]{1,0:T(2,128)S(1)} %fusion.114, f32[2048]{0:T(1024)S(1)} %copy-done.27, f32[2048,1024,1]{1,0,2:T(8,128)S(1)} %bitcast.162, f32[2,256,1024]{2,1,0:T(8,128)} %param.27, ...), kind=kOutput, calls=%fused_computation.73 | convolution fusion | flops 12891715584 | bytes 18896896 | tf_op jit(solution)/shard_map/dot_general | solution.py:165
  514.0 6.3 fusion.38
  520.6 7.2 fusion.45
  528.8 29.1 %fusion.19 = (f32[2,32,256]{2,1,0:T(8,128)S(1)}, f32[2,32,256]{2,1,0:T(8,128)}, f32[2,32,256]{2,1,0:T(8,128)S(1)}, f32[2,256,256]{2,1,0:T(8,128)}) fusion(f32[2,256,256]{2,1,0:T(8,128)S(1)} %fusion.131, f32[2,32,256]{2,1,0:T(8,128)S(1)} %copy.167, f32[2,32,256]{2,1,0:T(8,128)S(1)} %copy.166, pred[256,256]{1,0:T(8,128)(4,1)} %copy-done.40, ...), kind=kOutput, calls=%fused_computation.30 | convolution fusion | flops 3283959808 | bytes 9830400 | tf_op jit(solution)/shard_map/transpose(jvp(jvp()))/checkpoint/bhts,bshp->bthp/dot_general | solution.py:75
  560.5 5.2 multiply_reduce_fusion.8
  567.3 18.0 %fusion.59 = f32[256,8,8,128]{3,2,1,0:T(8,128)S(1)} fusion(f32[2,256,2048]{1,2,0:T(8,128)} %copy-done.4, f32[2048]{0:T(1024)S(1)} %copy-done.27, f32[2,256]{1,0:T(2,128)S(1)} %fusion.114, f32[2,256,1024]{2,1,0:T(8,128)} %param.27, f32[2,256]{1,0:T(2,128)S(1)} %compare_convert_fusion), kind=kOutput, calls=%fused_computation.95 | convolution fusion | flops 12887523328 | bytes 14692352 | tf_op jit(solution)/shard_map/dot_general | solution.py:164
  585.3 5.5 copy.232
  595.5 158.3 %all-gather.14.cloned.1.call-done = f32[16,32,64,128]{3,2,1,0:T(8,128)} async-done(((f32[2,32,64,128]{3,2,1,0:T(8,128)}), f32[16,32,64,128]{3,2,1,0:T(8,128)}) %all-gather.14.cloned.1.call-update) | async-done | bytes 16777232 | tf_op jit(solution)/shard_map/all_gather | solution.py:25
  753.8 36.0 %while.31 = (s32[]{:T(128)}, f32[2,32,64,128]{3,2,1,0:T(8,128)}, s32[]{:T(128)}, f32[8,2,32]{2,1,0:T(2,128)}, f32[8,2,32,64,128]{4,3,2,1,0:T(8,128)}, /*index=5*/s32[]{:T(128)}, s32[]{:T(128)}, s32[]{:T(128)}, s32[]{:T(128)}) while((s32[]{:T(128)}, f32[2,32,64,128]{3,2,1,0:T(8,128)}, s32[]{:T(128)}, f32[8,2,32]{2,1,0:T(2,128)}, ...), condition=%wide.region_9.10_spmd.clone, body=%wide.region_8.9_spmd.clone.sunk | while | flops 2097160 | bytes 6292399 | solution.py:38
  789.8 6.7 multiply_reduce_fusion.9
  802.3 16.6 %fusion.39 = f32[2,256,32,64]{1,3,2,0:T(8,128)} fusion(f32[2,256,32,64]{1,3,2,0:T(8,128)S(1)} %get-tuple-element.365, f32[2,256,32,64]{1,3,2,0:T(8,128)S(1)} %bitcast.156, f32[32]{0:T(128)S(1)} %copy-done.58, f32[2,256,32]{1,2,0:T(8,128)S(1)} %copy.160, f32[2,256,256]{2,1,0:T(8,128)S(1)} %copy-done.25, f32[2,32,256]{2,1,0:T(8,128)S(1)} %copy-done.37, ...), kind=kOutput, calls=%fused_computation.65 | convolution fusion | flops 3246391296 | bytes 13369472 | tf_op jit(solution)/shard_map/transpose(jvp(jvp()))/checkpoint/bhts,bshp->bthp/dot_general | solution.py:75
  818.9 13.1 multiply_reduce_fusion.4
  836.0 7.7 pad_add_fusion
  848.7 5.0 reduce-window.16
  864.0 5.7 slice_add_fusion
  871.9 64.1 %convolution_bitcast_fusion = f32[1024,4384]{1,0:T(8,128)} fusion(f32[2,256,32]{1,2,0:T(8,128)S(1)} %copy.191, f32[2,256,2304]{1,2,0:T(8,128)S(1)} %slice_add_fusion, f32[2,256,2048]{1,2,0:T(8,128)S(1)} %copy-done.15, f32[2,256,1024]{2,1,0:T(8,128)S(1)} %copy-done.10, f32[1024]{0:T(1024)S(1)} %copy-done.21, f32[2,256]{1,0:T(2,128)S(1)} %copy-done.23), kind=kOutput, calls=%fused_computation.25 | convolution fusion | flops 27587280896 | bytes 29038592 | tf_op jit(solution)/shard_map/dot_general | solution.py:189
  935.9 22.9 %reshape.285 = f32[4489216]{0:T(1024)} reshape(f32[1024,4384]{1,0:T(8,128)} %convolution_bitcast_fusion) | data formatting | bytes 35913728 | tf_op jit(solution)/shard_map/reshape | solution.py:196
  963.6 18.5 %add_multiply_fusion = f32[2,256,1024]{2,1,0:T(8,128)} fusion(f32[2,256,1024]{2,1,0:T(8,128)S(1)} %copy-done.10, f32[2048,1024,1]{1,0,2:T(8,128)} %reshape.298, f32[2,256,2048]{1,2,0:T(8,128)S(1)} %copy-done.5, f32[2048]{0:T(1024)S(1)} %copy-done.27, f32[2,256]{1,0:T(2,128)S(1)} %fusion.114, f32[2,256]{1,0:T(2,128)S(1)} %compare_convert_fusion), kind=kOutput, calls=%fused_computation.108 | convolution fusion | flops 12888047616 | bytes 16789504 | tf_op jit(solution)/shard_map/dot_general | solution.py:152
  982.3 65.7 %multiply_reduce_fusion.12 = (f32[1024]{0:T(1024)S(1)}, f32[2,256]{1,0:T(2,128)S(1)}, f32[2,256,1024]{2,1,0:T(8,128)}) fusion(f32[2,256,1024]{2,1,0:T(8,128)S(1)} %copy-done.10, f32[2,256]{1,0:T(2,128)S(1)} %copy-done.23, f32[1024]{0:T(1024)S(1)} %copy-done.21, f32[1024,4384]{1,0:T(8,128)} %reshape.274, f32[2,256,32]{1,2,0:T(8,128)S(1)} %copy.191, ...), kind=kOutput, calls=%fused_computation.103 | convolution fusion | flops 27589376000 | bytes 31141888 | tf_op jit(solution)/shard_map/dot_general | solution.py:190
  1047.9 44.2 %all-reduce.20 = (f32[1024]{0:T(1024)}, f32[9216]{0:T(1024)S(1)}, f32[2304]{0:T(1024)S(1)}, f32[32]{0:T(128)}, f32[32]{0:T(128)}, /*index=5*/f32[32]{0:T(128)}, f32[2048]{0:T(1024)}) all-reduce(f32[1024]{0:T(1024)S(1)} %get-tuple-element.302, f32[9216]{0:T(1024)S(1)} %reshape.286, ...), channel_id=1, replica_groups=mesh['dp'=4,'seq'=8] {'dp','seq'}, use_global_device_ids=true, to_apply=%region_21.22 | all-reduce | flops 14688 | bytes 117504 | tf_op jit(solution)/shard_map/psum | solution.py:201
  1097.5 269.5 %all-reduce.25.cloned.1.call-done = (f32[4489216]{0:T(1024)}, f32[2097152]{0:T(1024)}) async-done(((f32[4489216]{0:T(1024)}, f32[2097152]{0:T(1024)}), (f32[4489216]{0:T(1024)}, f32[2097152]{0:T(1024)})) %all-reduce.25.cloned.1.call-update) | async-done | bytes 26345488
  (275 shorter events, 139.1 us)
Async XLA Ops:
  7.2 125.2 %all-gather.8.cloned.1.call-start = ((), (), s32[]{:S(2)}) async-start(), calls=%async_computation | async-start | bytes 18518016 | tf_op jit(solution)/shard_map/all_gather | solution.py:111
  7.9 218.5 %all-gather.10.cloned.1.call-start = ((), (), s32[]{:S(2)}) async-start(), calls=%async_computation.1 | async-start | bytes 8650752 | tf_op jit(solution)/shard_map/all_gather | solution.py:114
  8.7 443.0 %all-gather.12.cloned.1.call-start = ((), (), s32[]{:S(2)}) async-start(), calls=%async_computation.2 | async-start | bytes 18874368 | tf_op jit(solution)/shard_map/all_gather | solution.py:25
  54.9 140.8 %copy-start.55 = (f32[32]{0:T(128)}, f32[32]{0:T(128)S(1)}, u32[]{:S(2)}) copy-start(f32[32]{0:T(128)S(1)} %exponential_negate_fusion) | copy-start | bytes 388
  54.9 98.8 %copy-start.22 = (f32[2,256]{1,0:T(2,128)}, f32[2,256]{1,0:T(2,128)S(1)}, u32[]{:S(2)}) copy-start(f32[2,256]{1,0:T(2,128)S(1)} %fusion.113) | copy-start | bytes 6148
  54.9 149.1 %copy-start.28 = (f32[2304]{0:T(1024)}, f32[2304]{0:T(1024)S(1)}, u32[]{:S(2)}) copy-start(f32[2304]{0:T(1024)S(1)} %get-tuple-element.359) | copy-start | bytes 27652
  54.9 149.1 %copy-start.30 = (f32[2304]{0:T(1024)}, f32[2304]{0:T(1024)S(1)}, u32[]{:S(2)}) copy-start(f32[2304]{0:T(1024)S(1)} %get-tuple-element.360) | copy-start | bytes 27652
  54.9 149.1 %copy-start.32 = (f32[2304]{0:T(1024)}, f32[2304]{0:T(1024)S(1)}, u32[]{:S(2)}) copy-start(f32[2304]{0:T(1024)S(1)} %get-tuple-element.361) | copy-start | bytes 27652
  54.9 149.1 %copy-start.34 = (f32[2304]{0:T(1024)}, f32[2304]{0:T(1024)S(1)}, u32[]{:S(2)}) copy-start(f32[2304]{0:T(1024)S(1)} %get-tuple-element.362) | copy-start | bytes 27652
  54.9 98.7 %copy-start.9 = (f32[2,256,1024]{2,1,0:T(8,128)S(1)}, f32[2,256,1024]{2,1,0:T(8,128)}, u32[]{:S(2)}) copy-start(f32[2,256,1024]{2,1,0:T(8,128)} %param.16) | copy-start | bytes 6291460
  55.0 98.7 %copy-start.20 = (f32[1024]{0:T(1024)S(1)}, f32[1024]{0:T(1024)}, u32[]{:S(2)}) copy-start(f32[1024]{0:T(1024)} %param.18) | copy-start | bytes 12292
  191.9 11.4 collective-permute-start
  226.2 527.6 %all-gather.14.cloned.1.call-start = ((), (), s32[]{:S(2)}) async-start(), calls=%async_computation.3 | async-start | bytes 18874368 | tf_op jit(solution)/shard_map/all_gather | solution.py:25
  226.4 247.1 %copy-start.40 = (pred[256,256]{1,0:T(8,128)(4,1)}, pred[256,256]{1,0:T(8,128)(4,1)S(1)}, u32[]{:S(2)}) copy-start(pred[256,256]{1,0:T(8,128)(4,1)S(1)} %iota_compare_fusion) | copy-start | bytes 196612
  468.7 24.7 %slice-start = ((s8[8978432]{0:T(1024)(128)(4,1)}), s8[4194304]{0:T(1024)(128)(4,1)S(1)}, s32[]{:S(2)}) async-start(s8[8978432]{0:T(1024)(128)(4,1)} %bitcast.157), calls=%async_computation.5 | async-start | bytes 8388608
  468.7 26.4 %slice-start.6 = ((s8[8388608]{0:T(1024)(128)(4,1)}), s8[4194304]{0:T(1024)(128)(4,1)S(1)}, s32[]{:S(2)}) async-start(s8[8388608]{0:T(1024)(128)(4,1)} %bitcast.161), calls=%async_computation.11 | async-start | bytes 8388608
  473.5 19.9 %slice-start.1 = ((s8[8978432]{0:T(1024)(128)(4,1)}), s8[4194304]{0:T(1024)(128)(4,1)S(1)}, s32[]{:S(2)}) async-start(s8[8978432]{0:T(1024)(128)(4,1)} %bitcast.157), calls=%async_computation.6 | async-start | bytes 8388608
  473.5 19.9 %slice-start.2 = ((s8[8978432]{0:T(1024)(128)(4,1)}), s8[589824]{0:T(1024)(128)(4,1)S(1)}, s32[]{:S(2)}) async-start(s8[8978432]{0:T(1024)(128)(4,1)} %bitcast.157), calls=%async_computation.7 | async-start | bytes 1179648
  473.5 21.6 %slice-start.7 = ((s8[8388608]{0:T(1024)(128)(4,1)}), s8[4194304]{0:T(1024)(128)(4,1)S(1)}, s32[]{:S(2)}) async-start(s8[8388608]{0:T(1024)(128)(4,1)} %bitcast.161), calls=%async_computation.12 | async-start | bytes 8388608
  495.1 18.9 %copy-start.4 = (f32[2,256,2048]{1,2,0:T(8,128)}, f32[2,256,2048]{1,2,0:T(8,128)S(1)}, u32[]{:S(2)}) copy-start(f32[2,256,2048]{1,2,0:T(8,128)S(1)} %get-tuple-element.341) | copy-start | bytes 12582916
  527.9 839.1 %all-reduce.25.cloned.1.call-start = ((), (), s32[]{:S(2)}) async-start(), calls=%async_computation.4 | async-start | bytes 52690944
  528.1 29.9 %copy-start.36 = (f32[2,32,256]{2,1,0:T(8,128)}, f32[2,32,256]{2,1,0:T(8,128)S(1)}, u32[]{:S(2)}) copy-start(f32[2,32,256]{2,1,0:T(8,128)S(1)} %copy.167) | copy-start | bytes 196612
  528.2 29.7 %copy-start.38 = (f32[2,32,256]{2,1,0:T(8,128)}, f32[2,32,256]{2,1,0:T(8,128)S(1)}, u32[]{:S(2)}) copy-start(f32[2,32,256]{2,1,0:T(8,128)S(1)} %copy.166) | copy-start | bytes 196612
  528.8 29.1 %copy-start.24 = (f32[2,256,256]{2,1,0:T(8,128)}, f32[2,256,256]{2,1,0:T(8,128)S(1)}, u32[]{:S(2)}) copy-start(f32[2,256,256]{2,1,0:T(8,128)S(1)} %fusion.131) | copy-start | bytes 1572868
  797.5 21.3 %slice-start.3 = ((s8[8978432]{0:T(1024)(128)(4,1)}), s8[4194304]{0:T(1024)(128)(4,1)S(1)}, s32[]{:S(2)}) async-start(s8[8978432]{0:T(1024)(128)(4,1)} %bitcast.159), calls=%async_computation.8 | async-start | bytes 8388608
  797.5 21.3 %slice-start.8 = ((s8[4718592]{0:T(1024)(128)(4,1)}), s8[524288]{0:T(1024)(128)(4,1)S(1)}, s32[]{:S(2)}) async-start(s8[4718592]{0:T(1024)(128)(4,1)} %bitcast.168), calls=%async_computation.13 | async-start | bytes 1048576
  855.5 6.3 collective-permute-start.1
  963.5 18.6 %copy-start.42 = (f32[2304]{0:T(1024)S(1)}, f32[2304]{0:T(1024)}, u32[]{:S(2)}) copy-start(f32[2304]{0:T(1024)} %get-tuple-element.301) | copy-start | bytes 27652
  963.5 18.7 %copy-start.59 = (f32[32]{0:T(128)S(1)}, f32[32]{0:T(128)}, u32[]{:S(2)}) copy-start(f32[32]{0:T(128)} %param.23) | copy-start | bytes 388
  982.2 65.7 %copy-start.46 = (f32[2304]{0:T(1024)S(1)}, f32[2304]{0:T(1024)}, u32[]{:S(2)}) copy-start(f32[2304]{0:T(1024)} %get-tuple-element.300) | copy-start | bytes 27652
  982.2 65.7 %copy-start.48 = (f32[2048]{0:T(1024)S(1)}, f32[2048]{0:T(1024)}, u32[]{:S(2)}) copy-start(f32[2048]{0:T(1024)} %get-tuple-element.298) | copy-start | bytes 24580
  982.2 111.2 %copy-start.50 = (f32[2,256]{1,0:T(2,128)S(1)}, f32[2,256]{1,0:T(2,128)}, u32[]{:S(2)}) copy-start(f32[2,256]{1,0:T(2,128)} %copy-done.49) | copy-start | bytes 6148
  (45 other events, 369.5 us)
Sparse Core Ops, SparseCore 0:
  10.9 121.4 all-gather.7
  135.4 77.9 all-gather.9
  226.4 225.2 all-gather.11
  528.0 225.7 all-gather.13
  959.0 407.9 all-reduce.24
where the time goes:
time: 1390 us; the launch traced here: 1380 us
  waiting for transfers between devices  703 us (51%)
  matrix products  326 us (23%)
  other arithmetic  124 us (9%)
  blocking collectives  102 us (7%)
  local copies, waits for them, and re-layouts  99.1 us (7%)
  between operations  15.2 us (1%)
    all_gather x2, waiting for transfers between devices, carried_in(): everything = jax.tree.map(lambda part: lax.all_gather(part, axis), value)  355 us
    unnamed x6, waiting for transfers between devices  271 us
    all_gather x1, waiting for transfers between devices, per_device(): lax.all_gather(in_weight, ('dp', 'seq'), axis=0, tiled=True)  77.4 us
    dot_general x1, matrix products, per_device(): jnp.dot(grad_proj, back_in.T, precision=highest)  65.7 us
    dot_general x3, matrix products, local_out(): inner = jnp.einsum('bhts,bshp->bthp', mixing, heads_in, precision=highest)  65.5 us
    dot_general x1, matrix products, per_device(): grad_win = jnp.dot(flat_normed.T, grad_proj, precision=highest)  64.1 us
    select_n x16, other arithmetic, step(): return jax.tree.map(lambda a, b: jnp.where(reached, a, b), new, before)  46.9 us
    psum x1, blocking collectives, per_device(): lax.psum((grad_ngain, grad_dtb, grad_alog, grad_skip, grad_ggain), ('dp',...  44.2 us
  transfers between devices with their start and end apart: 7, of which 4 were waited for; matrix products, arithmetic and copies ran while one was open for 19% of the time, Pallas kernels for 0%

commit v1 on v0

v1 whole, which is shorter than its diff:
```python
import functools

import jax
import jax.numpy as jnp
from jax import lax
from jax.experimental import pallas as pl
from jax.experimental.pallas import tpu as pltpu
from jax.sharding import Mesh
from jax.sharding import PartitionSpec as P

DI = 2048
HEADS = 32
HDIM = 64
STATE = 128
CONV = 4
MIXED = DI + 2 * STATE
RATED = MIXED + HEADS
CUT = 128
EDGE = 8
PAIR = 2 * HDIM
F32 = jnp.float32
BF16 = jnp.bfloat16
HIGH = lax.Precision.HIGH
EXACT = lax.Precision.HIGHEST
epsilon = 1e-05


def shift(block, axis, step=1):
    count = lax.axis_size(axis)
    return lax.ppermute(block, axis, [(i, (i + step) % count) for i in range(count)])


def gather_axis(block, axis):
    count, index = (lax.axis_size(axis), lax.axis_index(axis))
    whole = jnp.zeros((count,) + block.shape, block.dtype)
    whole = lax.dynamic_update_slice_in_dim(whole, block[None], index, 0)
    moving = block
    for k in range(1, count):
        moving = shift(moving, axis)
        whole = lax.dynamic_update_slice_in_dim(whole, moving[None], (index - k) % count, 0)
    return whole


AXES = ("y", "core", "zc", "p")


def gather_rows(piece, order):
    block = piece.reshape((1,) * len(AXES) + piece.shape)
    for axis in order:
        at = AXES.index(axis)
        block = jnp.moveaxis(gather_axis(block, axis), 0, at)
        block = block.reshape(block.shape[: at + 1] + block.shape[at + 2 :])
    return block.reshape(-1, piece.shape[-1])


def scatter_axis(parts, axis, dim):
    count, index = (lax.axis_size(axis), lax.axis_index(axis))
    moving = lax.dynamic_index_in_dim(parts, (index - 1) % count, dim, keepdims=False)
    for k in range(2, count + 1):
        moving = shift(moving, axis) + lax.dynamic_index_in_dim(
            parts, (index - k) % count, dim, keepdims=False
        )
    return moving


def scatter_rows(whole, order):
    left = list(AXES)
    block = whole.reshape([lax.axis_size(a) for a in AXES] + [-1, whole.shape[-1]])
    for axis in order:
        block = scatter_axis(block, axis, left.index(axis))
        left.remove(axis)
    return block


def gather_matrix(piece):
    half = piece.shape[1] // 256 * 128
    return (
        gather_rows(piece[:, :half], ("zc", "p", "y", "core")),
        gather_rows(piece[:, half:], ("zc", "y", "p", "core")),
    )


def scatter_matrix(whole):
    half = whole.shape[1] // 256 * 128
    return jnp.concatenate(
        [
            scatter_rows(whole[:, :half], ("core", "p", "y", "zc")),
            scatter_rows(whole[:, half:], ("core", "y", "p", "zc")),
        ],
        axis=1,
    )


def sum_everywhere(values):
    for axis in ("core", "p", "y", "zc"):
        if lax.axis_size(axis) == 2:
            values = values + shift(values, axis)
        else:
            values = jnp.sum(gather_axis(values, axis), axis=0)
    return values


def to_span(block, mine):
    keep = lax.dynamic_index_in_dim(block, mine, 0, keepdims=False)
    other = shift(lax.dynamic_index_in_dim(block, 1 - mine, 0, keepdims=False), "p")
    first = mine == 0
    return jnp.concatenate([jnp.where(first, keep, other), jnp.where(first, other, keep)], axis=0)


def from_span(span, mine):
    block = span.reshape(2, -1, span.shape[-1])
    keep = lax.dynamic_index_in_dim(block, mine, 0, keepdims=False)
    other = shift(lax.dynamic_index_in_dim(block, 1 - mine, 0, keepdims=False), "p")
    first = mine == 0
    return jnp.stack([jnp.where(first, keep, other), jnp.where(first, other, keep)], axis=0)


def chain(decay, leaving, reverse):
    count, index = (lax.axis_size("zc"), lax.axis_index("zc"))
    place = count - 1 - index if reverse else index
    route = [(i + 1, i) if reverse else (i, i + 1) for i in range(count - 1)]
    chunks = 4
    rows = leaving.shape[0] // chunks
    came, got = ([], None)
    for step in range(chunks + count - 2):
        at = jnp.clip(step - place, 0, chunks - 1) * rows
        send = lax.dynamic_slice_in_dim(leaving, at, rows, 0)
        if got is not None:
            send = send + decay * got
        got = lax.ppermute(send, "zc", route)
        came.append(got)
    return lax.dynamic_slice_in_dim(
        jnp.concatenate(came, axis=0), jnp.maximum(place - 1, 0) * rows, leaving.shape[0], 0
    )


def nn(a, b, precision=HIGH):
    return jnp.dot(a, b, precision=precision, preferred_element_type=F32)


def nt(a, b, precision=HIGH):
    return lax.dot_general(
        a, b, (((1,), (1,)), ((), ())), precision=precision, preferred_element_type=F32
    )


def tn(a, b, precision=HIGH):
    return lax.dot_general(
        a, b, (((0,), (0,)), ((), ())), precision=precision, preferred_element_type=F32
    )


def spread_heads(values, spreader):
    top = values.astype(BF16)
    rest = values - top.astype(F32)
    mid = rest.astype(BF16)
    low = (rest - mid.astype(F32)).astype(BF16)
    return jnp.dot(
        jnp.concatenate([top, mid, low], axis=1), spreader, preferred_element_type=F32
    )


def sum_heads(values, gatherer):
    top = values.astype(BF16)
    low = (values - top.astype(F32)).astype(BF16)
    return jnp.dot(top, gatherer, preferred_element_type=F32) + jnp.dot(
        low, gatherer, preferred_element_type=F32
    )


def order_mask(shape, kind):
    row, column = (lax.broadcasted_iota(jnp.int32, shape, d) for d in (0, 1))
    return {"ge": row >= column, "gt": row > column, "le": row <= column, "lt": row < column}[kind]


def triangle(kind):
    return jnp.where(order_mask((CUT, CUT), kind), 1.0, 0.0).astype(F32)


def conv_chunk(window_ref, taps_ref, bias_ref, cols):
    total = bias_ref[:, cols] + taps_ref[0:1, cols] * window_ref[EDGE - 3 : EDGE - 3 + CUT, cols]
    for k in range(1, CONV):
        at = EDGE - 3 + k
        total = total + taps_ref[k : k + 1, cols] * window_ref[at : at + CUT, cols]
    return total


def prepare_kernel(
    proj_ref,
    edge_ref,
    taps_ref,
    bias_ref,
    dtb_ref,
    alog_ref,
    spreader_ref,
    act_ref,
    step_ref,
    slope_ref,
    logd_ref,
    local_ref,
    before_ref,
    total_ref,
    window,
    state,
    logs,
):
    q = pl.program_id(0)

    @pl.when(q == 0)
    def _():
        window[0:EDGE, :] = edge_ref[:, 0:MIXED]
        state[...] = jnp.zeros_like(state)
        logs[...] = jnp.zeros_like(logs)

    @pl.when(q > 0)
    def _():
        window[0:EDGE, :] = window[CUT : CUT + EDGE, :]

    window[EDGE : EDGE + CUT, :] = proj_ref[:, 0:MIXED]

    def conv(c, carry):
        cols = pl.ds(pl.multiple_of(c * 256, 256), 256)
        out = conv_chunk(window, taps_ref, bias_ref, cols)
        act_ref[:, cols] = out * jax.nn.sigmoid(out)
        return carry

    lax.fori_loop(0, MIXED // 256, conv, 0)
    raw = proj_ref[:, MIXED:RATED] + dtb_ref[...]
    step = jnp.maximum(raw, 0.0) + jnp.log1p(jnp.exp(-jnp.abs(raw)))
    logd = nn(triangle("ge"), -jnp.exp(alog_ref[...]) * step, EXACT)
    step_ref[...] = step
    slope_ref[...] = jax.nn.sigmoid(raw)
    logd_ref[...] = logd
    last = logd[CUT - 1 : CUT, :]
    tail = spread_heads(jnp.exp(last - logd) * step, spreader_ref[...])
    added = tn(act_ref[:, DI : DI + STATE], act_ref[:, 0:DI] * tail)
    decay = spread_heads(jnp.broadcast_to(jnp.exp(last), (8, HEADS)), spreader_ref[...])
    state[...] = state[...] * decay[0:1, :] + added
    local_ref[0] = state[...]
    before_ref[...] = jnp.exp(logs[...])
    logs[...] = logs[...] + jnp.broadcast_to(last, (8, HEADS))
    total_ref[...] = jnp.exp(logs[...])


def full(shape):
    return pl.BlockSpec(shape, lambda i: (0,) * len(shape))


def params():
    return pltpu.CompilerParams(
        dimension_semantics=("arbitrary",), vmem_limit_bytes=52 * 1024 * 1024
    )


def prepare(proj, taps, bias, dt_bias, a_log, spreader):
    width = proj.shape[1]
    rows = proj.shape[0] - EDGE
    cuts = rows // CUT
    return pl.pallas_call(
        prepare_kernel,
        grid=(cuts,),
        in_specs=[
            pl.BlockSpec((CUT, width), lambda i: (i, 0)),
            pl.BlockSpec((EDGE, width), lambda i: (rows // EDGE, 0)),
            full((CONV, MIXED)),
            full((1, MIXED)),
            full((1, HEADS)),
            full((1, HEADS)),
            full((3 * HEADS, DI)),
        ],
        out_specs=[
            pl.BlockSpec((CUT, MIXED), lambda i: (i, 0)),
            pl.BlockSpec((CUT, HEADS), lambda i: (i, 0)),
            pl.BlockSpec((CUT, HEADS), lambda i: (i, 0)),
            pl.BlockSpec((CUT, HEADS), lambda i: (i, 0)),
            pl.BlockSpec((1, STATE, DI), lambda i: (i, 0, 0)),
            pl.BlockSpec((8, HEADS), lambda i: (i, 0)),
            full((8, HEADS)),
        ],
        out_shape=[
            jax.ShapeDtypeStruct((rows, MIXED), F32),
            jax.ShapeDtypeStruct((rows, HEADS), F32),
            jax.ShapeDtypeStruct((rows, HEADS), F32),
            jax.ShapeDtypeStruct((rows, HEADS), F32),
            jax.ShapeDtypeStruct((cuts, STATE, DI), F32),
            jax.ShapeDtypeStruct((8 * cuts, HEADS), F32),
            jax.ShapeDtypeStruct((8, HEADS), F32),
        ],
        scratch_shapes=[
            pltpu.VMEM((CUT + EDGE, MIXED), F32),
            pltpu.VMEM((STATE, DI), F32),
            pltpu.VMEM((8, HEADS), F32),
        ],
        compiler_params=params(),
        cost_estimate=pl.CostEstimate(
            flops=6 * rows * STATE * DI, bytes_accessed=24_000_000, transcendentals=rows * MIXED
        ),
        name="prepare",
    )(proj, proj, taps, bias, dt_bias, a_log, spreader)


def both_columns(pair, left):
    turned = pltpu.roll(pair, HDIM, 1)
    return (jnp.where(left, pair, turned), jnp.where(left, turned, pair))


def stacked_pair(pair, left):
    zero = jnp.zeros_like(pair)
    return jnp.concatenate([jnp.where(left, pair, zero), jnp.where(left, zero, pair)], axis=0)


def mixer_kernel(
    act_ref,
    step_ref,
    logd_ref,
    gate_ref,
    dng_ref,
    local_ref,
    enter_ref,
    before_ref,
    skip_ref,
    ggain_ref,
    spreader_ref,
    ng_ref,
    dy_ref,
    dz_ref,
    gin_ref,
    ggrad_ref,
    skipg_ref,
    logx,
    weighted,
    out,
    log_rows,
    gstate,
    scores,
):
    i = pl.program_id(0)
    q = pl.num_programs(0) - 1 - i
    spreader = spreader_ref[...]

    @pl.when(i == 0)
    def _():
        gstate[...] = jnp.zeros_like(gstate)
        ggrad_ref[...] = jnp.zeros_like(ggrad_ref)
        skipg_ref[...] = jnp.zeros_like(skipg_ref)

    logd = logd_ref[...]
    logx[...] = spread_heads(logd, spreader)
    log_rows[...] = logd.T
    heads_in = act_ref[:, 0:DI]
    weighted[...] = heads_in * spread_heads(step_ref[...], spreader)
    before = spread_heads(before_ref[...], spreader)[0:1, :]
    entering = enter_ref[...] * before + jnp.where(q == 0, 0.0, local_ref[0])
    b_state = act_ref[:, DI : DI + STATE]
    c_state = act_ref[:, DI + STATE : MIXED]
    out[...] = jnp.exp(logx[...]) * nn(c_state, entering) + skip_ref[...] * heads_in
    scores[...] = nt(c_state, b_state)

    def pair(j, carry):
        cols = pl.ds(pl.multiple_of(j * PAIR, PAIR), PAIR)
        left = lax.broadcasted_iota(jnp.int32, (CUT, PAIR), 1) < HDIM
        mask = order_mask((CUT, CUT), "ge")
        mixes = []
        for side, column in enumerate(both_columns(logx[:, cols], left)):
            row = log_rows[pl.ds(2 * j + side, 1), :]
            mixes.append(jnp.exp(jnp.where(mask, column - row, -1e30)) * scores[...])
        out[:, cols] += nn(
            jnp.concatenate(mixes, axis=1), stacked_pair(weighted[:, cols], left)
        )
        return carry

    lax.fori_loop(0, HEADS // 2, pair, 0)

    def gate(k, carry):
        rows = pl.ds(pl.multiple_of(k * 8, 8), 8)
        ssd = out[rows, :]
        gate_in = gate_ref[rows, :]
        sg = jax.nn.sigmoid(gate_in)
        silu = gate_in * sg
        gated = ssd * silu
        scale = lax.rsqrt(jnp.mean(gated * gated, axis=1, keepdims=True) + epsilon)
        unit = gated * scale
        ng_ref[rows, :] = unit * ggain_ref[...]
        dng = dng_ref[rows, :]
        e = dng * ggain_ref[...]
        ggrad_ref[...] += dng * unit
        dgated = scale * (e - unit * jnp.mean(e * unit, axis=1, keepdims=True))
        dy = dgated * silu
        dy_ref[rows, :] = dy
        dz_ref[rows, :] = dgated * ssd * (sg * (1.0 + gate_in * (1.0 - sg)))
        skipg_ref[...] += dy * act_ref[rows, 0:DI]
        return carry

    lax.fori_loop(0, CUT // 8, gate, 0)
    decay = spread_heads(
        jnp.broadcast_to(jnp.exp(logd[CUT - 1 : CUT, :]), (8, HEADS)), spreader
    )[0:1, :]
    gstate[...] = gstate[...] * decay + tn(c_state, jnp.exp(logx[...]) * dy_ref[...])
    gin_ref[0] = gstate[...]


def mixer(act, step, logd, gate_in, dng, local, entering, before, skip, ggain, spreader):
    rows = act.shape[0]
    cuts = rows // CUT

    def back(width):
        return pl.BlockSpec((CUT, width), lambda i: (cuts - 1 - i, 0))

    wide = jax.ShapeDtypeStruct((rows, DI), F32)
    return pl.pallas_call(
        mixer_kernel,
        grid=(cuts,),
        in_specs=[
            back(MIXED),
            back(HEADS),
            back(HEADS),
            back(DI),
            back(DI),
            pl.BlockSpec((1, STATE, DI), lambda i: (jnp.maximum(cuts - 2 - i, 0), 0, 0)),
            full((STATE, DI)),
            pl.BlockSpec((8, HEADS), lambda i: (cuts - 1 - i, 0)),
            full((1, DI)),
            full((1, DI)),
            full((3 * HEADS, DI)),
        ],
        out_specs=[
            back(DI),
            back(DI),
            back(DI),
            pl.BlockSpec((1, STATE, DI), lambda i: (cuts - 1 - i, 0, 0)),
            full((8, DI)),
            full((8, DI)),
        ],
        out_shape=[
            wide,
            wide,
            wide,
            jax.ShapeDtypeStruct((cuts, STATE, DI), F32),
            jax.ShapeDtypeStruct((8, DI), F32),
            jax.ShapeDtypeStruct((8, DI), F32),
        ],
        scratch_shapes=[
            pltpu.VMEM((CUT, DI), F32),
            pltpu.VMEM((CUT, DI), F32),
            pltpu.VMEM((CUT, DI), F32),
            pltpu.VMEM((HEADS, CUT), F32),
            pltpu.VMEM((STATE, DI), F32),
            pltpu.VMEM((CUT, CUT), F32),
        ],
        compiler_params=params(),
        cost_estimate=pl.CostEstimate(
            flops=30 * rows * STATE * DI, bytes_accessed=38_000_000, transcendentals=rows * CUT * HEADS
        ),
        name="mixer",
    )(act, step, logd, gate_in, dng, local, entering, before, skip, ggain, spreader)


def back_kernel(
    act_ref,
    step_ref,
    slope_ref,
    logd_ref,
    dy_ref,
    local_ref,
    enter_ref,
    before_ref,
    gin_ref,
    gout_ref,
    proj_ref,
    halo_ref,
    taps_ref,
    bias_ref,
    alog_ref,
    skip_ref,
    spreader_ref,
    gatherer_ref,
    dproj_ref,
    dtaps_ref,
    dbias_ref,
    dlog_ref,
    ddtb_ref,
    logx,
    weighted,
    dweighted,
    log_rows,
    sum_rows,
    scores,
    dscores,
    sum_columns,
    dact,
    window,
    dwindow,
    after,
):
    i = pl.program_id(0)
    cuts = pl.num_programs(0)
    q = cuts - 1 - i
    spreader = spreader_ref[...]
    gatherer = gatherer_ref[...]

    @pl.when(i == 0)
    def _():
        after[...] = jnp.zeros_like(after)
        dwindow[...] = jnp.zeros_like(dwindow)
        for ref in (dtaps_ref, dbias_ref, dlog_ref, ddtb_ref):
            ref[...] = jnp.zeros_like(ref)

    @pl.when(i > 0)
    def _():
        dwindow[CUT : CUT + EDGE, :] = dwindow[0:EDGE, :]

    logd = logd_ref[...]
    step = step_ref[...]
    last = logd[CUT - 1 : CUT, :]
    logx[...] = spread_heads(logd, spreader)
    log_rows[...] = logd.T
    heads_in = act_ref[:, 0:DI]
    steps = spread_heads(step, spreader)
    weighted[...] = heads_in * steps
    before = spread_heads(before_ref[...], spreader)[0:1, :]
    entering = enter_ref[...] * before + jnp.where(q == 0, 0.0, local_ref[0])
    later = spread_heads(jnp.exp(after[...]), spreader)[0:1, :]
    gout = gout_ref[...] * later + jnp.where(i == 0, 0.0, gin_ref[0])
    after[...] = after[...] + jnp.broadcast_to(last, (8, HEADS))
    b_state = act_ref[:, DI : DI + STATE]
    c_state = act_ref[:, DI + STATE : MIXED]
    scores[...] = nt(b_state, c_state)
    dscores[...] = jnp.zeros_like(dscores)
    sum_columns[...] = jnp.zeros_like(sum_columns)

    def pair(j, carry):
        cols = pl.ds(pl.multiple_of(j * PAIR, PAIR), PAIR)
        left = lax.broadcasted_iota(jnp.int32, (CUT, PAIR), 1) < HDIM
        mask = order_mask((CUT, CUT), "le")
        strict = order_mask((CUT, CUT), "lt")
        dy = dy_ref[:, cols]
        dmix = nt(stacked_pair(weighted[:, cols], left), dy)
        mixes = []
        lane = lax.broadcasted_iota(jnp.int32, (CUT, CUT), 1)
        for side, column in enumerate(both_columns(logx[:, cols], left)):
            row = log_rows[pl.ds(2 * j + side, 1), :]
            weights = jnp.exp(jnp.where(mask, row - column, -1e30))
            mixes.append(weights * scores[...])
            part = dmix[side * CUT : (side + 1) * CUT, :] * weights
            dscores[...] += part
            moved = jnp.where(strict, part * scores[...], 0.0)
            sum_rows[pl.ds(2 * j + side, 1), :] = jnp.sum(moved, axis=0, keepdims=True)
            sum_columns[...] += jnp.where(
                lane == 2 * j + side, jnp.sum(moved, axis=1, keepdims=True), 0.0
            )
        dweighted[:, cols] = nn(jnp.concatenate(mixes, axis=1), stacked_pair(dy, left))
        return carry

    lax.fori_loop(0, HEADS // 2, pair, 0)
    tail = jnp.exp(logx[CUT - 1 : CUT, :] - logx[...])
    from_state = tail * nn(b_state, gout)
    left_part = weighted[...] * from_state
    dweighted[...] += from_state
    carried = jnp.exp(logx[...]) * dy_ref[...]
    dact[:, DI : DI + STATE] = nn(dscores[...], c_state) + nt(tail * weighted[...], gout)
    dact[:, DI + STATE : MIXED] = tn(dscores[...], b_state) + nt(carried, entering)
    dact[:, 0:DI] = dweighted[...] * steps + skip_ref[...] * dy_ref[...]
    moved = (
        log_rows_to_columns(sum_rows)
        - sum_columns[:, 0:HEADS]
        + sum_heads(carried * nn(c_state, entering), gatherer)
    )
    kept = sum_heads(
        jnp.broadcast_to(jnp.sum(gout * entering, axis=0, keepdims=True), (8, DI)), gatherer
    )[0:1, :]
    dlog = (
        nn(triangle("le"), moved, EXACT)
        + nn(triangle("gt"), sum_heads(left_part, gatherer), EXACT)
        + jnp.exp(last) * kept
    )
    rate = -jnp.exp(alog_ref[...])
    dlog_ref[...] += jnp.broadcast_to(
        jnp.sum(dlog * step, axis=0, keepdims=True) * rate, (8, HEADS)
    )
    draw = (sum_heads(heads_in * dweighted[...], gatherer) + dlog * rate) * slope_ref[...]
    ddtb_ref[...] += jnp.broadcast_to(jnp.sum(draw, axis=0, keepdims=True), (8, HEADS))
    here = pl.ds(pl.multiple_of(q * CUT, CUT), CUT)
    width = dproj_ref.shape[1]
    dproj_ref[here, MIXED:width] = jnp.concatenate(
        [draw, jnp.zeros((CUT, width - RATED), F32)], axis=1
    )

    window[0:EDGE, :] = halo_ref[:, 0:MIXED]
    window[EDGE : EDGE + CUT, :] = proj_ref[:, 0:MIXED]

    def conv(c, carry):
        cols = pl.ds(pl.multiple_of(c * 256, 256), 256)
        out = conv_chunk(window, taps_ref, bias_ref, cols)
        sg = jax.nn.sigmoid(out)
        dout = dact[:, cols] * (sg * (1.0 + out * (1.0 - sg)))
        dwindow[0:CUT, cols] = dout
        dbias_ref[:, cols] += jnp.sum(dout.reshape(CUT // 8, 8, 256), axis=0)
        for k in range(CONV):
            at = EDGE - 3 + k
            dtaps_ref[8 * k : 8 * k + 8, cols] += jnp.sum(
                (dout * window[at : at + CUT, cols]).reshape(CUT // 8, 8, 256), axis=0
            )
        din = taps_ref[CONV - 1 : CONV, cols] * dout
        for k in range(CONV - 1):
            din = din + taps_ref[k : k + 1, cols] * dwindow[3 - k : 3 - k + CUT, cols]
        dproj_ref[here, cols] = din
        return carry

    lax.fori_loop(0, MIXED // 256, conv, 0)

    @pl.when(q == 0)
    def _():
        rows = cuts * CUT
        window[0:EDGE, :] = jnp.zeros((EDGE, MIXED), F32)
        window[EDGE : 2 * EDGE, :] = dwindow[0:EDGE, :]
        din = taps_ref[CONV - 1 : CONV, :] * window[0:EDGE, :]
        for k in range(CONV - 1):
            din = din + taps_ref[k : k + 1, :] * window[3 - k : 3 - k + EDGE, :]
        dproj_ref[rows : rows + EDGE, 0:MIXED] = din
        dproj_ref[rows : rows + EDGE, MIXED:width] = jnp.zeros((EDGE, width - MIXED), F32)


def log_rows_to_columns(ref):
    return ref[...].T


def back(
    act, step, slope, logd, dy, local, entering, before, gin, gout, proj, taps, bias, a_log, skip,
    spreader, gatherer,
):
    rows = act.shape[0]
    cuts = rows // CUT
    width = proj.shape[1]

    def at(size):
        return pl.BlockSpec((CUT, size), lambda i: (cuts - 1 - i, 0))

    def halo(i):
        q = cuts - 1 - i
        return (jnp.where(q == 0, rows // EDGE, q * (CUT // EDGE) - 1), 0)

    return pl.pallas_call(
        back_kernel,
        grid=(cuts,),
        in_specs=[
            at(MIXED),
            at(HEADS),
            at(HEADS),
            at(HEADS),
            at(DI),
            pl.BlockSpec((1, STATE, DI), lambda i: (jnp.maximum(cuts - 2 - i, 0), 0, 0)),
            full((STATE, DI)),
            pl.BlockSpec((8, HEADS), lambda i: (cuts - 1 - i, 0)),
            pl.BlockSpec((1, STATE, DI), lambda i: (jnp.minimum(cuts - i, cuts - 1), 0, 0)),
            full((STATE, DI)),
            at(width),
            pl.BlockSpec((EDGE, width), halo),
            full((CONV, MIXED)),
            full((1, MIXED)),
            full((1, HEADS)),
            full((1, DI)),
            full((3 * HEADS, DI)),
            full((DI, HEADS)),
        ],
        out_specs=[
            full((rows + EDGE, width)),
            full((8 * CONV, MIXED)),
            full((8, MIXED)),
            full((8, HEADS)),
            full((8, HEADS)),
        ],
        out_shape=[
            jax.ShapeDtypeStruct((rows + EDGE, width), F32),
            jax.ShapeDtypeStruct((8 * CONV, MIXED), F32),
            jax.ShapeDtypeStruct((8, MIXED), F32),
            jax.ShapeDtypeStruct((8, HEADS), F32),
            jax.ShapeDtypeStruct((8, HEADS), F32),
        ],
        scratch_shapes=[
            pltpu.VMEM((CUT, DI), F32),
            pltpu.VMEM((CUT, DI), F32),
            pltpu.VMEM((CUT, DI), F32),
            pltpu.VMEM((HEADS, CUT), F32),
            pltpu.VMEM((HEADS, CUT), F32),
            pltpu.VMEM((CUT, CUT), F32),
            pltpu.VMEM((CUT, CUT), F32),
            pltpu.VMEM((CUT, CUT), F32),
            pltpu.VMEM((CUT, MIXED), F32),
            pltpu.VMEM((CUT + EDGE, MIXED), F32),
            pltpu.VMEM((CUT + EDGE, MIXED), F32),
            pltpu.VMEM((8, HEADS), F32),
        ],
        compiler_params=params(),
        cost_estimate=pl.CostEstimate(
            flops=60 * rows * STATE * DI, bytes_accessed=40_000_000, transcendentals=rows * CUT * HEADS
        ),
        name="back",
    )(
        act, step, slope, logd, dy, local, entering, before, gin, gout, proj, proj, taps, bias,
        a_log, skip, spreader, gatherer,
    )


def head_spreader():
    head = lax.broadcasted_iota(jnp.int32, (3 * HEADS, DI), 0) % HEADS
    return (head == lax.broadcasted_iota(jnp.int32, (3 * HEADS, DI), 1) // HDIM).astype(BF16)


def head_gatherer():
    channel = lax.broadcasted_iota(jnp.int32, (DI, HEADS), 0) // HDIM
    return (channel == lax.broadcasted_iota(jnp.int32, (DI, HEADS), 1)).astype(BF16)


def per_device(
    hidden_in,
    lengths,
    norm_gain,
    in_weight,
    conv_weight,
    conv_bias,
    dt_bias,
    a_log,
    skip_gain,
    gated_gain,
    out_weight,
    cotangent,
):
    width = hidden_in.shape[-1]
    devices = 1
    for axis in AXES:
        devices *= lax.axis_size(axis)
    mine, place = (lax.axis_index("p"), lax.axis_index("zc"))
    hidden = to_span(hidden_in, mine)
    rows = hidden.shape[0]
    own_rows = width // devices

    in_piece = in_weight.reshape(own_rows, -1)
    small = jnp.concatenate([conv_weight, conv_bias])
    extra = -(-small.shape[0] // own_rows)
    padded = jnp.pad(small, (0, extra * own_rows - small.shape[0])).reshape(own_rows, extra)
    w_conv = jnp.concatenate(
        gather_matrix(jnp.concatenate([in_piece[:, DI:], padded], axis=1)), axis=1
    )
    w_gate = jnp.concatenate(gather_matrix(in_piece[:, :DI]), axis=1)
    w_out = jnp.concatenate(gather_matrix(out_weight.reshape(-1, width)), axis=1)
    smalls = w_conv[:, RATED:].reshape(devices, own_rows * extra)
    taps = smalls[:, : conv_weight.shape[0]].reshape(CONV, MIXED)
    bias = smalls[:, conv_weight.shape[0] : small.shape[0]].reshape(1, MIXED)

    count = lax.axis_size("zc")
    edge = lax.ppermute(hidden[rows - EDGE :], "zc", [(i, i + 1) for i in range(count - 1)])
    extended = jnp.concatenate([hidden, edge], axis=0)
    scale = lax.rsqrt(jnp.mean(extended * extended, axis=1, keepdims=True) + epsilon)
    unit = extended * scale
    normed = unit * norm_gain
    spreader, gatherer = (head_spreader(), head_gatherer())
    dt_row, alog_row = (dt_bias.reshape(1, -1), a_log.reshape(1, -1))
    proj = nn(normed, w_conv)
    act, step, slope, logd, local, before, total = prepare(
        proj, taps, bias, dt_row, alog_row, spreader
    )
    total_row = jnp.repeat(total[0], HDIM).reshape(1, DI)
    entering = chain(total_row, local[-1], False)
    gate_in = nn(normed[:rows], w_gate)
    positions = place * rows + lax.iota(jnp.int32, rows)
    length = lax.dynamic_index_in_dim(lengths, mine, 0, keepdims=False)
    valid = (positions < length).astype(F32)[:, None]
    grad_out = to_span(cotangent, mine) * valid
    dng = nt(grad_out, w_out)
    skip_row = jnp.repeat(skip_gain, HDIM).reshape(1, DI)
    ng, dy, dz, gin, ggrad, skipg = mixer(
        act, step, logd, gate_in, dng, local, entering, before, skip_row,
        gated_gain.reshape(1, DI), spreader,
    )
    gout = chain(total_row, gin[0], True)
    grad_wout = scatter_matrix(tn(ng, grad_out))
    output = from_span((hidden + nn(ng, w_out)) * valid, mine)
    grad_wgate = scatter_matrix(tn(normed[:rows], dz))
    dproj, dtaps, dbias, dlog, ddtb = back(
        act, step, slope, logd, dy, local, entering, before, gin, gout, proj, taps, bias,
        alog_row, skip_row, spreader, gatherer,
    )
    dtaps = jnp.sum(dtaps.reshape(CONV, 8, MIXED), axis=1).reshape(devices, -1)
    dbias = jnp.sum(dbias, axis=0).reshape(devices, -1)
    dsmall = jnp.concatenate([dtaps, dbias], axis=1)
    dsmall = jnp.pad(dsmall, ((0, 0), (0, extra * own_rows - small.shape[0])))
    grad_wconv = scatter_matrix(
        jnp.concatenate([tn(normed, dproj)[:, :RATED], dsmall.reshape(width, extra)], axis=1)
    )
    dnormed = nt(dproj[:, :RATED], w_conv[:, :RATED])
    returned = lax.ppermute(dnormed[rows:], "zc", [(i + 1, i) for i in range(count - 1)])
    dnormed = dnormed[:rows] + nt(dz, w_gate)
    dnormed = jnp.concatenate([dnormed[: rows - EDGE], dnormed[rows - EDGE :] + returned], axis=0)
    unit = unit[:rows]
    dunit = dnormed * norm_gain
    dhidden = scale[:rows] * (dunit - unit * jnp.mean(dunit * unit, axis=1, keepdims=True))
    grad_input = from_span(grad_out + dhidden, mine)
    grad_skip = jnp.sum(jnp.sum(skipg, axis=0).reshape(HEADS, HDIM), axis=1)
    sums = jnp.concatenate(
        [
            jnp.sum(dnormed * unit, axis=0),
            jnp.sum(ggrad, axis=0),
            ddtb[0],
            dlog[0],
            grad_skip,
        ]
    )
    sums = sum_everywhere(jnp.pad(sums, (0, -sums.shape[0] % 128)).reshape(-1, 128)).reshape(-1)
    parts = []
    for size in (width, DI, HEADS, HEADS, HEADS):
        parts.append(sums[:size])
        sums = sums[size:]
    small_grad = grad_wconv[:, RATED:].reshape(-1)
    return (
        output,
        grad_input,
        parts[0],
        jnp.concatenate([grad_wgate, grad_wconv[:, :RATED]], axis=1).reshape(-1),
        small_grad[: conv_weight.shape[0]],
        small_grad[conv_weight.shape[0] : small.shape[0]],
        parts[2],
        parts[3],
        parts[4],
        parts[1],
        grad_wout.reshape(-1),
    )


def solution(mesh):
    dp, seq = (mesh.shape["dp"], mesh.shape["seq"])
    finer = Mesh(mesh.devices.reshape(dp // 2, 2, seq // 2, 2), AXES)
    over_dp, over_seq = (("y", "core"), ("zc", "p"))
    tokens = P(over_dp, over_seq, None)
    in_specs = (
        tokens, P(over_dp), P(), P(AXES), P(AXES), P(AXES), P(), P(), P(), P(), P(AXES), tokens,
    )
    out_specs = (
        tokens, tokens, P(), P(AXES), P(AXES), P(AXES), P(), P(), P(), P(), P(AXES),
    )
    return jax.shard_map(
        per_device, mesh=finer, in_specs=in_specs, out_specs=out_specs, check_vma=False
    )
```

time: 1390 us -> 773 us (0.56)
  waiting for transfers between devices: 703 us -> 263 us
  matrix products: 326 us -> 97.8 us
  Pallas kernels: 0 us -> 112 us
  starting transfers between devices: 8.12 us -> 120 us
  blocking collectives: 102 us -> 0 us
  other arithmetic: 124 us -> 34.7 us
  local copies, waits for them, and re-layouts: 99.1 us -> 131 us
    all_gather x4 -> x0, waiting for transfers between devices: 432 us -> none  [the longest x2 355 us: carried_in(): everything = jax.tree.map(lambda part: lax.all_gather(part, axis), value)]
    unnamed x6 -> x0, waiting for transfers between devices: 271 us -> none
    ppermute x2 -> x96, waiting for transfers between devices: 0.01 us -> 263 us  [the longest x82 230 us: shift(): lax.ppermute(block, axis, [(i, (i + step) % count) for i in range(count)])]
    dot_general x20 -> x9, matrix products: 326 us -> 97.8 us  [the longest x3 36.8 us: nn(): return jnp.dot(a, b, precision=precision, preferred_element_type=F32)]
    ppermute x2 -> x96, starting transfers between devices: 7.92 us -> 120 us  [the longest x82 84.5 us: shift(): lax.ppermute(block, axis, [(i, (i + step) % count) for i in range(count)])]
    pallas_call x0 -> x3, Pallas kernels: none -> 112 us  [the longest x1 54.8 us: back(): pl.pallas_call(back_kernel, grid=(cuts,), in_specs=[at(MIXED), at(HEADS),...]
    reshape x5 -> x16, local copies, waits for them, and re-layouts: 53.8 us -> 5.35 us  [the longest x3 2.11 us: gather_rows(): block = piece.reshape((1,) * len(AXES) + piece.shape)]
    psum x1 -> x0, blocking collectives: 44.2 us -> none  [per_device(): lax.psum((grad_ngain, grad_dtb, grad_alog, grad_skip, grad_ggain), ('dp',...]
  transfers between devices with their start and end apart: 7 -> 96, of which waited for: 4 -> 59; matrix products, arithmetic and copies ran while one was open for 19% -> 31% of each run, Pallas kernels for 0% -> 9%
where the time goes in v1:
time: 773 us; the launch traced here: 761 us
  waiting for transfers between devices  263 us (34%)
  local copies, waits for them, and re-layouts  131 us (17%)
  starting transfers between devices  120 us (16%)
  Pallas kernels  112 us (14%)
  matrix products  97.8 us (13%)
  other arithmetic  34.7 us (4%)
    ppermute x82, waiting for transfers between devices, shift(): lax.ppermute(block, axis, [(i, (i + step) % count) for i in range(count)])  230 us
    ppermute x82, starting transfers between devices, shift(): lax.ppermute(block, axis, [(i, (i + step) % count) for i in range(count)])  84.5 us
    pallas_call x1, Pallas kernels, back(): pl.pallas_call(back_kernel, grid=(cuts,), in_specs=[at(MIXED), at(HEADS),...  54.8 us
    pallas_call x1, Pallas kernels, mixer(): pl.pallas_call(mixer_kernel, grid=(cuts,), in_specs=[back(MIXED), back(HE...  45.1 us
    dot_general x3, matrix products, nn(): return jnp.dot(a, b, precision=precision, preferred_element_type=F32)  36.8 us
    dot_general x3, matrix products, nt(): lax.dot_general(a, b, (((1,), (1,)), ((), ())), precision=precision, pref...  30.9 us
    ppermute x12, starting transfers between devices, chain(): got = lax.ppermute(send, 'zc', route)  30.9 us
    dot_general x3, matrix products, tn(): lax.dot_general(a, b, (((0,), (0,)), ((), ())), precision=precision, pref...  30 us
  transfers between devices with their start and end apart: 96, of which 59 were waited for; matrix products, arithmetic and copies ran while one was open for 31% of the time, Pallas kernels for 9%

profile of v1, /device:TPU:8, one launch (start us, length us, event | category | flops | bytes accessed | tf_op | source)
XLA Modules:
  0.0 761.4 jit_solution(8907241552461519568)
XLA Ops:
  67.0 9.4 %collective-permute-done.23 = f32[1,1,4,1,32,1024]{5,4,2,3,1,0:T(8,128)S(1)} collective-permute-done((f32[1,1,4,1,32,1024]{5,4,2,3,1,0:T(8,128)S(1)}, f32[1,1,4,1,32,1024]{5,4,2,3,1,0:T(8,128)S(1)}, u32[]{:S(2)}, u32[]{:S(2)}) %collective-permute-start.23) | collective-permute-done | bytes 524320 | tf_op jit(solution)/shard_map/ppermute | solution.py:30
  97.9 5.9 collective-permute-done.5
  120.6 5.7 collective-permute-done.24
  132.4 16.4 %collective-permute-done.37 = f32[2,1,4,1,64,512]{5,4,0,2,3,1:T(8,128)S(1)} collective-permute-done((f32[2,1,4,1,64,512]{5,4,0,2,3,1:T(8,128)S(1)}, f32[2,1,4,1,64,512]{5,4,0,2,3,1:T(8,128)S(1)}, u32[]{:S(2)}, u32[]{:S(2)}) %collective-permute-start.37) | collective-permute-done | bytes 1048608 | tf_op jit(solution)/shard_map/ppermute | solution.py:30
  155.5 11.7 %collective-permute-done.6 = f32[1,1,4,2,32,1152]{5,4,3,2,1,0:T(8,128)S(1)} collective-permute-done((f32[1,1,4,2,32,1152]{5,4,3,2,1,0:T(8,128)S(1)}, f32[1,1,4,2,32,1152]{5,4,3,2,1,0:T(8,128)S(1)}, u32[]{:S(2)}, u32[]{:S(2)}) %collective-permute-start.6) | collective-permute-done | bytes 1179680 | tf_op jit(solution)/shard_map/ppermute | solution.py:30
  182.9 13.4 %fusion.3.proj_ref.edge_ref.halo_ref = f32[520,2348]{1,0:T(8,128)} fusion(f32[520,1024]{1,0:T(8,128)S(1)} %get-tuple-element.49, f32[1024,1152]{1,0:T(8,128)} %bitcast.499, f32[1024,1196]{1,0:T(8,128)} %bitcast.489), kind=kOutput, calls=%fused_computation.5 | convolution fusion | flops 7503982592 | bytes 16631168 | tf_op jit(solution)/shard_map/dot_general | solution.py:138
  196.3 11.7 %prepare.1 = (f32[512,2304]{1,0:T(8,128)}, f32[512,32]{1,0:T(8,128)S(1)}, f32[512,32]{1,0:T(8,128)S(1)}, f32[512,32]{1,0:T(8,128)S(1)}, f32[4,128,2048]{2,1,0:T(...) custom-call(f32[520,2348]{1,0:T(8,128)} %fusion.3.proj_ref.edge_ref.halo_ref, ...), custom_call_target="tpu_custom_call" | custom-call | flops 805306368 | bytes 24000000 | tf_op jit(solution)/shard_map/prepare/pallas_call | solution.py:259
  236.1 12.0 %fusion.7.gate_ref = f32[512,2048]{1,0:T(8,128)} fusion(f32[1024,1024]{1,0:T(8,128)S(1)} %bitcast.484, f32[1024,1024]{1,0:T(8,128)} %bitcast.486, f32[520,1024]{1,0:T(8,128)S(1)} %get-tuple-element.49), kind=kOutput, calls=%fused_computation.11 | convolution fusion | flops 6444548096 | bytes 14680064 | tf_op jit(solution)/shard_map/dot_general | solution.py:138
  268.6 8.8 %fusion.5.dng_ref = f32[512,2048]{1,0:T(8,128)} fusion(f32[2048,512]{1,0:T(8,128)S(1)} %bitcast.519, f32[2048,512]{1,0:T(8,128)S(1)} %bitcast.521, f32[256,1024]{1,0:T(8,128)S(1)} %copy-done.29, f32[256,1024]{1,0:T(8,128)S(1)} %copy-done.27, f32[512]{0:T(512)S(1)} %fusion.28), kind=kOutput, calls=%fused_computation.9 | convolution fusion | flops 6445596672 | bytes 14682112 | tf_op jit(solution)/shard_map/dot_general | solution.py:142
  278.6 45.1 %mixer.1 = (f32[512,2048]{1,0:T(8,128)}, f32[512,2048]{1,0:T(8,128)}, f32[512,2048]{1,0:T(8,128)}, f32[4,128,2048]{2,1,0:T(8,128)}, f32[8,2048]{1,0:T(8,128)S(1)}, /*index=5*/f32[8,2048]{1,0:T(8,128)S(1)}) custom-call(f32[512,2304]{1,0:T(8,128)} %get-tuple-element.29.act_ref, f32[512,32]{1,0:T(8,128)S(1)} %get-tuple-element.30.step_ref, ...), custom_call_target="tpu_custom_call" | custom-call | flops 4026531840 | bytes 38000000 | tf_op jit(solution)/shard_map/mixer/pallas_call | solution.py:410
  323.8 11.4 %fusion.9 = f32[512,1024]{1,0:T(8,128)S(1)} fusion(f32[256,1024]{1,0:T(8,128)S(1)} %copy-done.24, f32[256,1024]{1,0:T(8,128)S(1)} %copy-done.26, f32[512]{0:T(512)S(1)} %fusion.28, f32[512,2048]{1,0:T(8,128)} %get-tuple-element.35, f32[2048,512]{1,0:T(8,128)S(1)} %bitcast.520, f32[2048,512]{1,0:T(8,128)} %bitcast.522), kind=kOutput, calls=%fused_computation.26 | convolution fusion | flops 6446120960 | bytes 16779264 | tf_op jit(solution)/shard_map/dot_general | solution.py:138
  342.7 7.6 fusion.10
  350.3 7.5 fusion.14
  399.1 5.8 collective-permute-done.51
  405.9 54.8 %back.1 = (f32[520,2348]{1,0:T(8,128)}, f32[32,2304]{1,0:T(8,128)S(1)}, f32[8,2304]{1,0:T(8,128)S(1)}, f32[8,32]{1,0:T(8,128)S(1)}, f32[8,32]{1,0:T(8,128)S(1)}) custom-call(f32[512,2304]{1,0:T(8,128)} %get-tuple-element.29.act_ref, f32[512,32]{1,0:T(8,128)S(1)} %get-tuple-element.30.step_ref, f32[512,32]{1,0:T(8,128)S(1)} %get-tuple-element.36.slope_ref, ...), custom_call_target="tpu_custom_call" | custom-call | flops 8053063680 | bytes 40000000 | tf_op jit(solution)/shard_map/back/pallas_call | solution.py:642
  460.7 13.6 %fusion.1 = f32[520,1024]{1,0:T(8,128)S(1)} fusion(f32[1024,1196]{1,0:T(8,128)} %bitcast.490, f32[1024,1152]{1,0:T(8,128)} %bitcast.500, f32[520,2348]{1,0:T(8,128)} %get-tuple-element.39), kind=kOutput, calls=%fused_computation.4 | convolution fusion | flops 7465631744 | bytes 16631168 | tf_op jit(solution)/shard_map/dot_general | solution.py:142
  474.4 8.5 %slice_add_fusion = f32[512,1024]{1,0:T(8,128)} fusion(f32[520,1024]{1,0:T(8,128)S(1)} %fusion.1, f32[512,2048]{1,0:T(8,128)S(1)} %copy-done.22, f32[1024,1024]{1,0:T(8,128)S(1)} %bitcast.485, f32[1024,1024]{1,0:T(8,128)S(1)} %bitcast.487), kind=kOutput, calls=%fused_computation.24 | convolution fusion | flops 6445072384 | bytes 16777216 | tf_op jit(solution)/shard_map/dot_general | solution.py:142
  482.9 14.9 %fusion.40 = f32[1024,2348]{0,1:T(8,128)} fusion(f32[520,1024]{1,0:T(8,128)S(1)} %copy-done.4, f32[520,2348]{1,0:T(8,128)S(1)} %copy-done.61), kind=kOutput, calls=%fused_computation.249 | convolution fusion | flops 7501578240 | bytes 16631168 | tf_op jit(solution)/shard_map/dot_general | solution.py:148
  504.4 9.4 %slice.235 = f32[1024,2336]{0,1:T(8,128)} slice(f32[1024,2348]{0,1:T(8,128)} %fusion.40), slice={[0:1024], [0:2336]} | slice | bytes 19136512 | tf_op jit(solution)/shard_map/slice | solution.py:788
  515.2 5.4 pad_maximum_fusion.8
  520.7 5.9 copy.166
  531.2 5.2 slice.234
  536.4 6.1 copy.164
  575.7 15.9 %collective-permute-done.53 = f32[256,1024]{1,0:T(8,128)S(1)} collective-permute-done((f32[256,1024]{1,0:T(8,128)S(1)}, f32[256,1024]{1,0:T(8,128)S(1)}, u32[]{:S(2)}, u32[]{:S(2)}) %collective-permute-start.53) | collective-permute-done | bytes 1048608 | tf_op jit(solution)/shard_map/ppermute | solution.py:30
  596.2 17.9 %collective-permute-done.61 = f32[2,4,32,1024]{3,2,1,0:T(8,128)S(1)} collective-permute-done((f32[2,4,32,1024]{3,2,1,0:T(8,128)S(1)}, f32[2,4,32,1024]{3,2,1,0:T(8,128)S(1)}, u32[]{:S(2)}, u32[]{:S(2)}) %collective-permute-start.61) | collective-permute-done | bytes 1048608 | tf_op jit(solution)/shard_map/ppermute | solution.py:30
  617.8 18.6 %collective-permute-done.85 = f32[2,4,64,512]{3,2,1,0:T(8,128)S(1)} collective-permute-done((f32[2,4,64,512]{3,2,1,0:T(8,128)S(1)}, f32[2,4,64,512]{3,2,1,0:T(8,128)S(1)}, u32[]{:S(2)}, u32[]{:S(2)}) %collective-permute-start.85) | collective-permute-done | bytes 1048608 | tf_op jit(solution)/shard_map/ppermute | solution.py:30
  638.0 9.7 %collective-permute-done.68 = f32[4,32,1024]{2,1,0:T(8,128)S(1)} collective-permute-done((f32[4,32,1024]{2,1,0:T(8,128)S(1)}, f32[4,32,1024]{2,1,0:T(8,128)S(1)}, u32[]{:S(2)}, u32[]{:S(2)}) %collective-permute-start.68) | collective-permute-done | bytes 524320 | tf_op jit(solution)/shard_map/ppermute | solution.py:30
  649.4 8.6 %collective-permute-done.92 = f32[4,64,512]{2,1,0:T(8,128)S(1)} collective-permute-done((f32[4,64,512]{2,1,0:T(8,128)S(1)}, f32[4,64,512]{2,1,0:T(8,128)S(1)}, u32[]{:S(2)}, u32[]{:S(2)}) %collective-permute-start.92) | collective-permute-done | bytes 524320 | tf_op jit(solution)/shard_map/ppermute | solution.py:30
  693.6 17.4 %collective-permute-done.73 = f32[2,4,32,1152]{3,2,1,0:T(8,128)S(1)} collective-permute-done((f32[2,4,32,1152]{3,2,1,0:T(8,128)S(1)}, f32[2,4,32,1152]{3,2,1,0:T(8,128)S(1)}, u32[]{:S(2)}, u32[]{:S(2)}) %collective-permute-start.73) | collective-permute-done | bytes 1179680 | tf_op jit(solution)/shard_map/ppermute | solution.py:30
  712.7 10.4 %collective-permute-done.79 = f32[4,2,32,1196]{3,2,1,0:T(8,128)S(1)} collective-permute-done((f32[4,2,32,1196]{3,2,1,0:T(8,128)S(1)}, f32[4,2,32,1196]{3,2,1,0:T(8,128)S(1)}, u32[]{:S(2)}, u32[]{:S(2)}) %collective-permute-start.79) | collective-permute-done | bytes 1224736 | tf_op jit(solution)/shard_map/ppermute | solution.py:30
  724.6 7.2 collective-permute-done.74
  746.9 4.6 collective-permute-done.82
  (566 shorter events, 351.5 us)
Async XLA Ops:
  3.1 102.7 %collective-permute-start = (f32[256,1024]{1,0:T(8,128)}, f32[256,1024]{1,0:T(8,128)}, u32[]{:S(2)}, u32[]{:S(2)}) collective-permute-start(f32[256,1024]{1,0:T(8,128)} %dynamic-slice_bitcast_fusion.15), channel_id=1, source_target_pairs={{0,1},{1,0},{2,3},{3,2},{4,5},{5,4},{6,7},{7,6},{8,9},{9,8},{10,11... | collective-permute-start | bytes 3145736 | tf_op jit(solution)/shard_map/ppermute | solution.py:30
  5.6 23.7 %collective-permute-start.2 = (f32[1,1,1,1,32,1152]{5,4,3,2,1,0:T(8,128)}, f32[1,1,1,1,32,1152]{5,4,3,2,1,0:T(8,128)}, u32[]{:S(2)}, u32[]{:S(2)}) collective-permute-start(f32[1,1,1,1,32,1152]{5,4,3,2,1,0:T(8,128)} %slice_bitcast_fusion), channel_id=1, source_target_pairs={{0,2},{2,4},{4,6},{6,0},{1,3},{3,5},{5,7},{7,1},{8,10},{10,12},{12... | collective-permute-start | bytes 442376 | tf_op jit(solution)/shard_map/ppermute | solution.py:30
  7.5 24.5 %collective-permute-start.8 = (f32[1,1,1,1,32,1196]{5,4,3,2,1,0:T(8,128)S(1)}, f32[1,1,1,1,32,1196]{5,4,3,2,1,0:T(8,128)S(1)}, u32[]{:S(2)}, u32[]{:S(2)}) collective-permute-start(f32[1,1,1,1,32,1196]{5,4,3,2,1,0:T(8,128)S(1)} %fusion.24), channel_id=1, source_target_pairs={{0,2},{2,4},{4,6},{6,0},{1,3},{3,5},{5,7},{7,1},{8,10},{10,12},{12... | collective-permute-start | bytes 459272 | tf_op jit(solution)/shard_map/ppermute | solution.py:30
  25.6 83.0 %collective-permute-start.26 = (f32[256,1024]{1,0:T(8,128)S(1)}, f32[256,1024]{1,0:T(8,128)S(1)}, u32[]{:S(2)}, u32[]{:S(2)}) collective-permute-start(f32[256,1024]{1,0:T(8,128)S(1)} %dynamic-slice_bitcast_fusion.14), channel_id=1, source_target_pairs={{0,1},{1,0},{2,3},{3,2},{4,5},{5,4},{6,7},{7,6},{8,9},{9,8},{10,11... | collective-permute-start | bytes 3145736 | tf_op jit(solution)/shard_map/ppermute | solution.py:30
  63.7 22.7 %collective-permute-start.17 = (f32[1,1,4,1,32,1024]{5,4,2,3,1,0:T(8,128)S(1)}, f32[1,1,4,1,32,1024]{5,4,2,3,1,0:T(8,128)S(1)}, u32[]{:S(2)}, u32[]{:S(2)}) collective-permute-start(f32[1,1,4,1,32,1024]{5,4,2,3,1,0:T(8,128)S(1)} %bitcast.527), channel_id=1, source_target_pairs={{0,1},{1,0},{2,3},{3,2},{4,5},{5,4},{6,7},{7,6},{8,9},{9,8},{10,11... | collective-permute-start | bytes 1572872 | tf_op jit(solution)/shard_map/ppermute | solution.py:30
  86.4 24.5 %collective-permute-start.11 = (f32[1,1,4,1,32,1196]{5,4,2,3,1,0:T(8,128)S(1)}, f32[1,1,4,1,32,1196]{5,4,2,3,1,0:T(8,128)S(1)}, u32[]{:S(2)}, u32[]{:S(2)}) collective-permute-start(f32[1,1,4,1,32,1196]{5,4,2,3,1,0:T(8,128)S(1)} %bitcast.523), channel_id=1, source_target_pairs={{0,16},{16,0},{1,17},{17,1},{2,18},{18,2},{3,19},{19,3},{4,20},{20... | collective-permute-start | bytes 1837064 | tf_op jit(solution)/shard_map/ppermute | solution.py:30
  91.2 35.1 %collective-permute-start.24 = (f32[2,1,4,1,32,1024]{5,4,0,2,3,1:T(8,128)S(1)}, f32[2,1,4,1,32,1024]{5,4,0,2,3,1:T(8,128)S(1)}, u32[]{:S(2)}, u32[]{:S(2)}) collective-permute-start(f32[2,1,4,1,32,1024]{5,4,0,2,3,1:T(8,128)S(1)} %bitcast.516), channel_id=1, source_target_pairs={{0,1},{1,0},{2,3},{3,2},{4,5},{5,4},{6,7},{7,6},{8,9},{9,8},{10,11... | collective-permute-start | bytes 3145736 | tf_op jit(solution)/shard_map/ppermute | solution.py:30
  103.9 27.2 %collective-permute-start.18 = (f32[1,1,4,2,32,1024]{5,4,3,2,1,0:T(8,128)S(1)}, f32[1,1,4,2,32,1024]{5,4,3,2,1,0:T(8,128)S(1)}, u32[]{:S(2)}, u32[]{:S(2)}) collective-permute-start(f32[1,1,4,2,32,1024]{5,4,3,2,1,0:T(8,128)S(1)} %bitcast.515), channel_id=1, source_target_pairs={{0,16},{16,0},{1,17},{17,1},{2,18},{18,2},{3,19},{19,3},{4,20},{20... | collective-permute-start | bytes 3145736 | tf_op jit(solution)/shard_map/ppermute | solution.py:30
  105.8 43.0 %collective-permute-start.37 = (f32[2,1,4,1,64,512]{5,4,0,2,3,1:T(8,128)S(1)}, f32[2,1,4,1,64,512]{5,4,0,2,3,1:T(8,128)S(1)}, u32[]{:S(2)}, u32[]{:S(2)}) collective-permute-start(f32[2,1,4,1,64,512]{5,4,0,2,3,1:T(8,128)S(1)} %bitcast.517), channel_id=1, source_target_pairs={{0,1},{1,0},{2,3},{3,2},{4,5},{5,4},{6,7},{7,6},{8,9},{9,8},{10,11... | collective-permute-start | bytes 3145736 | tf_op jit(solution)/shard_map/ppermute | solution.py:30
  108.6 61.5 %collective-permute-start.31 = (f32[1,1,4,2,64,512]{5,4,3,2,1,0:T(8,128)S(1)}, f32[1,1,4,2,64,512]{5,4,3,2,1,0:T(8,128)S(1)}, u32[]{:S(2)}, u32[]{:S(2)}) collective-permute-start(f32[1,1,4,2,64,512]{5,4,3,2,1,0:T(8,128)S(1)} %bitcast.518), channel_id=1, source_target_pairs={{0,16},{16,0},{1,17},{17,1},{2,18},{18,2},{3,19},{19,3},{4,20},{20... | collective-permute-start | bytes 3145736 | tf_op jit(solution)/shard_map/ppermute | solution.py:30
  117.5 49.7 %collective-permute-start.6 = (f32[1,1,4,2,32,1152]{5,4,3,2,1,0:T(8,128)S(1)}, f32[1,1,4,2,32,1152]{5,4,3,2,1,0:T(8,128)S(1)}, u32[]{:S(2)}, u32[]{:S(2)}) collective-permute-start(f32[1,1,4,2,32,1152]{5,4,3,2,1,0:T(8,128)S(1)} %bitcast.514), channel_id=1, source_target_pairs={{0,16},{16,0},{1,17},{17,1},{2,18},{18,2},{3,19},{19,3},{4,20},{20... | collective-permute-start | bytes 3538952 | tf_op jit(solution)/shard_map/ppermute | solution.py:30
  126.4 43.6 %collective-permute-start.12 = (f32[2,1,4,1,32,1196]{5,4,2,0,3,1:T(8,128)S(1)}, f32[2,1,4,1,32,1196]{5,4,2,0,3,1:T(8,128)S(1)}, u32[]{:S(2)}, u32[]{:S(2)}) collective-permute-start(f32[2,1,4,1,32,1196]{5,4,2,0,3,1:T(8,128)S(1)} %bitcast.513), channel_id=1, source_target_pairs={{0,1},{1,0},{2,3},{3,2},{4,5},{5,4},{6,7},{7,6},{8,9},{9,8},{10,11... | collective-permute-start | bytes 3674120 | tf_op jit(solution)/shard_map/ppermute | solution.py:30
  131.1 82.4 %collective-permute-start.25 = (f32[2,1,4,2,32,1024]{5,4,3,2,0,1:T(8,128)}, f32[2,1,4,2,32,1024]{5,4,3,2,0,1:T(8,128)}, u32[]{:S(2)}, u32[]{:S(2)}) collective-permute-start(f32[2,1,4,2,32,1024]{5,4,3,2,0,1:T(8,128)} %bitcast.86), channel_id=1, source_target_pairs={{0,8},{8,0},{1,9},{9,1},{2,10},{10,2},{3,11},{11,3},{4,12},{12,4},... | collective-permute-start | bytes 6291464 | tf_op jit(solution)/shard_map/ppermute | solution.py:30
  148.8 76.9 %collective-permute-start.19 = (f32[2,1,4,2,32,1024]{5,4,3,2,0,1:T(8,128)}, f32[2,1,4,2,32,1024]{5,4,3,2,0,1:T(8,128)}, u32[]{:S(2)}, u32[]{:S(2)}) collective-permute-start(f32[2,1,4,2,32,1024]{5,4,3,2,0,1:T(8,128)} %bitcast.62), channel_id=1, source_target_pairs={{0,8},{8,0},{1,9},{9,1},{2,10},{10,2},{3,11},{11,3},{4,12},{12,4},... | collective-permute-start | bytes 6291464 | tf_op jit(solution)/shard_map/ppermute | solution.py:30
  167.2 84.2 %collective-permute-start.38 = (f32[2,1,4,2,64,512]{5,4,3,2,0,1:T(8,128)}, f32[2,1,4,2,64,512]{5,4,3,2,0,1:T(8,128)}, u32[]{:S(2)}, u32[]{:S(2)}) collective-permute-start(f32[2,1,4,2,64,512]{5,4,3,2,0,1:T(8,128)} %bitcast.136), channel_id=1, source_target_pairs={{0,8},{8,0},{1,9},{9,1},{2,10},{10,2},{3,11},{11,3},{4,12},{12,4},... | collective-permute-start | bytes 6291464 | tf_op jit(solution)/shard_map/ppermute | solution.py:30
  177.3 83.0 %collective-permute-start.32 = (f32[2,1,4,2,64,512]{5,4,3,2,0,1:T(8,128)}, f32[2,1,4,2,64,512]{5,4,3,2,0,1:T(8,128)}, u32[]{:S(2)}, u32[]{:S(2)}) collective-permute-start(f32[2,1,4,2,64,512]{5,4,3,2,0,1:T(8,128)} %bitcast.112), channel_id=1, source_target_pairs={{0,8},{8,0},{1,9},{9,1},{2,10},{10,2},{3,11},{11,3},{4,12},{12,4},... | collective-permute-start | bytes 6291464 | tf_op jit(solution)/shard_map/ppermute | solution.py:30
  336.3 57.9 %collective-permute-start.45 = (f32[256,1024]{1,0:T(8,128)}, f32[256,1024]{1,0:T(8,128)}, u32[]{:S(2)}, u32[]{:S(2)}) collective-permute-start(f32[256,1024]{1,0:T(8,128)} %dynamic-slice_bitcast_fusion.13), channel_id=1, source_target_pairs={{0,1},{1,0},{2,3},{3,2},{4,5},{5,4},{6,7},{7,6},{8,9},{9,8},{10,11... | collective-permute-start | bytes 3145736 | tf_op jit(solution)/shard_map/ppermute | solution.py:30
  371.8 190.3 %collective-permute-start.66 = (f32[2,4,2,32,1024]{4,3,2,1,0:T(8,128)}, f32[2,4,2,32,1024]{4,3,2,1,0:T(8,128)}, u32[]{:S(2)}, u32[]{:S(2)}) collective-permute-start(f32[2,4,2,32,1024]{4,3,2,1,0:T(8,128)} %dynamic-slice_bitcast_fusion.4), channel_id=1, source_target_pairs={{0,8},{8,0},{1,9},{9,1},{2,10},{10,2},{3,11},{11,3},{4,12},{12,4},... | collective-permute-start | bytes 6291464 | tf_op jit(solution)/shard_map/ppermute | solution.py:30
  373.2 192.2 %collective-permute-start.60 = (f32[2,4,2,32,1024]{4,3,2,1,0:T(8,128)}, f32[2,4,2,32,1024]{4,3,2,1,0:T(8,128)}, u32[]{:S(2)}, u32[]{:S(2)}) collective-permute-start(f32[2,4,2,32,1024]{4,3,2,1,0:T(8,128)} %dynamic-slice_bitcast_fusion.5), channel_id=1, source_target_pairs={{0,8},{8,0},{1,9},{9,1},{2,10},{10,2},{3,11},{11,3},{4,12},{12,4},... | collective-permute-start | bytes 6291464 | tf_op jit(solution)/shard_map/ppermute | solution.py:30
  390.0 179.0 %collective-permute-start.90 = (f32[2,4,2,64,512]{4,3,2,1,0:T(8,128)}, f32[2,4,2,64,512]{4,3,2,1,0:T(8,128)}, u32[]{:S(2)}, u32[]{:S(2)}) collective-permute-start(f32[2,4,2,64,512]{4,3,2,1,0:T(8,128)} %dynamic-slice_bitcast_fusion.2), channel_id=1, source_target_pairs={{0,8},{8,0},{1,9},{9,1},{2,10},{10,2},{3,11},{11,3},{4,12},{12,4},... | collective-permute-start | bytes 6291464 | tf_op jit(solution)/shard_map/ppermute | solution.py:30
  394.2 178.1 %collective-permute-start.84 = (f32[2,4,2,64,512]{4,3,2,1,0:T(8,128)}, f32[2,4,2,64,512]{4,3,2,1,0:T(8,128)}, u32[]{:S(2)}, u32[]{:S(2)}) collective-permute-start(f32[2,4,2,64,512]{4,3,2,1,0:T(8,128)} %dynamic-slice_bitcast_fusion.3), channel_id=1, source_target_pairs={{0,8},{8,0},{1,9},{9,1},{2,10},{10,2},{3,11},{11,3},{4,12},{12,4},... | collective-permute-start | bytes 6291464 | tf_op jit(solution)/shard_map/ppermute | solution.py:30
  560.1 127.5 %collective-permute-start.78 = (f32[2,4,2,32,1196]{4,3,2,1,0:T(8,128)}, f32[2,4,2,32,1196]{4,3,2,1,0:T(8,128)S(1)}, u32[]{:S(2)}, u32[]{:S(2)}) collective-permute-start(f32[2,4,2,32,1196]{4,3,2,1,0:T(8,128)} %dynamic-slice_bitcast_fusion), channel_id=1, source_target_pairs={{0,8},{8,0},{1,9},{9,1},{2,10},{10,2},{3,11},{11,3},{4,12},{12,4},... | collective-permute-start | bytes 7348232 | tf_op jit(solution)/shard_map/ppermute | solution.py:30
  562.0 122.4 %collective-permute-start.72 = (f32[2,4,2,32,1152]{4,3,2,1,0:T(8,128)}, f32[2,4,2,32,1152]{4,3,2,1,0:T(8,128)S(1)}, u32[]{:S(2)}, u32[]{:S(2)}) collective-permute-start(f32[2,4,2,32,1152]{4,3,2,1,0:T(8,128)} %dynamic-slice_bitcast_fusion.1), channel_id=1, source_target_pairs={{0,8},{8,0},{1,9},{9,1},{2,10},{10,2},{3,11},{11,3},{4,12},{12,4},... | collective-permute-start | bytes 7077896 | tf_op jit(solution)/shard_map/ppermute | solution.py:30
  565.5 26.1 %collective-permute-start.53 = (f32[256,1024]{1,0:T(8,128)S(1)}, f32[256,1024]{1,0:T(8,128)S(1)}, u32[]{:S(2)}, u32[]{:S(2)}) collective-permute-start(f32[256,1024]{1,0:T(8,128)S(1)} %copy-done.53), channel_id=1, source_target_pairs={{0,1},{1,0},{2,3},{3,2},{4,5},{5,4},{6,7},{7,6},{8,9},{9,8},{10,11... | collective-permute-start | bytes 3145736 | tf_op jit(solution)/shard_map/ppermute | solution.py:30
  569.0 26.1 %collective-permute-start.67 = (f32[4,2,32,1024]{3,2,1,0:T(8,128)S(1)}, f32[4,2,32,1024]{3,2,1,0:T(8,128)S(1)}, u32[]{:S(2)}, u32[]{:S(2)}) collective-permute-start(f32[4,2,32,1024]{3,2,1,0:T(8,128)S(1)} %dynamic-slice_bitcast_fusion.10), channel_id=1, source_target_pairs={{0,16},{16,0},{1,17},{17,1},{2,18},{18,2},{3,19},{19,3},{4,20},{20... | collective-permute-start | bytes 3145736 | tf_op jit(solution)/shard_map/ppermute | solution.py:30
  572.3 41.7 %collective-permute-start.61 = (f32[2,4,32,1024]{3,2,1,0:T(8,128)S(1)}, f32[2,4,32,1024]{3,2,1,0:T(8,128)S(1)}, u32[]{:S(2)}, u32[]{:S(2)}) collective-permute-start(f32[2,4,32,1024]{3,2,1,0:T(8,128)S(1)} %dynamic-slice_bitcast_fusion.11), channel_id=1, source_target_pairs={{0,1},{1,0},{2,3},{3,2},{4,5},{5,4},{6,7},{7,6},{8,9},{9,8},{10,11... | collective-permute-start | bytes 3145736 | tf_op jit(solution)/shard_map/ppermute | solution.py:30
  591.5 24.8 %collective-permute-start.91 = (f32[4,2,64,512]{3,2,1,0:T(8,128)S(1)}, f32[4,2,64,512]{3,2,1,0:T(8,128)S(1)}, u32[]{:S(2)}, u32[]{:S(2)}) collective-permute-start(f32[4,2,64,512]{3,2,1,0:T(8,128)S(1)} %dynamic-slice_bitcast_fusion.8), channel_id=1, source_target_pairs={{0,16},{16,0},{1,17},{17,1},{2,18},{18,2},{3,19},{19,3},{4,20},{20... | collective-permute-start | bytes 3145736 | tf_op jit(solution)/shard_map/ppermute | solution.py:30
  595.1 41.3 %collective-permute-start.85 = (f32[2,4,64,512]{3,2,1,0:T(8,128)S(1)}, f32[2,4,64,512]{3,2,1,0:T(8,128)S(1)}, u32[]{:S(2)}, u32[]{:S(2)}) collective-permute-start(f32[2,4,64,512]{3,2,1,0:T(8,128)S(1)} %dynamic-slice_bitcast_fusion.9), channel_id=1, source_target_pairs={{0,1},{1,0},{2,3},{3,2},{4,5},{5,4},{6,7},{7,6},{8,9},{9,8},{10,11... | collective-permute-start | bytes 3145736 | tf_op jit(solution)/shard_map/ppermute | solution.py:30
  614.0 33.7 %collective-permute-start.68 = (f32[4,32,1024]{2,1,0:T(8,128)S(1)}, f32[4,32,1024]{2,1,0:T(8,128)S(1)}, u32[]{:S(2)}, u32[]{:S(2)}) collective-permute-start(f32[4,32,1024]{2,1,0:T(8,128)S(1)} %dynamic-slice_bitcast_fusion.20), channel_id=1, source_target_pairs={{0,1},{1,0},{2,3},{3,2},{4,5},{5,4},{6,7},{7,6},{8,9},{9,8},{10,11... | collective-permute-start | bytes 1572872 | tf_op jit(solution)/shard_map/ppermute | solution.py:30
  616.4 32.9 %collective-permute-start.62 = (f32[4,32,1024]{2,1,0:T(8,128)S(1)}, f32[4,32,1024]{2,1,0:T(8,128)S(1)}, u32[]{:S(2)}, u32[]{:S(2)}) collective-permute-start(f32[4,32,1024]{2,1,0:T(8,128)S(1)} %dynamic-slice_bitcast_fusion.21), channel_id=1, source_target_pairs={{0,16},{16,0},{1,17},{17,1},{2,18},{18,2},{3,19},{19,3},{4,20},{20... | collective-permute-start | bytes 1572872 | tf_op jit(solution)/shard_map/ppermute | solution.py:30
  687.6 23.5 %collective-permute-start.73 = (f32[2,4,32,1152]{3,2,1,0:T(8,128)S(1)}, f32[2,4,32,1152]{3,2,1,0:T(8,128)S(1)}, u32[]{:S(2)}, u32[]{:S(2)}) collective-permute-start(f32[2,4,32,1152]{3,2,1,0:T(8,128)S(1)} %dynamic-slice_bitcast_fusion.7), channel_id=1, source_target_pairs={{0,1},{1,0},{2,3},{3,2},{4,5},{5,4},{6,7},{7,6},{8,9},{9,8},{10,11... | collective-permute-start | bytes 3538952 | tf_op jit(solution)/shard_map/ppermute | solution.py:30
  691.4 31.7 %collective-permute-start.79 = (f32[4,2,32,1196]{3,2,1,0:T(8,128)S(1)}, f32[4,2,32,1196]{3,2,1,0:T(8,128)S(1)}, u32[]{:S(2)}, u32[]{:S(2)}) collective-permute-start(f32[4,2,32,1196]{3,2,1,0:T(8,128)S(1)} %dynamic-slice_bitcast_fusion.6), channel_id=1, source_target_pairs={{0,16},{16,0},{1,17},{17,1},{2,18},{18,2},{3,19},{19,3},{4,20},{20... | collective-permute-start | bytes 3674120 | tf_op jit(solution)/shard_map/ppermute | solution.py:30
  (132 other events, 1563.6 us)

commit v2 on v1

v2 whole, which is shorter than its diff:
```python
import functools

import jax
import jax.numpy as jnp
from jax import lax
from jax.experimental import pallas as pl
from jax.experimental.pallas import tpu as pltpu
from jax.sharding import Mesh
from jax.sharding import PartitionSpec as P

DI = 2048
HEADS = 32
HDIM = 64
STATE = 128
CONV = 4
MIXED = DI + 2 * STATE
RATED = MIXED + HEADS
CUT = 128
EDGE = 8
PAIR = 2 * HDIM
SPARE = 128 - HEADS
WIDE = RATED + SPARE
STRIP = 128
BLOCK = 512
F32 = jnp.float32
BF16 = jnp.bfloat16
HIGH = lax.Precision.HIGH
EXACT = lax.Precision.HIGHEST
epsilon = 1e-05
FREE = pl.CostEstimate(flops=0, bytes_accessed=0, transcendentals=0)


def shift(block, axis, step=1):
    count = lax.axis_size(axis)
    return lax.ppermute(block, axis, [(i, (i + step) % count) for i in range(count)])


AXES = ("y", "core", "zc", "p")


def offsets(block, axis):
    count = lax.axis_size(axis)
    return [block] + [shift(block, axis, k) for k in range(1, count)]


def ring(block, axis):
    held = [block]
    for _ in range(1, lax.axis_size(axis)):
        held.append(shift(held[-1], axis))
    return held


def after(value, *others):
    return lax.optimization_barrier((value,) + others)[0]


def place_kernel(count, own_rows, where_ref, *refs):
    blocks, whole = (refs[:count], refs[count])
    spot = 0
    for block in blocks:
        for k in range(block.shape[0] // own_rows):
            at = pl.multiple_of(where_ref[spot] * own_rows, own_rows)
            whole[pl.ds(at, own_rows), :] = block[k * own_rows : (k + 1) * own_rows, :]
            spot += 1


def place(blocks, own_rows):
    sizes = {axis: lax.axis_size(axis) for axis in AXES}
    index = {axis: lax.axis_index(axis) for axis in AXES}
    devices = 1
    for axis in AXES:
        devices *= sizes[axis]
    where = []
    for slot, lines, _ in blocks:
        for k in lines:
            at = 0
            for axis in AXES:
                back = k if axis == "zc" else slot.get(axis, 0)
                at = at * sizes[axis] + (index[axis] - back) % sizes[axis]
            where.append(at)
    arrays = [block for _, _, block in blocks]
    cols = arrays[0].shape[1]
    if own_rows % 8:
        whole = jnp.zeros((devices, own_rows, cols), F32)
        spots = iter(where)
        for block in arrays:
            for k in range(block.shape[0] // own_rows):
                whole = lax.dynamic_update_slice_in_dim(
                    whole, block[None, k * own_rows : (k + 1) * own_rows], next(spots), 0
                )
        return whole.reshape(devices * own_rows, cols)
    return pl.pallas_call(
        functools.partial(place_kernel, len(blocks), own_rows),
        in_specs=[pl.BlockSpec(memory_space=pltpu.SMEM)]
        + [pl.BlockSpec(memory_space=pltpu.VMEM)] * len(blocks),
        out_specs=pl.BlockSpec(memory_space=pltpu.VMEM),
        out_shape=jax.ShapeDtypeStruct((devices * own_rows, cols), F32),
        compiler_params=pltpu.CompilerParams(vmem_limit_bytes=32 * 1024 * 1024),
        cost_estimate=FREE,
        name="place",
    )(jnp.stack(where).astype(jnp.int32), *arrays)


def tied(values, *others):
    return list(lax.optimization_barrier((tuple(values), tuple(others)))[0])


class Gather:
    def __init__(self, piece):
        self.piece, self.rows = (piece, piece.shape[0])

    def line(self, *tie):
        (piece,) = tied([self.piece], *tie)
        self.lines = list(range(lax.axis_size("zc")))
        self.block = jnp.concatenate(offsets(piece, "zc"), axis=0)

    def line_at_once(self, *tie):
        (piece,) = tied([self.piece], *tie)
        count, index = (lax.axis_size("zc"), lax.axis_index("zc"))
        whole = lax.all_to_all(jnp.broadcast_to(piece, (count,) + piece.shape), "zc", 0, 0)
        self.lines = [index - k for k in range(count)]
        self.block = whole.reshape(-1, piece.shape[1])

    def near(self, *tie):
        (block,) = tied([self.block], *tie)
        self.rings = {axis: ring(block, axis)[1:] for axis in ("p", "y")}
        return [b for r in self.rings.values() for b in r]

    def far(self, *tie):
        middle = len(self.lines) // 2
        cut = middle * self.rows
        sides = {"p": [b[:cut] for b in self.rings["p"]], "y": [b[cut:] for b in self.rings["y"]]}
        other = {"p": "y", "y": "p"}
        self.corners = []
        for axis, blocks in sides.items():
            lines = self.lines[:middle] if axis == "p" else self.lines[middle:]
            blocks = tied(blocks, *tie)
            for k, block in enumerate(blocks):
                for n, moved in enumerate(ring(block, other[axis])[1:]):
                    self.corners.append(({axis: k + 1, other[axis]: n + 1}, lines, moved))
        return [b for _, _, b in self.corners]

    def held_near(self):
        near = [
            ({axis: k + 1}, self.lines, b) for axis, r in self.rings.items() for k, b in enumerate(r)
        ]
        return [({}, self.lines, self.block)] + near

    def held(self):
        return self.held_near() + self.corners

    def across(self, blocks, *tie):
        arrays = tied([b for _, _, b in blocks], *tie)
        return [
            ({**slot, "core": 1}, lines, shift(b, "core"))
            for (slot, lines, _), b in zip(blocks, arrays)
        ]


def indexed(addends, at, dim):
    total = None
    for addend in addends:
        part = lax.dynamic_index_in_dim(addend, at, dim, keepdims=False)
        total = part if total is None else total + part
    return total


class Scatter:
    def __init__(self, send, keep):
        self.shape = [lax.axis_size(a) for a in ("y", "zc", "p")] + [-1, keep.shape[-1]]
        moved = shift(send, "core")
        self.came = [moved]
        both = [keep.reshape(self.shape), moved.reshape(self.shape)]
        middle = self.shape[1] // 2
        self.parts = [
            ([v[:, :middle] for v in both], ["y", "zc", "p"]),
            ([v[:, middle:] for v in both], ["y", "zc", "p"]),
        ]

    def stage(self, axes, *tie):
        self.came, parts = ([], [])
        for (addends, left), axis in zip(self.parts, axes):
            count, index, dim = (lax.axis_size(axis), lax.axis_index(axis), left.index(axis))
            came = []
            for k in range(1, count):
                moving = indexed(addends, (index + k) % count, dim)
                if tie:
                    moving = after(moving, *tie)
                came.append(shift(moving, axis, k))
            kept = [lax.dynamic_index_in_dim(v, index, dim, keepdims=False) for v in addends]
            parts.append((kept + came, [a for a in left if a != axis]))
            self.came += came
        self.parts = parts

    def last(self, *tie):
        count, index = (lax.axis_size("zc"), lax.axis_index("zc"))
        line = jnp.concatenate([functools.reduce(jnp.add, v) for v, _ in self.parts], axis=0)
        if tie:
            line = after(line, *tie)
        self.came = [
            shift(lax.dynamic_index_in_dim(line, (index + k) % count, 0, keepdims=False), "zc", k)
            for k in range(1, count)
        ]
        self.kept = lax.dynamic_index_in_dim(line, index, 0, keepdims=False)

    def last_at_once(self, *tie):
        line = jnp.concatenate([functools.reduce(jnp.add, v) for v, _ in self.parts], axis=0)
        (line,) = tied([line], *tie)
        line = lax.all_to_all(line, "zc", 0, 0)
        self.came, self.kept = ([line[k] for k in range(1, line.shape[0])], line[0])

    def result(self):
        return functools.reduce(jnp.add, self.came, self.kept)


def sum_everywhere(values):
    for axis in ("core", "p", "y", "zc"):
        count, index = (lax.axis_size(axis), lax.axis_index(axis))
        if count == 2:
            values = values + shift(values, axis)
        else:
            held = jnp.stack(offsets(values, axis))
            total = None
            for k in range(count):
                part = lax.dynamic_index_in_dim(held, (index - k) % count, 0, keepdims=False)
                total = part if total is None else total + part
            values = total
    return values


def to_span(block, mine):
    keep = lax.dynamic_index_in_dim(block, mine, 0, keepdims=False)
    other = shift(lax.dynamic_index_in_dim(block, 1 - mine, 0, keepdims=False), "p")
    first = mine == 0
    return jnp.concatenate([jnp.where(first, keep, other), jnp.where(first, other, keep)], axis=0)


def from_span(span, mine):
    block = span.reshape(2, -1, span.shape[-1])
    keep = lax.dynamic_index_in_dim(block, mine, 0, keepdims=False)
    other = shift(lax.dynamic_index_in_dim(block, 1 - mine, 0, keepdims=False), "p")
    first = mine == 0
    return jnp.stack([jnp.where(first, keep, other), jnp.where(first, other, keep)], axis=0)


class States:
    chunks = 1

    def __init__(self, decay, added, reverse):
        self.count, self.reverse, self.distance = (lax.axis_size("zc"), reverse, 1)
        rows = added.shape[0] // self.chunks
        decay = jnp.broadcast_to(decay, (8, added.shape[1]))
        self.decay = decay
        self.added = [added[k * rows : (k + 1) * rows] for k in range(self.chunks)]
        self.held = [None] * self.chunks
        self.span = None

    def send(self, *tie):
        w = self.distance
        pairs = [(i, i + w) for i in range(self.count - w)]
        route = [(b, a) if self.reverse else (a, b) for a, b in pairs]
        came = []
        for k in range(self.chunks):
            block = self.added[k]
            if self.held[k] is not None:
                block = block + self.decay[0:1] * self.held[k]
            if k == 0 and 2 * w < self.count:
                span = self.decay if self.span is None else self.decay * self.span
                block = jnp.concatenate([block, span], axis=0)
            if tie:
                block = after(block, *tie)
            came.append(lax.ppermute(block, "zc", route))
        rows = self.added[0].shape[0]
        for k in range(self.chunks):
            new = came[k][:rows]
            if self.held[k] is not None:
                new = self.held[k] + self.span[0:1] * new
            self.held[k] = new
        if 2 * w < self.count:
            span = came[0][rows:]
            self.span = span if self.span is None else self.span * span
        self.distance = 2 * w
        return came

    def result(self, *tie):
        while self.distance < self.count:
            self.send(*tie)
        return jnp.concatenate(self.held, axis=0)


def nn(a, b, precision=HIGH):
    return jnp.dot(a, b, precision=precision, preferred_element_type=F32)


def nt(a, b, precision=HIGH):
    return lax.dot_general(
        a, b, (((1,), (1,)), ((), ())), precision=precision, preferred_element_type=F32
    )


def tn(a, b, precision=HIGH):
    return lax.dot_general(
        a, b, (((0,), (0,)), ((), ())), precision=precision, preferred_element_type=F32
    )


def bf16_dot(a, b):
    return jnp.dot(a, b, preferred_element_type=F32)


def split_heads(values):
    top = values.astype(BF16)
    rest = values - top.astype(F32)
    mid = rest.astype(BF16)
    low = (rest - mid.astype(F32)).astype(BF16)
    return jnp.concatenate([top, mid, low], axis=1)


def spread_heads(values, spreader):
    return bf16_dot(split_heads(values), spreader)


def sum_heads(values, gatherer):
    top = values.astype(BF16)
    low = (values - top.astype(F32)).astype(BF16)
    return jnp.dot(top, gatherer, preferred_element_type=F32) + jnp.dot(
        low, gatherer, preferred_element_type=F32
    )


def order_mask(shape, kind):
    row, column = (lax.broadcasted_iota(jnp.int32, shape, d) for d in (0, 1))
    return {"ge": row >= column, "gt": row > column, "le": row <= column, "lt": row < column}[kind]


def triangle(kind):
    return jnp.where(order_mask((CUT, CUT), kind), 1.0, 0.0).astype(F32)


def conv_chunk(window_ref, taps_ref, bias_ref, cols):
    total = bias_ref[:, cols] + taps_ref[0:1, cols] * window_ref[EDGE - 3 : EDGE - 3 + CUT, cols]
    for k in range(1, CONV):
        at = EDGE - 3 + k
        total = total + taps_ref[k : k + 1, cols] * window_ref[at : at + CUT, cols]
    return total


def prepare_kernel(
    proj_ref,
    edge_ref,
    taps_ref,
    bias_ref,
    dtb_ref,
    alog_ref,
    spreader_ref,
    act_ref,
    step_ref,
    slope_ref,
    logd_ref,
    local_ref,
    before_ref,
    total_ref,
    window,
    state,
    logs,
):
    q = pl.program_id(0)

    @pl.when(q == 0)
    def _():
        window[0:EDGE, :] = edge_ref[:, 0:MIXED]
        state[...] = jnp.zeros_like(state)
        logs[...] = jnp.zeros_like(logs)

    @pl.when(q > 0)
    def _():
        window[0:EDGE, :] = window[CUT : CUT + EDGE, :]

    window[EDGE : EDGE + CUT, :] = proj_ref[:, 0:MIXED]

    def conv(c, carry):
        cols = pl.ds(pl.multiple_of(c * STRIP, STRIP), STRIP)
        out = conv_chunk(window, taps_ref, bias_ref, cols)
        act_ref[:, cols] = out * jax.nn.sigmoid(out)
        return carry

    lax.fori_loop(0, MIXED // STRIP, conv, 0, unroll=3)
    raw = proj_ref[:, MIXED:RATED] + dtb_ref[...]
    step = jnp.maximum(raw, 0.0) + jnp.log1p(jnp.exp(-jnp.abs(raw)))
    logd = nn(triangle("ge"), -jnp.exp(alog_ref[...]) * step, EXACT)
    step_ref[...] = step
    slope_ref[...] = jax.nn.sigmoid(raw)
    logd_ref[...] = logd
    last = logd[CUT - 1 : CUT, :]
    tail = spread_heads(jnp.exp(last - logd) * step, spreader_ref[...])
    added = tn(act_ref[:, DI : DI + STATE], act_ref[:, 0:DI] * tail)
    decay = spread_heads(jnp.broadcast_to(jnp.exp(last), (8, HEADS)), spreader_ref[...])
    state[...] = state[...] * decay[0:1, :] + added
    local_ref[0] = state[...]
    before_ref[...] = jnp.exp(logs[...])
    logs[...] = logs[...] + jnp.broadcast_to(last, (8, HEADS))
    total_ref[...] = jnp.exp(logs[...])


def full(shape):
    return pl.BlockSpec(shape, lambda i: (0,) * len(shape))


def params():
    return pltpu.CompilerParams(
        dimension_semantics=("arbitrary",), vmem_limit_bytes=52 * 1024 * 1024
    )


def prepare(proj, taps, bias, dt_bias, a_log, spreader):
    rows = proj.shape[0] - EDGE
    cuts = rows // CUT
    return pl.pallas_call(
        prepare_kernel,
        grid=(cuts,),
        in_specs=[
            pl.BlockSpec((CUT, WIDE), lambda i: (i, 0)),
            pl.BlockSpec((EDGE, WIDE), lambda i: (rows // EDGE, 0)),
            full((CONV, MIXED)),
            full((1, MIXED)),
            full((1, HEADS)),
            full((1, HEADS)),
            full((3 * HEADS, DI)),
        ],
        out_specs=[
            pl.BlockSpec((CUT, MIXED), lambda i: (i, 0)),
            pl.BlockSpec((CUT, HEADS), lambda i: (i, 0)),
            pl.BlockSpec((CUT, HEADS), lambda i: (i, 0)),
            pl.BlockSpec((CUT, HEADS), lambda i: (i, 0)),
            pl.BlockSpec((1, STATE, DI), lambda i: (i, 0, 0)),
            pl.BlockSpec((8, HEADS), lambda i: (i, 0)),
            full((8, HEADS)),
        ],
        out_shape=[
            jax.ShapeDtypeStruct((rows, MIXED), F32),
            jax.ShapeDtypeStruct((rows, HEADS), F32),
            jax.ShapeDtypeStruct((rows, HEADS), F32),
            jax.ShapeDtypeStruct((rows, HEADS), F32),
            jax.ShapeDtypeStruct((cuts, STATE, DI), F32),
            jax.ShapeDtypeStruct((8 * cuts, HEADS), F32),
            jax.ShapeDtypeStruct((8, HEADS), F32),
        ],
        scratch_shapes=[
            pltpu.VMEM((CUT + EDGE, MIXED), F32),
            pltpu.VMEM((STATE, DI), F32),
            pltpu.VMEM((8, HEADS), F32),
        ],
        compiler_params=params(),
        cost_estimate=FREE,
        name="prepare",
    )(proj, proj, taps, bias, dt_bias, a_log, spreader)


def both_columns(pair, left):
    turned = pltpu.roll(pair, HDIM, 1)
    return (jnp.where(left, pair, turned), jnp.where(left, turned, pair))


def stacked_pair(pair, left):
    zero = jnp.zeros_like(pair)
    return jnp.concatenate([jnp.where(left, pair, zero), jnp.where(left, zero, pair)], axis=0)


UNROLL = 8


def intra_kernel(
    act_ref, step_ref, logd_ref, skip_ref, spreader_ref, out_ref, logx, weighted, log_rows, scores
):
    spreader = spreader_ref[...]
    logd = logd_ref[...]
    logx[...] = spread_heads(logd, spreader)
    log_rows[...] = logd.T
    heads_in = act_ref[:, 0:DI]
    weighted[...] = heads_in * spread_heads(step_ref[...], spreader)
    scores[...] = nt(act_ref[:, DI + STATE : MIXED], act_ref[:, DI : DI + STATE])

    def pair(j, carry):
        cols = pl.ds(pl.multiple_of(j * PAIR, PAIR), PAIR)
        left = lax.broadcasted_iota(jnp.int32, (CUT, PAIR), 1) < HDIM
        mask = order_mask((CUT, CUT), "ge")
        mixes = []
        for side, column in enumerate(both_columns(logx[:, cols], left)):
            row = log_rows[pl.ds(2 * j + side, 1), :]
            mixes.append(jnp.exp(jnp.where(mask, column - row, -1e30)) * scores[...])
        out_ref[:, cols] = skip_ref[:, cols] * act_ref[:, cols] + nn(
            jnp.concatenate(mixes, axis=1), stacked_pair(weighted[:, cols], left)
        )
        return carry

    lax.fori_loop(0, HEADS // 2, pair, 0, unroll=UNROLL)


def intra(act, step, logd, skip, spreader):
    rows = act.shape[0]

    def at(width):
        return pl.BlockSpec((CUT, width), lambda i: (i, 0))

    return pl.pallas_call(
        intra_kernel,
        grid=(rows // CUT,),
        in_specs=[at(MIXED), at(HEADS), at(HEADS), full((1, DI)), full((3 * HEADS, DI))],
        out_specs=at(DI),
        out_shape=jax.ShapeDtypeStruct((rows, DI), F32),
        scratch_shapes=[
            pltpu.VMEM((CUT, DI), F32),
            pltpu.VMEM((CUT, DI), F32),
            pltpu.VMEM((HEADS, CUT), F32),
            pltpu.VMEM((CUT, CUT), F32),
        ],
        compiler_params=params(),
        cost_estimate=FREE,
        name="intra",
    )(act, step, logd, skip, spreader)


def mixer_kernel(
    act_ref,
    logd_ref,
    inner_ref,
    gate_ref,
    dng_ref,
    local_ref,
    enter_ref,
    before_ref,
    ggain_ref,
    spreader_ref,
    ng_ref,
    dy_ref,
    dz_ref,
    gin_ref,
    ggrad_ref,
    skipg_ref,
    grown,
    out,
    gstate,
):
    i = pl.program_id(0)
    q = pl.num_programs(0) - 1 - i
    spreader = spreader_ref[...]

    @pl.when(i == 0)
    def _():
        gstate[...] = jnp.zeros_like(gstate)
        ggrad_ref[...] = jnp.zeros_like(ggrad_ref)
        skipg_ref[...] = jnp.zeros_like(skipg_ref)

    logd = logd_ref[...]
    grown[...] = spread_heads(jnp.exp(logd), spreader)
    before = spread_heads(before_ref[...], spreader)[0:1, :]
    entering = enter_ref[...] * before + jnp.where(q == 0, 0.0, local_ref[0])
    c_state = act_ref[:, DI + STATE : MIXED]
    out[...] = grown[...] * nn(c_state, entering) + inner_ref[...]

    def gate(k, carry):
        rows = pl.ds(pl.multiple_of(k * 8, 8), 8)
        ssd = out[rows, :]
        gate_in = gate_ref[rows, :]
        sg = jax.nn.sigmoid(gate_in)
        silu = gate_in * sg
        gated = ssd * silu
        scale = lax.rsqrt(jnp.mean(gated * gated, axis=1, keepdims=True) + epsilon)
        unit = gated * scale
        ng_ref[rows, :] = unit * ggain_ref[...]
        dng = dng_ref[rows, :]
        e = dng * ggain_ref[...]
        ggrad_ref[...] += dng * unit
        dgated = scale * (e - unit * jnp.mean(e * unit, axis=1, keepdims=True))
        dy = dgated * silu
        dy_ref[rows, :] = dy
        dz_ref[rows, :] = dgated * ssd * (sg * (1.0 + gate_in * (1.0 - sg)))
        skipg_ref[...] += dy * act_ref[rows, 0:DI]
        return carry

    lax.fori_loop(0, CUT // 8, gate, 0, unroll=GATE_UNROLL)
    gstate[...] = gstate[...] * grown[CUT - 1 : CUT, :] + tn(c_state, grown[...] * dy_ref[...])
    gin_ref[0] = gstate[...]


GATE_UNROLL = 4


def mixer(act, logd, inner, gate_in, dng, local, entering, before, ggain, spreader):
    rows = act.shape[0]
    cuts = rows // CUT

    def back(width):
        return pl.BlockSpec((CUT, width), lambda i: (cuts - 1 - i, 0))

    wide = jax.ShapeDtypeStruct((rows, DI), F32)
    return pl.pallas_call(
        mixer_kernel,
        grid=(cuts,),
        in_specs=[
            back(MIXED),
            back(HEADS),
            back(DI),
            back(DI),
            back(DI),
            pl.BlockSpec((1, STATE, DI), lambda i: (jnp.maximum(cuts - 2 - i, 0), 0, 0)),
            full((STATE, DI)),
            pl.BlockSpec((8, HEADS), lambda i: (cuts - 1 - i, 0)),
            full((1, DI)),
            full((3 * HEADS, DI)),
        ],
        out_specs=[
            back(DI),
            back(DI),
            back(DI),
            pl.BlockSpec((1, STATE, DI), lambda i: (cuts - 1 - i, 0, 0)),
            full((8, DI)),
            full((8, DI)),
        ],
        out_shape=[
            wide,
            wide,
            wide,
            jax.ShapeDtypeStruct((cuts, STATE, DI), F32),
            jax.ShapeDtypeStruct((8, DI), F32),
            jax.ShapeDtypeStruct((8, DI), F32),
        ],
        scratch_shapes=[
            pltpu.VMEM((CUT, DI), F32),
            pltpu.VMEM((CUT, DI), F32),
            pltpu.VMEM((STATE, DI), F32),
        ],
        compiler_params=params(),
        cost_estimate=FREE,
        name="mixer",
    )(act, logd, inner, gate_in, dng, local, entering, before, ggain, spreader)


def back_intra_kernel(
    act_ref,
    step_ref,
    logd_ref,
    dy_ref,
    spreader_ref,
    dweighted_ref,
    dstates_ref,
    moved_ref,
    logx,
    weighted,
    log_rows,
    sum_rows,
    scores,
    dscores,
    sum_columns,
):
    spreader = spreader_ref[...]
    logd = logd_ref[...]
    logx[...] = spread_heads(logd, spreader)
    log_rows[...] = logd.T
    weighted[...] = act_ref[:, 0:DI] * spread_heads(step_ref[...], spreader)
    b_state = act_ref[:, DI : DI + STATE]
    c_state = act_ref[:, DI + STATE : MIXED]
    scores[...] = nt(b_state, c_state)
    dscores[...] = jnp.zeros_like(dscores)
    sum_columns[...] = jnp.zeros_like(sum_columns)

    def pair(j, carry):
        cols = pl.ds(pl.multiple_of(j * PAIR, PAIR), PAIR)
        left = lax.broadcasted_iota(jnp.int32, (CUT, PAIR), 1) < HDIM
        mask = order_mask((CUT, CUT), "le")
        strict = order_mask((CUT, CUT), "lt")
        dy = dy_ref[:, cols]
        dmix = nt(stacked_pair(weighted[:, cols], left), dy)
        mixes = []
        lane = lax.broadcasted_iota(jnp.int32, (CUT, CUT), 1)
        for side, column in enumerate(both_columns(logx[:, cols], left)):
            row = log_rows[pl.ds(2 * j + side, 1), :]
            weights = jnp.exp(jnp.where(mask, row - column, -1e30))
            mixes.append(weights * scores[...])
            part = dmix[side * CUT : (side + 1) * CUT, :] * weights
            dscores[...] += part
            moved = jnp.where(strict, part * scores[...], 0.0)
            sum_rows[pl.ds(2 * j + side, 1), :] = jnp.sum(moved, axis=0, keepdims=True)
            sum_columns[...] += jnp.where(
                lane == 2 * j + side, jnp.sum(moved, axis=1, keepdims=True), 0.0
            )
        dweighted_ref[:, cols] = nn(jnp.concatenate(mixes, axis=1), stacked_pair(dy, left))
        return carry

    lax.fori_loop(0, HEADS // 2, pair, 0, unroll=BACK_UNROLL)
    dstates_ref[:, 0:STATE] = nn(dscores[...], c_state)
    dstates_ref[:, STATE : 2 * STATE] = tn(dscores[...], b_state)
    moved_ref[...] = sum_rows[...].T - sum_columns[:, 0:HEADS]


BACK_UNROLL = 4


def back_intra(act, step, logd, dy, spreader):
    rows = act.shape[0]

    def at(width):
        return pl.BlockSpec((CUT, width), lambda i: (i, 0))

    return pl.pallas_call(
        back_intra_kernel,
        grid=(rows // CUT,),
        in_specs=[at(MIXED), at(HEADS), at(HEADS), at(DI), full((3 * HEADS, DI))],
        out_specs=[at(DI), at(2 * STATE), at(HEADS)],
        out_shape=[
            jax.ShapeDtypeStruct((rows, DI), F32),
            jax.ShapeDtypeStruct((rows, 2 * STATE), F32),
            jax.ShapeDtypeStruct((rows, HEADS), F32),
        ],
        scratch_shapes=[
            pltpu.VMEM((CUT, DI), F32),
            pltpu.VMEM((CUT, DI), F32),
            pltpu.VMEM((HEADS, CUT), F32),
            pltpu.VMEM((HEADS, CUT), F32),
            pltpu.VMEM((CUT, CUT), F32),
            pltpu.VMEM((CUT, CUT), F32),
            pltpu.VMEM((CUT, CUT), F32),
        ],
        compiler_params=params(),
        cost_estimate=FREE,
        name="back_intra",
    )(act, step, logd, dy, spreader)


def back_kernel(
    act_ref,
    step_ref,
    slope_ref,
    logd_ref,
    dy_ref,
    dweighted_ref,
    dstates_ref,
    moved_ref,
    local_ref,
    enter_ref,
    before_ref,
    gin_ref,
    gout_ref,
    proj_ref,
    halo_ref,
    taps_ref,
    bias_ref,
    alog_ref,
    skip_ref,
    spreader_ref,
    gatherer_ref,
    dproj_ref,
    dtaps_ref,
    dbias_ref,
    dlog_ref,
    ddtb_ref,
    dact,
    window,
    dwindow,
    after,
):
    i = pl.program_id(0)
    cuts = pl.num_programs(0)
    q = cuts - 1 - i

    @pl.when(i == 0)
    def _():
        after[...] = jnp.zeros_like(after)
        dwindow[...] = jnp.zeros_like(dwindow)
        for ref in (dtaps_ref, dbias_ref, dlog_ref, ddtb_ref):
            ref[...] = jnp.zeros_like(ref)

    @pl.when(i > 0)
    def _():
        dwindow[CUT : CUT + EDGE, :] = dwindow[0:EDGE, :]

    logd = logd_ref[...]
    step = step_ref[...]
    last = logd[CUT - 1 : CUT, :]
    b_state = act_ref[:, DI : DI + STATE]
    c_state = act_ref[:, DI + STATE : MIXED]
    grow_parts = split_heads(jnp.exp(logd))
    tail_parts = split_heads(jnp.exp(last - logd))
    step_parts = split_heads(step)
    before_parts = split_heads(before_ref[...])
    later_parts = split_heads(jnp.exp(after[...]))
    after[...] = after[...] + jnp.broadcast_to(last, (8, HEADS))
    db = dstates_ref[:, 0:STATE]
    dc = dstates_ref[:, STATE : 2 * STATE]
    moved = moved_ref[...]
    lost = jnp.zeros((CUT, HEADS), F32)
    dstep = jnp.zeros((CUT, HEADS), F32)
    kept = jnp.zeros((8, HEADS), F32)
    for c in range(DI // BLOCK):
        cols = slice(c * BLOCK, (c + 1) * BLOCK)
        spreader = spreader_ref[:, cols]
        gatherer = gatherer_ref[cols, :]
        entering = enter_ref[:, cols] * bf16_dot(before_parts, spreader)[0:1, :]
        entering = entering + jnp.where(q == 0, 0.0, local_ref[0, :, cols])
        gout = gout_ref[:, cols] * bf16_dot(later_parts, spreader)[0:1, :]
        gout = gout + jnp.where(i == 0, 0.0, gin_ref[0, :, cols])
        tail = bf16_dot(tail_parts, spreader)
        steps = bf16_dot(step_parts, spreader)
        heads_in = act_ref[:, cols]
        dy = dy_ref[:, cols]
        from_state = tail * nn(b_state, gout)
        stepped = heads_in * steps
        dweighted = dweighted_ref[:, cols] + from_state
        carried = bf16_dot(grow_parts, spreader) * dy
        db = db + nt(tail * stepped, gout)
        dc = dc + nt(carried, entering)
        dact[:, cols] = dweighted * steps + skip_ref[:, cols] * dy
        moved = moved + sum_heads(carried * nn(c_state, entering), gatherer)
        lost = lost + sum_heads(stepped * from_state, gatherer)
        dstep = dstep + sum_heads(heads_in * dweighted, gatherer)
        kept = kept + sum_heads(
            jnp.broadcast_to(jnp.sum(gout * entering, axis=0, keepdims=True), (8, BLOCK)), gatherer
        )
    dact[:, DI : DI + STATE] = db
    dact[:, DI + STATE : MIXED] = dc
    dlog = (
        nn(triangle("le"), moved, EXACT)
        + nn(triangle("gt"), lost, EXACT)
        + jnp.exp(last) * kept[0:1, :]
    )
    rate = -jnp.exp(alog_ref[...])
    dlog_ref[...] += jnp.broadcast_to(
        jnp.sum(dlog * step, axis=0, keepdims=True) * rate, (8, HEADS)
    )
    draw = (dstep + dlog * rate) * slope_ref[...]
    ddtb_ref[...] += jnp.broadcast_to(jnp.sum(draw, axis=0, keepdims=True), (8, HEADS))
    here = pl.ds(pl.multiple_of(q * CUT, CUT), CUT)
    dproj_ref[here, MIXED:WIDE] = jnp.concatenate([draw, jnp.zeros((CUT, SPARE), F32)], axis=1)
    window[0:EDGE, :] = halo_ref[:, 0:MIXED]
    window[EDGE : EDGE + CUT, :] = proj_ref[:, 0:MIXED]

    def conv(c, carry):
        cols = pl.ds(pl.multiple_of(c * STRIP, STRIP), STRIP)
        out = conv_chunk(window, taps_ref, bias_ref, cols)
        sg = jax.nn.sigmoid(out)
        dout = dact[:, cols] * (sg * (1.0 + out * (1.0 - sg)))
        dwindow[0:CUT, cols] = dout
        dbias_ref[:, cols] += jnp.sum(dout.reshape(CUT // 8, 8, STRIP), axis=0)
        for k in range(CONV):
            at = EDGE - 3 + k
            dtaps_ref[8 * k : 8 * k + 8, cols] += jnp.sum(
                (dout * window[at : at + CUT, cols]).reshape(CUT // 8, 8, STRIP), axis=0
            )
        din = taps_ref[CONV - 1 : CONV, cols] * dout
        for k in range(CONV - 1):
            din = din + taps_ref[k : k + 1, cols] * dwindow[3 - k : 3 - k + CUT, cols]
        dproj_ref[here, cols] = din
        return carry

    lax.fori_loop(0, MIXED // STRIP, conv, 0, unroll=3)

    @pl.when(q == 0)
    def _():
        rows = cuts * CUT
        window[0:EDGE, :] = jnp.zeros((EDGE, MIXED), F32)
        window[EDGE : 2 * EDGE, :] = dwindow[0:EDGE, :]
        din = taps_ref[CONV - 1 : CONV, :] * window[0:EDGE, :]
        for k in range(CONV - 1):
            din = din + taps_ref[k : k + 1, :] * window[3 - k : 3 - k + EDGE, :]
        dproj_ref[rows : rows + EDGE, 0:MIXED] = din
        dproj_ref[rows : rows + EDGE, MIXED:WIDE] = jnp.zeros((EDGE, WIDE - MIXED), F32)


def back(
    act, step, slope, logd, dy, dweighted, dstates, moved, local, entering, before, gin, gout, proj, taps, bias, a_log,
    skip, spreader, gatherer,
):
    rows = act.shape[0]
    cuts = rows // CUT

    def at(size):
        return pl.BlockSpec((CUT, size), lambda i: (cuts - 1 - i, 0))

    def halo(i):
        q = cuts - 1 - i
        return (jnp.where(q == 0, rows // EDGE, q * (CUT // EDGE) - 1), 0)

    return pl.pallas_call(
        back_kernel,
        grid=(cuts,),
        in_specs=[
            at(MIXED),
            at(HEADS),
            at(HEADS),
            at(HEADS),
            at(DI),
            at(DI),
            at(2 * STATE),
            at(HEADS),
            pl.BlockSpec((1, STATE, DI), lambda i: (jnp.maximum(cuts - 2 - i, 0), 0, 0)),
            full((STATE, DI)),
            pl.BlockSpec((8, HEADS), lambda i: (cuts - 1 - i, 0)),
            pl.BlockSpec((1, STATE, DI), lambda i: (jnp.minimum(cuts - i, cuts - 1), 0, 0)),
            full((STATE, DI)),
            at(WIDE),
            pl.BlockSpec((EDGE, WIDE), halo),
            full((CONV, MIXED)),
            full((1, MIXED)),
            full((1, HEADS)),
            full((1, DI)),
            full((3 * HEADS, DI)),
            full((DI, HEADS)),
        ],
        out_specs=[
            full((rows + EDGE, WIDE)),
            full((8 * CONV, MIXED)),
            full((8, MIXED)),
            full((8, HEADS)),
            full((8, HEADS)),
        ],
        out_shape=[
            jax.ShapeDtypeStruct((rows + EDGE, WIDE), F32),
            jax.ShapeDtypeStruct((8 * CONV, MIXED), F32),
            jax.ShapeDtypeStruct((8, MIXED), F32),
            jax.ShapeDtypeStruct((8, HEADS), F32),
            jax.ShapeDtypeStruct((8, HEADS), F32),
        ],
        scratch_shapes=[
            pltpu.VMEM((CUT, MIXED), F32),
            pltpu.VMEM((CUT + EDGE, MIXED), F32),
            pltpu.VMEM((CUT + EDGE, MIXED), F32),
            pltpu.VMEM((8, HEADS), F32),
        ],
        compiler_params=params(),
        cost_estimate=FREE,
        name="back",
    )(
        act, step, slope, logd, dy, dweighted, dstates, moved, local, entering, before, gin, gout, proj, proj,
        taps, bias, a_log, skip, spreader, gatherer,
    )


def head_spreader():
    head = lax.broadcasted_iota(jnp.int32, (3 * HEADS, DI), 0) % HEADS
    return (head == lax.broadcasted_iota(jnp.int32, (3 * HEADS, DI), 1) // HDIM).astype(BF16)


def head_gatherer():
    channel = lax.broadcasted_iota(jnp.int32, (DI, HEADS), 0) // HDIM
    return (channel == lax.broadcasted_iota(jnp.int32, (DI, HEADS), 1)).astype(BF16)


def per_device(
    hidden_in,
    lengths,
    norm_gain,
    in_weight,
    conv_weight,
    conv_bias,
    dt_bias,
    a_log,
    skip_gain,
    gated_gain,
    out_weight,
    cotangent,
):
    width = hidden_in.shape[-1]
    devices = 1
    for axis in AXES:
        devices *= lax.axis_size(axis)
    mine, spot, count = (lax.axis_index("p"), lax.axis_index("zc"), lax.axis_size("zc"))
    own_rows = width // devices

    in_piece = in_weight.reshape(own_rows, -1)
    small = jnp.concatenate([conv_weight, conv_bias])
    padded = jnp.pad(small, (0, SPARE * own_rows - small.shape[0])).reshape(own_rows, SPARE)
    conv = Gather(jnp.concatenate([in_piece[:, DI:], padded], axis=1))
    gate = Gather(in_piece[:, :DI])
    out = Gather(out_weight.reshape(-1, width))
    conv.line()
    hidden = to_span(hidden_in, mine)
    rows = hidden.shape[0]
    near = conv.near()
    conv_over = conv.across(conv.held_near()[:1], conv.block)
    far = conv.far(hidden)
    conv_over += conv.across(conv.held_near()[1:])
    gate.line_at_once(conv.block)
    other = to_span(tied([cotangent], *near)[0], mine)
    conv_over += conv.across(conv.corners)
    w_conv = place(conv.held() + conv_over, conv.rows)
    gate_near = gate.near(*far)
    out.line_at_once(gate.block, *far)
    edge = lax.ppermute(
        tied([hidden[rows - EDGE :]], *near)[0], "zc", [(i, i + 1) for i in range(count - 1)]
    )
    smalls = w_conv[:, RATED:].reshape(devices, own_rows * SPARE)
    taps = smalls[:, : conv_weight.shape[0]].reshape(CONV, MIXED)
    bias = smalls[:, conv_weight.shape[0] : small.shape[0]].reshape(1, MIXED)

    extended = jnp.concatenate([hidden, edge], axis=0)
    scale = lax.rsqrt(jnp.mean(extended * extended, axis=1, keepdims=True) + epsilon)
    unit = extended * scale
    normed = unit * norm_gain
    inner = normed[:rows]
    spreader, gatherer = (head_spreader(), head_gatherer())
    dt_row, alog_row = (dt_bias.reshape(1, -1), a_log.reshape(1, -1))
    skip_row = jnp.repeat(skip_gain, HDIM).reshape(1, DI)
    positions = spot * rows + lax.iota(jnp.int32, rows)
    length = lax.dynamic_index_in_dim(lengths, mine, 0, keepdims=False)
    valid = (positions < length).astype(F32)[:, None]
    proj = nn(normed, w_conv)
    act, step, slope, logd, local, before, total = prepare(
        proj, taps, bias, dt_row, alog_row, spreader
    )
    total_row = jnp.repeat(total[0], HDIM).reshape(1, DI)
    states = States(total_row, local[-1], False)
    came = states.send(*gate_near)
    gate_far = gate.far(act)
    gate_over = gate.across(gate.held_near(), act)
    within = intra(act, step, logd, skip_row, spreader)
    out_near = out.near(within, *gate_far)
    while states.distance < count:
        came = states.send()
    gate_over += gate.across(gate.corners, within)
    w_gate = place(gate.held() + gate_over, gate.rows)
    gate_in = nn(tied([inner], within)[0], w_gate)
    out_far = out.far(gate_in)
    out_over = out.across(out.held_near(), gate_in) + out.across(out.corners)
    w_out = place(out.held() + out_over, out.rows)
    grad_out = other * valid
    dng = nt(grad_out, w_out)
    entering = states.result()
    ng, dy, dz, gin, ggrad, skipg = mixer(
        act, logd, within, gate_in, dng, local, entering, before, gated_gain.reshape(1, DI), spreader
    )
    ng_keep, ng_send = core_columns(ng)
    in_keep, in_send = core_columns(normed)
    grads = States(total_row, gin[0], True)
    came = grads.send()
    first = tn(ng_send, grad_out)
    (turn,) = tied([grad_out], first)
    second = tn(ng_keep, turn)
    grad_wout = Scatter(first, second)
    branch = nn(tied([ng], second)[0], w_out)
    (send_from,) = tied([dz], branch, *grad_wout.came)
    grad_wout.stage(("p", "y"))
    first = tn(in_send[:rows], send_from)
    (turn,) = tied([send_from], first)
    second = tn(in_keep[:rows], turn)
    grad_wgate = Scatter(first, second)
    back_parts = back_intra(tied([act], second, *came)[0], step, logd, dy, spreader)
    while grads.distance < count:
        came = grads.send()
    (turn,) = tied([dz], back_parts[1], *grad_wgate.came, *grad_wout.came)
    grad_wout.stage(("y", "p"))
    dgate_normed = nt(turn, w_gate)
    grad_wgate.stage(("p", "y"))
    gout = grads.result()
    dproj, dtaps, dbias, dlog, ddtb = back(
        tied([act], dgate_normed, *grad_wout.came)[0], step, slope, logd, dy, *back_parts, local,
        entering, before, gin, gout, proj, taps, bias, alog_row, skip_row, spreader, gatherer,
    )
    grad_wout.last_at_once()
    dtaps = jnp.sum(dtaps.reshape(CONV, 8, MIXED), axis=1).reshape(devices, -1)
    dbias = jnp.sum(dbias, axis=0).reshape(devices, -1)
    dsmall = jnp.concatenate([dtaps, dbias], axis=1)
    dsmall = jnp.pad(dsmall, ((0, 0), (0, SPARE * own_rows - small.shape[0])))
    dsmall = jnp.pad(dsmall.reshape(width, SPARE), ((0, 0), (RATED, 0)))
    small_keep, small_send = (core_rows(dsmall, k) for k in (0, 1))
    first = tn(in_send, dproj) + small_send
    (turn,) = tied([dproj], first, *grad_wgate.came)
    second = tn(in_keep, turn) + small_keep
    grad_wconv = Scatter(first, second)
    grad_wgate.stage(("y", "p"))
    (turn,) = tied([dproj], second)
    dnormed = nt(turn, w_conv)
    (dnormed,) = tied([dnormed], *grad_wconv.came, *grad_wgate.came)
    grad_wgate.last_at_once()
    grad_wconv.stage(("p", "y"))
    returned = lax.ppermute(dnormed[rows:], "zc", [(i + 1, i) for i in range(count - 1)])
    near = grad_wconv.came
    output = from_span((hidden + branch) * valid, mine)
    grad_wconv.stage(("y", "p"))
    grad_wconv.last()
    dnormed = dnormed[:rows] + dgate_normed
    dnormed = dnormed + jnp.pad(returned, ((rows - EDGE, 0), (0, 0)))
    unit = unit[:rows]
    dunit = dnormed * norm_gain
    dhidden = scale[:rows] * (dunit - unit * jnp.mean(dunit * unit, axis=1, keepdims=True))
    grad_input = from_span(tied([grad_out + dhidden], *near)[0], mine)
    grad_skip = jnp.sum(jnp.sum(skipg, axis=0).reshape(HEADS, HDIM), axis=1)
    sums = jnp.concatenate(
        [
            jnp.sum(dnormed * unit, axis=0),
            jnp.sum(ggrad, axis=0),
            ddtb[0],
            dlog[0],
            grad_skip,
        ]
    )
    (sums,) = tied([jnp.pad(sums, (0, -sums.shape[0] % 128)).reshape(-1, 128)], *near)
    sums = sum_everywhere(sums).reshape(-1)
    parts = []
    for size in (width, DI, HEADS, HEADS, HEADS):
        parts.append(sums[:size])
        sums = sums[size:]
    conv_grad = grad_wconv.result()
    small_grad = conv_grad[:, RATED:].reshape(-1)
    return (
        output,
        grad_input,
        parts[0],
        jnp.concatenate([grad_wgate.result(), conv_grad[:, :RATED]], axis=1).reshape(-1),
        small_grad[: conv_weight.shape[0]],
        small_grad[conv_weight.shape[0] : small.shape[0]],
        parts[2],
        parts[3],
        parts[4],
        parts[1],
        grad_wout.result().reshape(-1),
    )


def core_columns(values):
    size = values.shape[1] // (2 * lax.axis_size("y"))
    core = lax.axis_index("core")
    return [
        jnp.concatenate(
            [
                lax.dynamic_slice_in_dim(values, (2 * y + (core + k) % 2) * size, size, 1)
                for y in range(lax.axis_size("y"))
            ],
            axis=1,
        )
        for k in (0, 1)
    ]


def core_rows(values, k):
    size = values.shape[0] // (2 * lax.axis_size("y"))
    core = lax.axis_index("core")
    return jnp.concatenate(
        [
            lax.dynamic_slice_in_dim(values, (2 * y + (core + k) % 2) * size, size, 0)
            for y in range(lax.axis_size("y"))
        ],
        axis=0,
    )


def solution(mesh):
    dp, seq = (mesh.shape["dp"], mesh.shape["seq"])
    finer = Mesh(mesh.devices.reshape(dp // 2, 2, seq // 2, 2), AXES)
    over_dp, over_seq = (("y", "core"), ("zc", "p"))
    tokens = P(over_dp, over_seq, None)
    in_specs = (
        tokens, P(over_dp), P(), P(AXES), P(AXES), P(AXES), P(), P(), P(), P(), P(AXES), tokens,
    )
    out_specs = (
        tokens, tokens, P(), P(AXES), P(AXES), P(AXES), P(), P(), P(), P(), P(AXES),
    )
    return jax.shard_map(
        per_device, mesh=finer, in_specs=in_specs, out_specs=out_specs, check_vma=False
    )
```

time: 773 us -> 629 us (0.81)
  waiting for transfers between devices: 263 us -> 181 us
  local copies, waits for them, and re-layouts: 131 us -> 68.3 us
  other arithmetic: 34.7 us -> 72.6 us
  starting transfers between devices: 120 us -> 103 us
  Pallas kernels: 112 us -> 99.9 us
    ppermute x82 -> x58, waiting for transfers between devices: 230 us -> 148 us  [shift(): lax.ppermute(block, axis, [(i, (i + step) % count) for i in range(count)])]
    pallas_call x0 -> x5, Pallas kernels: none -> 38.6 us  [the longest x1 18.2 us: back_intra(): pl.pallas_call(back_intra_kernel, grid=(rows // CUT,), in_specs=[at(MIXED...]
    all_to_all x0 -> x4, starting transfers between devices: none -> 33 us  [the longest x2 23.3 us: last_at_once(): line = lax.all_to_all(line, 'zc', 0, 0)]
    dynamic_update_slice x63 -> x0, local copies, waits for them, and re-layouts: 32.2 us -> none  [the longest x39 18.8 us: gather_axis(): lax.dynamic_update_slice_in_dim(whole, moving[None], (index - k) % count, 0)]
    ppermute x82 -> x58, starting transfers between devices: 84.5 us -> 53.5 us  [shift(): lax.ppermute(block, axis, [(i, (i + step) % count) for i in range(count)])]
    pallas_call x1, Pallas kernels: 45.1 us -> 16.5 us  [mixer(): pl.pallas_call(mixer_kernel, grid=(cuts,), in_specs=[back(MIXED), back(HE...]
    pallas_call x1, Pallas kernels: 54.8 us -> 33.2 us  [back(): pl.pallas_call(back_kernel, grid=(cuts,), in_specs=[at(MIXED), at(HEADS),...]
    add x48 -> x27, other arithmetic: 15.1 us -> 36.4 us  [the longest x12 15.8 us: indexed(): total = part if total is None else total + part]
  transfers between devices with their start and end apart: 96 -> 68, of which waited for: 59 -> 27; matrix products, arithmetic and copies ran while one was open for 31% -> 34% of each run, Pallas kernels for 9% -> 13%
where the time goes in v2:
time: 629 us; the launch traced here: 624 us
  waiting for transfers between devices  181 us (29%)
  starting transfers between devices  103 us (16%)
  Pallas kernels  99.9 us (16%)
  matrix products  96.8 us (15%)
  other arithmetic  72.6 us (12%)
  local copies, waits for them, and re-layouts  68.3 us (11%)
    ppermute x58, waiting for transfers between devices, shift(): lax.ppermute(block, axis, [(i, (i + step) % count) for i in range(count)])  148 us
    ppermute x58, starting transfers between devices, shift(): lax.ppermute(block, axis, [(i, (i + step) % count) for i in range(count)])  53.5 us
    dot_general x6, matrix products, tn(): lax.dot_general(a, b, (((0,), (0,)), ((), ())), precision=precision, pref...  39.4 us
    pallas_call x1, Pallas kernels, back(): pl.pallas_call(back_kernel, grid=(cuts,), in_specs=[at(MIXED), at(HEADS),...  33.2 us
    dot_general x3, matrix products, nt(): lax.dot_general(a, b, (((1,), (1,)), ((), ())), precision=precision, pref...  30.7 us
    ppermute x4, waiting for transfers between devices, send(): came.append(lax.ppermute(block, 'zc', route))  29.4 us
    dot_general x3, matrix products, nn(): return jnp.dot(a, b, precision=precision, preferred_element_type=F32)  26.6 us
    all_to_all x2, starting transfers between devices, last_at_once(): line = lax.all_to_all(line, 'zc', 0, 0)  23.3 us
  transfers between devices with their start and end apart: 68, of which 27 were waited for; matrix products, arithmetic and copies ran while one was open for 34% of the time, Pallas kernels for 13%

profile of v2, /device:TPU:8, one launch (start us, length us, event | category | flops | bytes accessed | tf_op | source)
XLA Modules:
  0.0 623.7 jit_solution(13278587703387005221)
XLA Ops:
  11.3 15.5 %collective-permute-done.3 = f32[32,2432]{1,0:T(8,128)S(1)} collective-permute-done((f32[32,2432]{1,0:T(8,128)S(1)}, f32[32,2432]{1,0:T(8,128)S(1)}, u32[]{:S(2)}, u32[]{:S(2)}) %collective-permute-start.3) | collective-permute-done | bytes 311328 | tf_op jit(solution)/shard_map/ppermute | solution.py:35
  26.9 5.8 collective-permute-done.1
  38.0 5.3 all-to-all-start
  46.1 16.4 %collective-permute-done.5.refs_2_ = f32[128,2432]{1,0:T(8,128)} collective-permute-done((f32[128,2432]{1,0:T(8,128)S(1)}, f32[128,2432]{1,0:T(8,128)}, u32[]{:S(2)}, u32[]{:S(2)}) %collective-permute-start.5) | collective-permute-done | bytes 1245216 | tf_op jit(solution)/shard_map/ppermute | solution.py:35
  68.6 9.3 %collective-permute-done.8.refs_4_ = f32[64,2432]{1,0:T(8,128)S(1)} collective-permute-done((f32[64,2432]{1,0:T(8,128)S(1)}, f32[64,2432]{1,0:T(8,128)S(1)}, u32[]{:S(2)}, u32[]{:S(2)}) %collective-permute-start.8) | collective-permute-done | bytes 622624 | tf_op jit(solution)/shard_map/ppermute | solution.py:35
  103.8 10.7 %fusion.92.proj_ref.edge_ref.halo_ref = f32[520,2432]{1,0:T(8,128)} fusion(f32[520,1024]{1,0:T(8,128)S(1)} %copy-done.20, f32[1024,2432]{1,0:T(8,128)S(1)} %place.3), kind=kOutput, calls=%fused_computation.211 | convolution fusion | flops 7769948160 | bytes 17149952 | tf_op jit(solution)/shard_map/dot_general | solution.py:292
  115.3 11.6 %prepare.1 = (f32[512,2304]{1,0:T(8,128)}, f32[512,32]{1,0:T(8,128)S(1)}, f32[512,32]{1,0:T(8,128)S(1)}, f32[512,32]{1,0:T(8,128)S(1)}, f32[4,128,2048]{2,1,0:T(...) custom-call(f32[520,2432]{1,0:T(8,128)} %fusion.92.proj_ref.edge_ref.halo_ref, ...), custom_call_target="tpu_custom_call" | custom-call | tf_op jit(solution)/shard_map/prepare/pallas_call | solution.py:418
  131.9 10.6 %intra.1.inner_ref = f32[512,2048]{1,0:T(8,128)} custom-call(f32[512,2304]{1,0:T(8,128)} %get-tuple-element.119.act_ref, f32[512,32]{1,0:T(8,128)S(1)} %get-tuple-element.83.step_ref, f32[512,32]{1,0:T(8,128)S(1)} %get-tuple-element.82.logd_ref, f32[1,2048]{1,0:T(1,128)S(1)} %reshape_reshape.4.skip_ref, bf16[96,2048]{1,0:T(8,128)(2,1)S(1)} %fusion.34.spreader_ref), custom_call_target="tpu_custom_call" | custom-call | tf_op jit(solution)/shard_map/intra/pallas_call | solution.py:505
  167.3 8.4 %fusion.93.gate_ref = f32[512,2048]{1,0:T(8,128)} fusion(f32[512,1024]{1,0:T(8,128)S(1)} %slice.284, f32[1024,2048]{1,0:T(8,128)S(1)} %place.4), kind=kOutput, calls=%fused_computation.212 | convolution fusion | flops 6442450944 | bytes 14680064 | tf_op jit(solution)/shard_map/dot_general | solution.py:292
  175.8 6.9 %collective-permute-done.24.refs_1_ = f32[256,1024]{1,0:T(8,128)} collective-permute-done((f32[256,1024]{1,0:T(8,128)}, f32[256,1024]{1,0:T(8,128)}, u32[]{:S(2)}, u32[]{:S(2)}) %collective-permute-start.24) | collective-permute-done | bytes 1048608 | tf_op jit(solution)/shard_map/ppermute | solution.py:35
  193.5 11.5 %collective-permute-done.23 = f32[256,1024]{1,0:T(8,128)} collective-permute-done((f32[256,1024]{1,0:T(8,128)}, f32[256,1024]{1,0:T(8,128)}, u32[]{:S(2)}, u32[]{:S(2)}) %collective-permute-start.23) | collective-permute-done | bytes 1048608 | tf_op jit(solution)/shard_map/ppermute | solution.py:35
  208.6 6.3 %collective-permute-done.27.refs_4_ = f32[128,1024]{1,0:T(8,128)S(1)} collective-permute-done((f32[128,1024]{1,0:T(8,128)S(1)}, f32[128,1024]{1,0:T(8,128)S(1)}, u32[]{:S(2)}, u32[]{:S(2)}) %collective-permute-start.27) | collective-permute-done | bytes 524320 | tf_op jit(solution)/shard_map/ppermute | solution.py:35
  214.9 17.8 %collective-permute-done.34 = f32[128,2048]{1,0:T(8,128)} collective-permute-done((f32[128,2048]{1,0:T(8,128)}, f32[128,2048]{1,0:T(8,128)}, u32[]{:S(2)}, u32[]{:S(2)}) %collective-permute-start.34) | collective-permute-done | bytes 1048608 | tf_op jit(solution)/shard_map/ppermute | solution.py:272
  237.3 8.3 %fusion.94.dng_ref = f32[512,2048]{1,0:T(8,128)} fusion(f32[512,1024]{1,0:T(8,128)S(1)} %maximum_multiply_fusion, f32[2048,1024]{1,0:T(8,128)S(1)} %place.5), kind=kOutput, calls=%fused_computation.213 | convolution fusion | flops 6442450944 | bytes 14680064 | tf_op jit(solution)/shard_map/dot_general | solution.py:296
  245.6 16.5 %mixer.1 = (f32[512,2048]{1,0:T(8,128)}, f32[512,2048]{1,0:T(8,128)}, f32[512,2048]{1,0:T(8,128)}, f32[4,128,2048]{2,1,0:T(8,128)}, f32[8,2048]{1,0:T(8,128)S(1)}, /*index=5*/f32[8,2048]{1,0:T(8,128)S(1)}) custom-call(f32[512,2304]{1,0:T(8,128)} %get-tuple-element.119.act_ref, f32[512,32]{1,0:T(8,128)S(1)} %get-tuple-element.82.logd_ref, ...), custom_call_target="tpu_custom_call" | custom-call | tf_op jit(solution)/shard_map/mixer/pallas_call | solution.py:597
  282.3 5.5 fusion
  287.9 7.5 %add_multiply_fusion = f32[512,1024]{1,0:T(8,128)S(1)} fusion(f32[512]{0:T(512)S(1)} %copy-done.73, f32[256,1024]{1,0:T(8,128)S(1)} %copy-done.22, f32[256,1024]{1,0:T(8,128)S(1)} %copy-done.24, f32[512,2048]{1,0:T(8,128)S(1)} %copy-done.23, f32[2048,1024]{1,0:T(8,128)S(1)} %bitcast.386), kind=kOutput, calls=%fused_computation.24 | convolution fusion | flops 6444023808 | bytes 16779264 | tf_op jit(solution)/shard_map/dot_general | solution.py:292
  298.3 5.6 fusion.17
  315.2 6.7 %collective-permute-done.35 = f32[256,1024]{1,0:T(8,128)} collective-permute-done((f32[256,1024]{1,0:T(8,128)}, f32[256,1024]{1,0:T(8,128)}, u32[]{:S(2)}, u32[]{:S(2)}) %collective-permute-start.35) | collective-permute-done | bytes 1048608 | tf_op jit(solution)/shard_map/ppermute | solution.py:35
  331.9 6.9 %collective-permute-done.43 = f32[128,2048]{1,0:T(8,128)} collective-permute-done((f32[128,2048]{1,0:T(8,128)}, f32[128,2048]{1,0:T(8,128)}, u32[]{:S(2)}, u32[]{:S(2)}) %collective-permute-start.43) | collective-permute-done | bytes 1048608 | tf_op jit(solution)/shard_map/ppermute | solution.py:272
  345.1 8.3 %collective-permute-done.39 = f32[2,2,64,1024]{3,2,1,0:T(8,128)S(1)} collective-permute-done((f32[2,2,64,1024]{3,2,1,0:T(8,128)S(1)}, f32[2,2,64,1024]{3,2,1,0:T(8,128)S(1)}, u32[]{:S(2)}, u32[]{:S(2)}) %collective-permute-start.39) | collective-permute-done | bytes 1048608 | tf_op jit(solution)/shard_map/ppermute | solution.py:35
  360.5 18.2 %back_intra.1 = (f32[512,2048]{1,0:T(8,128)}, f32[512,256]{1,0:T(8,128)S(1)}, f32[512,32]{1,0:T(8,128)S(1)}) custom-call(f32[512,2304]{1,0:T(8,128)} %get-tuple-element.119.act_ref, f32[512,32]{1,0:T(8,128)S(1)} %get-tuple-element.83.step_ref, f32[512,32]{1,0:T(8,128)S(1)} %get-tuple-element.82.logd_ref, f32[512,2048]{1,0:T(8,128)} %get-tuple-element.116.dy_ref, ...), custom_call_target="tpu_custom_call" | custom-call | tf_op jit(solution)/shard_map/back_intra/pallas_call | solution.py:705
  382.7 18.0 %all-to-all-start.3 = ((f32[4,64,1024]{2,1,0:T(8,128)}), f32[4,64,1024]{2,1,0:T(8,128)}, u32[]{:S(2)}, u32[]{:S(2)}) async-start(f32[4,64,1024]{2,1,0:T(8,128)} %pad_maximum_fusion.8), calls=%async_computation.3 | async-start | bytes 2097152 | tf_op jit(solution)/shard_map/all_to_all | solution.py:209
  400.7 11.4 %fusion.95 = f32[512,1024]{1,0:T(8,128)} fusion(f32[512,2048]{1,0:T(8,128)} %get-tuple-element.118, f32[1024,2048]{1,0:T(8,128)} %copy-done.1), kind=kOutput, calls=%fused_computation.214 | convolution fusion | flops 6442450944 | bytes 14680064 | tf_op jit(solution)/shard_map/dot_general | solution.py:296
  412.2 33.2 %back.1 = (f32[520,2432]{1,0:T(8,128)}, f32[32,2304]{1,0:T(8,128)S(1)}, f32[8,2304]{1,0:T(8,128)S(1)}, f32[8,32]{1,0:T(8,128)S(1)}, f32[8,32]{1,0:T(8,128)S(1)}) custom-call(f32[512,2304]{1,0:T(8,128)} %get-tuple-element.119.act_ref, f32[512,32]{1,0:T(8,128)S(1)} %get-tuple-element.83.step_ref, f32[512,32]{1,0:T(8,128)S(1)} %copy-done.8, ...), custom_call_target="tpu_custom_call" | custom-call | tf_op jit(solution)/shard_map/back/pallas_call | solution.py:883
  450.2 10.6 %maximum_add_fusion = f32[512,2432]{1,0:T(8,128)} fusion(f32[256,2432]{1,0:T(8,128)S(1)} %get-tuple-element.172, f32[256,2432]{1,0:T(8,128)S(1)} %get-tuple-element.171, f32[520,2432]{1,0:T(8,128)} %get-tuple-element.127, f32[520,256]{1,0:T(8,128)S(1)} %copy-done.48, f32[520,256]{1,0:T(8,128)S(1)} %copy-done.50), kind=kOutput, calls=%fused_computation.4 | convolution fusion | flops 3887730688 | bytes 16084992 | tf_op jit(solution)/shard_map/dot_general | solution.py:302
  472.7 18.0 %collective-permute-done.44 = f32[2,2,32,2048]{3,2,1,0:T(8,128)} collective-permute-done((f32[2,2,32,2048]{3,2,1,0:T(8,128)}, f32[2,2,32,2048]{3,2,1,0:T(8,128)}, u32[]{:S(2)}, u32[]{:S(2)}) %collective-permute-start.44) | collective-permute-done | bytes 1048608 | tf_op jit(solution)/shard_map/ppermute | solution.py:35
  495.5 8.9 %maximum_add_fusion.1 = f32[512,2432]{1,0:T(8,128)S(1)} fusion(f32[256,2432]{1,0:T(8,128)S(1)} %copy-done.34, f32[256,2432]{1,0:T(8,128)S(1)} %get-tuple-element.173, f32[520,2432]{1,0:T(8,128)} %get-tuple-element.127, f32[520,256]{1,0:T(8,128)S(1)} %copy-done.46, f32[520,256]{1,0:T(8,128)S(1)} %get-tuple-element.164), kind=kOutput, calls=%fused_computation.5 | convolution fusion | flops 3887730688 | bytes 16084992 | tf_op jit(solution)/shard_map/dot_general | solution.py:302
  511.1 5.3 all-to-all-start.2
  528.4 11.0 %fusion.96 = f32[520,1024]{1,0:T(8,128)S(1)} fusion(f32[520,2432]{1,0:T(8,128)} %get-tuple-element.127, f32[1024,2432]{1,0:T(8,128)S(1)} %bitcast.388), kind=kOutput, calls=%fused_computation.215 | convolution fusion | flops 7769948160 | bytes 17149952 | tf_op jit(solution)/shard_map/dot_general | solution.py:296
  565.3 12.8 %collective-permute-done.55 = f32[25,128]{1,0:T(8,128)S(1)} collective-permute-done((f32[25,128]{1,0:T(8,128)S(1)}, f32[25,128]{1,0:T(8,128)S(1)}, u32[]{:S(2)}, u32[]{:S(2)}) %collective-permute-start.55) | collective-permute-done | bytes 12832 | tf_op jit(solution)/shard_map/ppermute | solution.py:35
  594.2 17.3 %collective-permute-done.61 = f32[32,2432]{1,0:T(8,128)S(1)} collective-permute-done((f32[32,2432]{1,0:T(8,128)S(1)}, f32[32,2432]{1,0:T(8,128)S(1)}, u32[]{:S(2)}, u32[]{:S(2)}) %collective-permute-start.61) | collective-permute-done | bytes 311328 | tf_op jit(solution)/shard_map/ppermute | solution.py:35
  (423 shorter events, 255.2 us)
Async XLA Ops:
  6.3 26.4 %collective-permute-start.1 = (f32[32,2432]{1,0:T(8,128)S(1)}, f32[32,2432]{1,0:T(8,128)}, u32[]{:S(2)}, u32[]{:S(2)}) collective-permute-start(f32[32,2432]{1,0:T(8,128)S(1)} %pad_maximum_fusion.10), channel_id=1, source_target_pairs={{0,2},{2,4},{4,6},{6,0},{1,3},{3,5},{5,7},{7,1},{8,10},{10,12},{12... | collective-permute-start | bytes 933896 | tf_op jit(solution)/shard_map/ppermute | solution.py:35
  9.8 33.5 %collective-permute-start = (f32[256,1024]{1,0:T(8,128)}, f32[256,1024]{1,0:T(8,128)}, u32[]{:S(2)}, u32[]{:S(2)}) collective-permute-start(f32[256,1024]{1,0:T(8,128)} %dynamic-slice_bitcast_fusion.3), channel_id=1, source_target_pairs={{0,1},{1,0},{2,3},{3,2},{4,5},{5,4},{6,7},{7,6},{8,9},{9,8},{10,11... | collective-permute-start | bytes 3145736 | tf_op jit(solution)/shard_map/ppermute | solution.py:35
  33.8 28.7 %collective-permute-start.5 = (f32[128,2432]{1,0:T(8,128)S(1)}, f32[128,2432]{1,0:T(8,128)}, u32[]{:S(2)}, u32[]{:S(2)}) collective-permute-start(f32[128,2432]{1,0:T(8,128)S(1)} %pad_maximum_fusion.6.refs_0_), channel_id=1, source_target_pairs={{0,16},{16,0},{1,17},{17,1},{2,18},{18,2},{3,19},{19,3},{4,20},{20... | collective-permute-start | bytes 3735560 | tf_op jit(solution)/shard_map/ppermute | solution.py:35
  35.4 29.8 %collective-permute-start.4 = (f32[128,2432]{1,0:T(8,128)S(1)}, f32[128,2432]{1,0:T(8,128)}, u32[]{:S(2)}, u32[]{:S(2)}) collective-permute-start(f32[128,2432]{1,0:T(8,128)S(1)} %pad_maximum_fusion.6.refs_0_), channel_id=1, source_target_pairs={{0,1},{1,0},{2,3},{3,2},{4,5},{5,4},{6,7},{7,6},{8,9},{9,8},{10,11... | collective-permute-start | bytes 3735560 | tf_op jit(solution)/shard_map/ppermute | solution.py:35
  38.0 49.1 %all-to-all-start = ((f32[4,32,2048]{2,1,0:T(8,128)}), f32[4,32,2048]{2,1,0:T(8,128)S(1)}, u32[]{:S(2)}, u32[]{:S(2)}) async-start(f32[4,32,2048]{2,1,0:T(8,128)} %broadcast_in_dim.13), calls=%async_computation | async-start | bytes 2097152 | tf_op jit(solution)/shard_map/all_to_all | solution.py:120
  67.9 31.7 %collective-permute-start.10 = (f32[128,2432]{1,0:T(8,128)}, f32[128,2432]{1,0:T(8,128)}, u32[]{:S(2)}, u32[]{:S(2)}) collective-permute-start(f32[128,2432]{1,0:T(8,128)} %collective-permute-done.4.refs_1_), channel_id=1, source_target_pairs={{0,8},{8,0},{1,9},{9,1},{2,10},{10,2},{3,11},{11,3},{4,12},{12,4},... | collective-permute-start | bytes 3735560 | tf_op jit(solution)/shard_map/ppermute | solution.py:35
  68.5 31.1 %collective-permute-start.11 = (f32[128,2432]{1,0:T(8,128)}, f32[128,2432]{1,0:T(8,128)}, u32[]{:S(2)}, u32[]{:S(2)}) collective-permute-start(f32[128,2432]{1,0:T(8,128)} %collective-permute-done.5.refs_2_), channel_id=1, source_target_pairs={{0,8},{8,0},{1,9},{9,1},{2,10},{10,2},{3,11},{11,3},{4,12},{12,4},... | collective-permute-start | bytes 3735560 | tf_op jit(solution)/shard_map/ppermute | solution.py:35
  87.1 39.8 %collective-permute-start.15 = (f32[128,2048]{1,0:T(8,128)S(1)}, f32[128,2048]{1,0:T(8,128)}, u32[]{:S(2)}, u32[]{:S(2)}) collective-permute-start(f32[128,2048]{1,0:T(8,128)S(1)} %bitcast.389), channel_id=1, source_target_pairs={{0,16},{16,0},{1,17},{17,1},{2,18},{18,2},{3,19},{19,3},{4,20},{20... | collective-permute-start | bytes 3145736 | tf_op jit(solution)/shard_map/ppermute | solution.py:35
  88.6 40.2 %collective-permute-start.14 = (f32[128,2048]{1,0:T(8,128)S(1)}, f32[128,2048]{1,0:T(8,128)}, u32[]{:S(2)}, u32[]{:S(2)}) collective-permute-start(f32[128,2048]{1,0:T(8,128)S(1)} %bitcast.390), channel_id=1, source_target_pairs={{0,1},{1,0},{2,3},{3,2},{4,5},{5,4},{6,7},{7,6},{8,9},{9,8},{10,11... | collective-permute-start | bytes 3145736 | tf_op jit(solution)/shard_map/ppermute | solution.py:35
  95.1 61.0 %all-to-all-start.1 = ((f32[4,64,1024]{2,1,0:T(8,128)}), f32[4,64,1024]{2,1,0:T(8,128)}, u32[]{:S(2)}, u32[]{:S(2)}) async-start(f32[4,64,1024]{2,1,0:T(8,128)} %broadcast_in_dim.14), calls=%async_computation.1 | async-start | bytes 2097152 | tf_op jit(solution)/shard_map/all_to_all | solution.py:120
  152.5 32.8 %collective-permute-start.33 = (f32[136,2048]{1,0:T(8,128)}, f32[136,2048]{1,0:T(8,128)}, u32[]{:S(2)}, u32[]{:S(2)}) collective-permute-start(f32[136,2048]{1,0:T(8,128)} %pad_maximum_fusion.5), channel_id=1, source_target_pairs={{0,2},{2,4},{4,6},{1,3},{3,5},{5,7},{8,10},{10,12},{12,14},{9,11},... | collective-permute-start | bytes 3342344 | tf_op jit(solution)/shard_map/ppermute | solution.py:272
  156.2 26.4 %collective-permute-start.24 = (f32[256,1024]{1,0:T(8,128)}, f32[256,1024]{1,0:T(8,128)}, u32[]{:S(2)}, u32[]{:S(2)}) collective-permute-start(f32[256,1024]{1,0:T(8,128)} %bitcast.72.refs_0_), channel_id=1, source_target_pairs={{0,1},{1,0},{2,3},{3,2},{4,5},{5,4},{6,7},{7,6},{8,9},{9,8},{10,11... | collective-permute-start | bytes 3145736 | tf_op jit(solution)/shard_map/ppermute | solution.py:35
  161.0 44.0 %collective-permute-start.23 = (f32[256,1024]{1,0:T(8,128)}, f32[256,1024]{1,0:T(8,128)}, u32[]{:S(2)}, u32[]{:S(2)}) collective-permute-start(f32[256,1024]{1,0:T(8,128)} %dynamic-slice_bitcast_fusion.2), channel_id=1, source_target_pairs={{0,1},{1,0},{2,3},{3,2},{4,5},{5,4},{6,7},{7,6},{8,9},{9,8},{10,11... | collective-permute-start | bytes 3145736 | tf_op jit(solution)/shard_map/ppermute | solution.py:35
  162.6 29.1 %collective-permute-start.25 = (f32[256,1024]{1,0:T(8,128)}, f32[256,1024]{1,0:T(8,128)}, u32[]{:S(2)}, u32[]{:S(2)}) collective-permute-start(f32[256,1024]{1,0:T(8,128)} %bitcast.72.refs_0_), channel_id=1, source_target_pairs={{0,16},{16,0},{1,17},{17,1},{2,18},{18,2},{3,19},{19,3},{4,20},{20... | collective-permute-start | bytes 3145736 | tf_op jit(solution)/shard_map/ppermute | solution.py:35
  187.9 44.8 %collective-permute-start.34 = (f32[128,2048]{1,0:T(8,128)}, f32[128,2048]{1,0:T(8,128)}, u32[]{:S(2)}, u32[]{:S(2)}) collective-permute-start(f32[128,2048]{1,0:T(8,128)} %multiply_add_fusion.4), channel_id=1, source_target_pairs={{0,4},{2,6},{1,5},{3,7},{8,12},{10,14},{9,13},{11,15},{16,20},{18,... | collective-permute-start | bytes 3145736 | tf_op jit(solution)/shard_map/ppermute | solution.py:272
  193.5 41.1 %collective-permute-start.28 = (f32[256,1024]{1,0:T(8,128)}, f32[256,1024]{1,0:T(8,128)S(1)}, u32[]{:S(2)}, u32[]{:S(2)}) collective-permute-start(f32[256,1024]{1,0:T(8,128)} %bitcast.72.refs_0_), channel_id=1, source_target_pairs={{0,8},{8,0},{1,9},{9,1},{2,10},{10,2},{3,11},{11,3},{4,12},{12,4},... | collective-permute-start | bytes 3145736 | tf_op jit(solution)/shard_map/ppermute | solution.py:35
  205.1 29.6 %collective-permute-start.29 = (f32[256,1024]{1,0:T(8,128)}, f32[256,1024]{1,0:T(8,128)S(1)}, u32[]{:S(2)}, u32[]{:S(2)}) collective-permute-start(f32[256,1024]{1,0:T(8,128)} %collective-permute-done.24.refs_1_), channel_id=1, source_target_pairs={{0,8},{8,0},{1,9},{9,1},{2,10},{10,2},{3,11},{11,3},{4,12},{12,4},... | collective-permute-start | bytes 3145736 | tf_op jit(solution)/shard_map/ppermute | solution.py:35
  205.1 29.6 %collective-permute-start.30 = (f32[256,1024]{1,0:T(8,128)}, f32[256,1024]{1,0:T(8,128)S(1)}, u32[]{:S(2)}, u32[]{:S(2)}) collective-permute-start(f32[256,1024]{1,0:T(8,128)} %collective-permute-done.25.refs_2_), channel_id=1, source_target_pairs={{0,8},{8,0},{1,9},{9,1},{2,10},{10,2},{3,11},{11,3},{4,12},{12,4},... | collective-permute-start | bytes 3145736 | tf_op jit(solution)/shard_map/ppermute | solution.py:35
  271.2 27.0 %collective-permute-start.36 = (f32[1024,1024]{1,0:T(8,128)}, f32[1024,1024]{1,0:T(8,128)}, u32[]{:S(2)}, u32[]{:S(2)}) collective-permute-start(f32[1024,1024]{1,0:T(8,128)} %fusion.4), channel_id=1, source_target_pairs={{0,8},{8,0},{1,9},{9,1},{2,10},{10,2},{3,11},{11,3},{4,12},{12,4},... | collective-permute-start | bytes 12582920 | tf_op jit(solution)/shard_map/ppermute | solution.py:35
  279.8 28.8 %collective-permute-start.37 = (f32[136,2048]{1,0:T(8,128)}, f32[136,2048]{1,0:T(8,128)}, u32[]{:S(2)}, u32[]{:S(2)}) collective-permute-start(f32[136,2048]{1,0:T(8,128)} %pad_maximum_fusion.4), channel_id=1, source_target_pairs={{2,0},{4,2},{6,4},{3,1},{5,3},{7,5},{10,8},{12,10},{14,12},{11,9},... | collective-permute-start | bytes 3342344 | tf_op jit(solution)/shard_map/ppermute | solution.py:272
  296.6 25.4 %collective-permute-start.35 = (f32[256,1024]{1,0:T(8,128)}, f32[256,1024]{1,0:T(8,128)}, u32[]{:S(2)}, u32[]{:S(2)}) collective-permute-start(f32[256,1024]{1,0:T(8,128)} %dynamic-slice_bitcast_fusion.1), channel_id=1, source_target_pairs={{0,1},{1,0},{2,3},{3,2},{4,5},{5,4},{6,7},{7,6},{8,9},{9,8},{10,11... | collective-permute-start | bytes 3145736 | tf_op jit(solution)/shard_map/ppermute | solution.py:35
  303.9 96.8 %collective-permute-start.38 = (f32[512,2048]{1,0:T(8,128)}, f32[512,2048]{1,0:T(8,128)}, u32[]{:S(2)}, u32[]{:S(2)}) collective-permute-start(f32[512,2048]{1,0:T(8,128)} %fusion.17), channel_id=1, source_target_pairs={{0,8},{8,0},{1,9},{9,1},{2,10},{10,2},{3,11},{11,3},{4,12},{12,4},... | collective-permute-start | bytes 12582920 | tf_op jit(solution)/shard_map/ppermute | solution.py:35
  311.3 27.4 %collective-permute-start.43 = (f32[128,2048]{1,0:T(8,128)}, f32[128,2048]{1,0:T(8,128)}, u32[]{:S(2)}, u32[]{:S(2)}) collective-permute-start(f32[128,2048]{1,0:T(8,128)} %multiply_add_fusion.2), channel_id=1, source_target_pairs={{4,0},{6,2},{5,1},{7,3},{12,8},{14,10},{13,9},{15,11},{20,16},{22,... | collective-permute-start | bytes 3145736 | tf_op jit(solution)/shard_map/ppermute | solution.py:272
  353.5 25.2 %collective-permute-start.41 = (f32[2,64,1024]{2,1,0:T(8,128)S(1)}, f32[2,64,1024]{2,1,0:T(8,128)S(1)}, u32[]{:S(2)}, u32[]{:S(2)}) collective-permute-start(f32[2,64,1024]{2,1,0:T(8,128)S(1)} %fusion.56), channel_id=1, source_target_pairs={{0,16},{16,0},{1,17},{17,1},{2,18},{18,2},{3,19},{19,3},{4,20},{20... | collective-permute-start | bytes 1572872 | tf_op jit(solution)/shard_map/ppermute | solution.py:35
  382.7 87.8 %all-to-all-start.3 = ((f32[4,64,1024]{2,1,0:T(8,128)}), f32[4,64,1024]{2,1,0:T(8,128)}, u32[]{:S(2)}, u32[]{:S(2)}) async-start(f32[4,64,1024]{2,1,0:T(8,128)} %pad_maximum_fusion.8), calls=%async_computation.3 | async-start | bytes 2097152 | tf_op jit(solution)/shard_map/all_to_all | solution.py:209
  460.8 55.6 %collective-permute-start.46 = (f32[512,2432]{1,0:T(8,128)}, f32[512,2432]{1,0:T(8,128)}, u32[]{:S(2)}, u32[]{:S(2)}) collective-permute-start(f32[512,2432]{1,0:T(8,128)} %maximum_add_fusion), channel_id=1, source_target_pairs={{0,8},{8,0},{1,9},{9,1},{2,10},{10,2},{3,11},{11,3},{4,12},{12,4},... | collective-permute-start | bytes 14942216 | tf_op jit(solution)/shard_map/ppermute | solution.py:35
  464.8 25.9 %collective-permute-start.44 = (f32[2,2,32,2048]{3,2,1,0:T(8,128)}, f32[2,2,32,2048]{3,2,1,0:T(8,128)}, u32[]{:S(2)}, u32[]{:S(2)}) collective-permute-start(f32[2,2,32,2048]{3,2,1,0:T(8,128)} %fusion.25), channel_id=1, source_target_pairs={{0,1},{1,0},{2,3},{3,2},{4,5},{5,4},{6,7},{7,6},{8,9},{9,8},{10,11... | collective-permute-start | bytes 3145736 | tf_op jit(solution)/shard_map/ppermute | solution.py:35
  467.8 25.9 %collective-permute-start.45 = (f32[2,2,32,2048]{3,2,0,1:T(8,128)}, f32[2,2,32,2048]{3,2,0,1:T(8,128)}, u32[]{:S(2)}, u32[]{:S(2)}) collective-permute-start(f32[2,2,32,2048]{3,2,0,1:T(8,128)} %fusion.27), channel_id=1, source_target_pairs={{0,16},{16,0},{1,17},{17,1},{2,18},{18,2},{3,19},{19,3},{4,20},{20... | collective-permute-start | bytes 3145736 | tf_op jit(solution)/shard_map/ppermute | solution.py:35
  511.1 31.5 %all-to-all-start.2 = ((f32[4,32,2048]{2,1,0:T(8,128)}), f32[4,32,2048]{2,1,0:T(8,128)S(1)}, u32[]{:S(2)}, u32[]{:S(2)}) async-start(f32[4,32,2048]{2,1,0:T(8,128)} %pad_maximum_fusion.7), calls=%async_computation.2 | async-start | bytes 2097152 | tf_op jit(solution)/shard_map/all_to_all | solution.py:209
  524.5 28.3 %collective-permute-start.50 = (f32[2,2,32,2432]{3,2,1,0:T(8,128)}, f32[2,2,32,2432]{3,2,1,0:T(8,128)}, u32[]{:S(2)}, u32[]{:S(2)}) collective-permute-start(f32[2,2,32,2432]{3,2,1,0:T(8,128)} %fusion.9), channel_id=1, source_target_pairs={{0,1},{1,0},{2,3},{3,2},{4,5},{5,4},{6,7},{7,6},{8,9},{9,8},{10,11... | collective-permute-start | bytes 3735560 | tf_op jit(solution)/shard_map/ppermute | solution.py:35
  527.2 28.2 %collective-permute-start.51 = (f32[2,2,32,2432]{3,2,0,1:T(8,128)}, f32[2,2,32,2432]{3,2,0,1:T(8,128)}, u32[]{:S(2)}, u32[]{:S(2)}) collective-permute-start(f32[2,2,32,2432]{3,2,0,1:T(8,128)} %fusion.10), channel_id=1, source_target_pairs={{0,16},{16,0},{1,17},{17,1},{2,18},{18,2},{3,19},{19,3},{4,20},{20... | collective-permute-start | bytes 3735560 | tf_op jit(solution)/shard_map/ppermute | solution.py:35
  584.4 36.3 %collective-permute-start.52 = (f32[256,1024]{1,0:T(8,128)}, f32[256,1024]{1,0:T(8,128)}, u32[]{:S(2)}, u32[]{:S(2)}) collective-permute-start(f32[256,1024]{1,0:T(8,128)} %dynamic-slice_bitcast_fusion), channel_id=1, source_target_pairs={{0,1},{1,0},{2,3},{3,2},{4,5},{5,4},{6,7},{7,6},{8,9},{9,8},{10,11... | collective-permute-start | bytes 3145736 | tf_op jit(solution)/shard_map/ppermute | solution.py:35
  (118 other events, 1415.5 us)

commit v3 on v2

--- a/solution.py
+++ b/solution.py
@@ -54,17 +54,21 @@
     return lax.optimization_barrier((value,) + others)[0]
 
 
-def place_kernel(count, own_rows, where_ref, *refs):
-    blocks, whole = (refs[:count], refs[count])
+def place_kernel(count, own_rows, parts, where_ref, *refs):
+    blocks, wholes = (refs[:count], refs[count:])
     spot = 0
     for block in blocks:
         for k in range(block.shape[0] // own_rows):
-            at = pl.multiple_of(where_ref[spot] * own_rows, own_rows)
-            whole[pl.ds(at, own_rows), :] = block[k * own_rows : (k + 1) * own_rows, :]
+            for whole, cuts in zip(wholes, parts):
+                for n, (start, stop) in enumerate(cuts):
+                    row = (where_ref[spot] * len(cuts) + n) * own_rows
+                    whole[pl.ds(pl.multiple_of(row, own_rows), own_rows), :] = block[
+                        k * own_rows : (k + 1) * own_rows, start:stop
+                    ]
             spot += 1
 
 
-def place(blocks, own_rows):
+def place(blocks, own_rows, parts):
     sizes = {axis: lax.axis_size(axis) for axis in AXES}
     index = {axis: lax.axis_index(axis) for axis in AXES}
     devices = 1
@@ -79,23 +83,26 @@
                 at = at * sizes[axis] + (index[axis] - back) % sizes[axis]
             where.append(at)
     arrays = [block for _, _, block in blocks]
-    cols = arrays[0].shape[1]
+    shapes = [(devices * own_rows * len(cuts), cuts[0][1] - cuts[0][0]) for cuts in parts]
     if own_rows % 8:
-        whole = jnp.zeros((devices, own_rows, cols), F32)
+        whole = jnp.zeros((devices, own_rows, arrays[0].shape[1]), F32)
         spots = iter(where)
         for block in arrays:
             for k in range(block.shape[0] // own_rows):
                 whole = lax.dynamic_update_slice_in_dim(
                     whole, block[None, k * own_rows : (k + 1) * own_rows], next(spots), 0
                 )
-        return whole.reshape(devices * own_rows, cols)
+        return [
+            jnp.concatenate([whole[:, :, a:b] for a, b in cuts], axis=1).reshape(shape)
+            for cuts, shape in zip(parts, shapes)
+        ]
     return pl.pallas_call(
-        functools.partial(place_kernel, len(blocks), own_rows),
+        functools.partial(place_kernel, len(blocks), own_rows, parts),
         in_specs=[pl.BlockSpec(memory_space=pltpu.SMEM)]
         + [pl.BlockSpec(memory_space=pltpu.VMEM)] * len(blocks),
-        out_specs=pl.BlockSpec(memory_space=pltpu.VMEM),
-        out_shape=jax.ShapeDtypeStruct((devices * own_rows, cols), F32),
-        compiler_params=pltpu.CompilerParams(vmem_limit_bytes=32 * 1024 * 1024),
+        out_specs=[pl.BlockSpec(memory_space=pltpu.VMEM)] * len(parts),
+        out_shape=[jax.ShapeDtypeStruct(shape, F32) for shape in shapes],
+        compiler_params=pltpu.CompilerParams(vmem_limit_bytes=48 * 1024 * 1024),
         cost_estimate=FREE,
         name="place",
     )(jnp.stack(where).astype(jnp.int32), *arrays)
@@ -106,8 +113,8 @@
 
 
 class Gather:
-    def __init__(self, piece):
-        self.piece, self.rows = (piece, piece.shape[0])
+    def __init__(self, piece, share):
+        self.piece, self.rows, self.share = (piece, piece.shape[0], share)
 
     def line(self, *tie):
         (piece,) = tied([self.piece], *tie)
@@ -126,8 +133,15 @@
         self.rings = {axis: ring(block, axis)[1:] for axis in ("p", "y")}
         return [b for r in self.rings.values() for b in r]
 
+    def keep_near(self, *others):
+        self.rings = {axis: tied(r, *others) for axis, r in self.rings.items()}
+
+    def keep_far(self, *others):
+        arrays = tied([b for _, _, b in self.corners], *others)
+        self.corners = [(slot, lines, b) for (slot, lines, _), b in zip(self.corners, arrays)]
+
     def far(self, *tie):
-        middle = len(self.lines) // 2
+        middle = int(len(self.lines) * self.share)
         cut = middle * self.rows
         sides = {"p": [b[:cut] for b in self.rings["p"]], "y": [b[cut:] for b in self.rings["y"]]}
         other = {"p": "y", "y": "p"}
@@ -177,19 +191,26 @@
             ([v[:, middle:] for v in both], ["y", "zc", "p"]),
         ]
 
-    def stage(self, axes, *tie):
-        self.came, parts = ([], [])
+    def stage(self, axes):
+        self.came, self.sends, parts = ([], [], [])
         for (addends, left), axis in zip(self.parts, axes):
             count, index, dim = (lax.axis_size(axis), lax.axis_index(axis), left.index(axis))
             came = []
             for k in range(1, count):
                 moving = indexed(addends, (index + k) % count, dim)
-                if tie:
-                    moving = after(moving, *tie)
+                self.sends.append(moving)
                 came.append(shift(moving, axis, k))
             kept = [lax.dynamic_index_in_dim(v, index, dim, keepdims=False) for v in addends]
             parts.append((kept + came, [a for a in left if a != axis]))
             self.came += came
+            self.fresh = len(came)
+        self.parts = parts
+
+    def keep(self, *others):
+        parts = []
+        for addends, left in self.parts:
+            fresh = self.fresh if left != ["y", "zc", "p"] else 1
+            parts.append((addends[:-fresh] + tied(addends[-fresh:], *others), left))
         self.parts = parts
 
     def last(self, *tie):
@@ -203,9 +224,9 @@
         ]
         self.kept = lax.dynamic_index_in_dim(line, index, 0, keepdims=False)
 
-    def last_at_once(self, *tie):
+    def last_at_once(self):
         line = jnp.concatenate([functools.reduce(jnp.add, v) for v, _ in self.parts], axis=0)
-        (line,) = tied([line], *tie)
+        self.sends = [line]
         line = lax.all_to_all(line, "zc", 0, 0)
         self.came, self.kept = ([line[k] for k in range(1, line.shape[0])], line[0])
 
@@ -220,27 +241,37 @@
             values = values + shift(values, axis)
         else:
             held = jnp.stack(offsets(values, axis))
-            total = None
-            for k in range(count):
-                part = lax.dynamic_index_in_dim(held, (index - k) % count, 0, keepdims=False)
-                total = part if total is None else total + part
-            values = total
+            values = functools.reduce(
+                jnp.add,
+                [
+                    lax.dynamic_index_in_dim(held, (index - k) % count, 0, keepdims=False)
+                    for k in range(count)
+                ],
+            )
     return values
 
 
-def to_span(block, mine):
-    keep = lax.dynamic_index_in_dim(block, mine, 0, keepdims=False)
-    other = shift(lax.dynamic_index_in_dim(block, 1 - mine, 0, keepdims=False), "p")
-    first = mine == 0
-    return jnp.concatenate([jnp.where(first, keep, other), jnp.where(first, other, keep)], axis=0)
-
-
-def from_span(span, mine):
-    block = span.reshape(2, -1, span.shape[-1])
-    keep = lax.dynamic_index_in_dim(block, mine, 0, keepdims=False)
-    other = shift(lax.dynamic_index_in_dim(block, 1 - mine, 0, keepdims=False), "p")
-    first = mine == 0
-    return jnp.stack([jnp.where(first, keep, other), jnp.where(first, other, keep)], axis=0)
+class Exchange:
+    def __init__(self, block, mine):
+        self.mine = mine
+        self.keep = lax.dynamic_index_in_dim(block, mine, 0, keepdims=False)
+        self.other = shift(lax.dynamic_index_in_dim(block, 1 - mine, 0, keepdims=False), "p")
+
+    def result(self, join, *others):
+        (other,) = tied([self.other], *others)
+        first = self.mine == 0
+        return join([jnp.where(first, self.keep, other), jnp.where(first, other, self.keep)], axis=0)
+
+
+def before_span(block, mine):
+    count = lax.axis_size("zc")
+    routes = [[(2 * i + 1, 2 * i + 2 + k) for i in range(count - 1)] for k in (0, 1)]
+    ends = [lax.ppermute(block[k, -EDGE:], ("zc", "p"), routes[k]) for k in (0, 1)]
+    return jnp.where(mine == 0, ends[0], ends[1])
+
+
+def halves(span):
+    return span.reshape(2, -1, span.shape[-1])
 
 
 class States:
@@ -255,11 +286,11 @@
         self.held = [None] * self.chunks
         self.span = None
 
-    def send(self, *tie):
+    def send(self):
         w = self.distance
         pairs = [(i, i + w) for i in range(self.count - w)]
         route = [(b, a) if self.reverse else (a, b) for a, b in pairs]
-        came = []
+        self.came, self.sends = ([], [])
         for k in range(self.chunks):
             block = self.added[k]
             if self.held[k] is not None:
@@ -267,10 +298,12 @@
             if k == 0 and 2 * w < self.count:
                 span = self.decay if self.span is None else self.decay * self.span
                 block = jnp.concatenate([block, span], axis=0)
-            if tie:
-                block = after(block, *tie)
-            came.append(lax.ppermute(block, "zc", route))
-        rows = self.added[0].shape[0]
+            self.sends.append(block)
+            self.came.append(lax.ppermute(block, "zc", route))
+
+    def absorb(self, *others):
+        w, rows = (self.distance, self.added[0].shape[0])
+        came = tied(self.came, *others) if others else self.came
         for k in range(self.chunks):
             new = came[k][:rows]
             if self.held[k] is not None:
@@ -280,11 +313,18 @@
             span = came[0][rows:]
             self.span = span if self.span is None else self.span * span
         self.distance = 2 * w
-        return came
-
-    def result(self, *tie):
+
+    def go_on(self, *others):
+        self.absorb(*others)
         while self.distance < self.count:
-            self.send(*tie)
+            self.send()
+            if 2 * self.distance >= self.count:
+                return
+            self.absorb()
+
+    def result(self, *others):
+        if self.distance < self.count:
+            self.absorb(*others)
         return jnp.concatenate(self.held, axis=0)
 
 
@@ -524,7 +564,8 @@
     act_ref,
     logd_ref,
     inner_ref,
-    gate_ref,
+    gate_left_ref,
+    gate_right_ref,
     dng_ref,
     local_ref,
     enter_ref,
@@ -561,7 +602,7 @@
     def gate(k, carry):
         rows = pl.ds(pl.multiple_of(k * 8, 8), 8)
         ssd = out[rows, :]
-        gate_in = gate_ref[rows, :]
+        gate_in = jnp.concatenate([gate_left_ref[rows, :], gate_right_ref[rows, :]], axis=1)
         sg = jax.nn.sigmoid(gate_in)
         silu = gate_in * sg
         gated = ssd * silu
@@ -586,7 +627,7 @@
 GATE_UNROLL = 4
 
 
-def mixer(act, logd, inner, gate_in, dng, local, entering, before, ggain, spreader):
+def mixer(act, logd, inner, gates, dng, local, entering, before, ggain, spreader):
     rows = act.shape[0]
     cuts = rows // CUT
 
@@ -601,7 +642,8 @@
             back(MIXED),
             back(HEADS),
             back(DI),
-            back(DI),
+            back(DI // 2),
+            back(DI // 2),
             back(DI),
             pl.BlockSpec((1, STATE, DI), lambda i: (jnp.maximum(cuts - 2 - i, 0), 0, 0)),
             full((STATE, DI)),
@@ -633,7 +675,7 @@
         compiler_params=params(),
         cost_estimate=FREE,
         name="mixer",
-    )(act, logd, inner, gate_in, dng, local, entering, before, ggain, spreader)
+    )(act, logd, inner, *gates, dng, local, entering, before, ggain, spreader)
 
 
 def back_intra_kernel(
@@ -935,6 +977,54 @@
     )
 
 
+COLUMNS = 512
+
+
+def right_kernel(x_ref, w_ref, added_ref, scale_ref, out_ref):
+    out_ref[...] = (nn(x_ref[...], w_ref[...]) + added_ref[...]) * scale_ref[...]
+
+
+def right(x, w, added, scale):
+    (rows, depth), cols = (x.shape, w.shape[1])
+    tile = pl.BlockSpec((rows, COLUMNS), lambda j: (0, j))
+    return pl.pallas_call(
+        right_kernel,
+        grid=(cols // COLUMNS,),
+        in_specs=[
+            full((rows, depth)), pl.BlockSpec((depth, COLUMNS), lambda j: (0, j)), tile, full((rows, 1)),
+        ],
+        out_specs=tile,
+        out_shape=jax.ShapeDtypeStruct((rows, cols), F32),
+        compiler_params=params(),
+        cost_estimate=FREE,
+        name="right",
+    )(x, w, added, scale)
+
+
+def right_back_kernel(x_ref, *refs):
+    *w_refs, out_ref = refs
+    total, at = (None, 0)
+    for w_ref in w_refs:
+        part = nt(x_ref[:, at : at + w_ref.shape[1]], w_ref[...])
+        total, at = (part if total is None else total + part, at + w_ref.shape[1])
+    out_ref[...] = total
+
+
+def right_back(x, weights):
+    rows, cols = (x.shape[0], weights[0].shape[0])
+    return pl.pallas_call(
+        right_back_kernel,
+        grid=(cols // COLUMNS,),
+        in_specs=[full(x.shape)]
+        + [pl.BlockSpec((COLUMNS, w.shape[1]), lambda j: (j, 0)) for w in weights],
+        out_specs=pl.BlockSpec((rows, COLUMNS), lambda j: (0, j)),
+        out_shape=jax.ShapeDtypeStruct((rows, cols), F32),
+        compiler_params=params(),
+        cost_estimate=FREE,
+        name="right_back",
+    )(x, *weights)
+
+
 def head_spreader():
     head = lax.broadcasted_iota(jnp.int32, (3 * HEADS, DI), 0) % HEADS
     return (head == lax.broadcasted_iota(jnp.int32, (3 * HEADS, DI), 1) // HDIM).astype(BF16)
@@ -969,25 +1059,26 @@
     in_piece = in_weight.reshape(own_rows, -1)
     small = jnp.concatenate([conv_weight, conv_bias])
     padded = jnp.pad(small, (0, SPARE * own_rows - small.shape[0])).reshape(own_rows, SPARE)
-    conv = Gather(jnp.concatenate([in_piece[:, DI:], padded], axis=1))
-    gate = Gather(in_piece[:, :DI])
-    out = Gather(out_weight.reshape(-1, width))
+    conv = Gather(jnp.concatenate([in_piece[:, DI:], padded], axis=1), 0.5)
+    edge = before_span(hidden_in, mine)
     conv.line()
-    hidden = to_span(hidden_in, mine)
+    trade = Exchange(hidden_in, mine)
+    hidden = trade.result(jnp.concatenate)
     rows = hidden.shape[0]
-    near = conv.near()
+    out_piece = out_weight.reshape(-1, width)
+    rest = jnp.concatenate([in_piece[:, :width], in_piece[:, width:DI], out_piece], axis=0)
+    rest = lax.all_gather(rest, AXES, axis=0).reshape(devices, -1, width)
+    w_gates = [
+        rest[:, k * own_rows : (k + 1) * own_rows].reshape(width, width) for k in range(DI // width)
+    ]
+    w_out = rest[:, DI // width * own_rows :].reshape(DI, width)
+    near = conv.near(trade.other)
     conv_over = conv.across(conv.held_near()[:1], conv.block)
-    far = conv.far(hidden)
+    far = conv.far()
     conv_over += conv.across(conv.held_near()[1:])
-    gate.line_at_once(conv.block)
-    other = to_span(tied([cotangent], *near)[0], mine)
     conv_over += conv.across(conv.corners)
-    w_conv = place(conv.held() + conv_over, conv.rows)
-    gate_near = gate.near(*far)
-    out.line_at_once(gate.block, *far)
-    edge = lax.ppermute(
-        tied([hidden[rows - EDGE :]], *near)[0], "zc", [(i, i + 1) for i in range(count - 1)]
-    )
+    (w_conv,) = place(conv.held() + conv_over, conv.rows, [[(0, WIDE)]])
+    other = Exchange(tied([cotangent], *far)[0], mine)
     smalls = w_conv[:, RATED:].reshape(devices, own_rows * SPARE)
     taps = smalls[:, : conv_weight.shape[0]].reshape(CONV, MIXED)
     bias = smalls[:, conv_weight.shape[0] : small.shape[0]].reshape(1, MIXED)
@@ -1009,80 +1100,78 @@
     )
     total_row = jnp.repeat(total[0], HDIM).reshape(1, DI)
     states = States(total_row, local[-1], False)
-    came = states.send(*gate_near)
-    gate_far = gate.far(act)
-    gate_over = gate.across(gate.held_near(), act)
-    within = intra(act, step, logd, skip_row, spreader)
-    out_near = out.near(within, *gate_far)
-    while states.distance < count:
-        came = states.send()
-    gate_over += gate.across(gate.corners, within)
-    w_gate = place(gate.held() + gate_over, gate.rows)
-    gate_in = nn(tied([inner], within)[0], w_gate)
-    out_far = out.far(gate_in)
-    out_over = out.across(out.held_near(), gate_in) + out.across(out.corners)
-    w_out = place(out.held() + out_over, out.rows)
-    grad_out = other * valid
-    dng = nt(grad_out, w_out)
-    entering = states.result()
+    states.send()
+    within = intra(tied([act], *states.sends)[0], step, logd, skip_row, spreader)
+    (turn,) = tied([inner], within)
+    gates = [nn(turn, w) for w in w_gates]
+    states.go_on(*gates)
+    grad_out = other.result(jnp.concatenate, within) * valid
+    dng = nt(tied([grad_out], *gates, *states.sends)[0], w_out)
+    entering = states.result(dng)
     ng, dy, dz, gin, ggrad, skipg = mixer(
-        act, logd, within, gate_in, dng, local, entering, before, gated_gain.reshape(1, DI), spreader
+        act, logd, within, gates, dng, local, entering, before, gated_gain.reshape(1, DI), spreader
     )
     ng_keep, ng_send = core_columns(ng)
     in_keep, in_send = core_columns(normed)
     grads = States(total_row, gin[0], True)
-    came = grads.send()
-    first = tn(ng_send, grad_out)
+    grads.send()
+    (turn,) = tied([ng_send], *grads.sends)
+    first = tn(turn, grad_out)
     (turn,) = tied([grad_out], first)
     second = tn(ng_keep, turn)
     grad_wout = Scatter(first, second)
-    branch = nn(tied([ng], second)[0], w_out)
-    (send_from,) = tied([dz], branch, *grad_wout.came)
+    branch = right(tied([ng], second)[0], w_out, hidden, valid)
+    grads.go_on(branch)
+    grad_wout.keep(branch)
     grad_wout.stage(("p", "y"))
-    first = tn(in_send[:rows], send_from)
-    (turn,) = tied([send_from], first)
+    (turn,) = tied([dz], branch, *grads.sends, *grad_wout.sends)
+    first = tn(in_send[:rows], turn)
+    (turn,) = tied([turn], first)
     second = tn(in_keep[:rows], turn)
     grad_wgate = Scatter(first, second)
-    back_parts = back_intra(tied([act], second, *came)[0], step, logd, dy, spreader)
-    while grads.distance < count:
-        came = grads.send()
-    (turn,) = tied([dz], back_parts[1], *grad_wgate.came, *grad_wout.came)
+    back_parts = back_intra(tied([act], second)[0], step, logd, dy, spreader)
+    grad_wout.keep(back_parts[1])
+    grad_wgate.keep(back_parts[1])
     grad_wout.stage(("y", "p"))
-    dgate_normed = nt(turn, w_gate)
     grad_wgate.stage(("p", "y"))
-    gout = grads.result()
+    (turn,) = tied([dz], back_parts[1], *grad_wout.sends, *grad_wgate.sends)
+    dgate_normed = right_back(turn, w_gates)
+    grad_wout.keep(dgate_normed)
+    grad_wout.last_at_once()
+    gout = grads.result(dgate_normed)
     dproj, dtaps, dbias, dlog, ddtb = back(
-        tied([act], dgate_normed, *grad_wout.came)[0], step, slope, logd, dy, *back_parts, local,
+        tied([act], dgate_normed, *grad_wout.sends)[0], step, slope, logd, dy, *back_parts, local,
         entering, before, gin, gout, proj, taps, bias, alog_row, skip_row, spreader, gatherer,
     )
-    grad_wout.last_at_once()
     dtaps = jnp.sum(dtaps.reshape(CONV, 8, MIXED), axis=1).reshape(devices, -1)
     dbias = jnp.sum(dbias, axis=0).reshape(devices, -1)
     dsmall = jnp.concatenate([dtaps, dbias], axis=1)
     dsmall = jnp.pad(dsmall, ((0, 0), (0, SPARE * own_rows - small.shape[0])))
     dsmall = jnp.pad(dsmall.reshape(width, SPARE), ((0, 0), (RATED, 0)))
     small_keep, small_send = (core_rows(dsmall, k) for k in (0, 1))
-    first = tn(in_send, dproj) + small_send
-    (turn,) = tied([dproj], first, *grad_wgate.came)
+    grad_wgate.keep(ddtb)
+    grad_wgate.stage(("y", "p"))
+    (turn,) = tied([dproj], *grad_wgate.sends)
+    first = tn(in_send, turn) + small_send
+    (turn,) = tied([dproj], first)
     second = tn(in_keep, turn) + small_keep
     grad_wconv = Scatter(first, second)
-    grad_wgate.stage(("y", "p"))
-    (turn,) = tied([dproj], second)
-    dnormed = nt(turn, w_conv)
-    (dnormed,) = tied([dnormed], *grad_wconv.came, *grad_wgate.came)
+    grad_wconv.keep(second)
+    grad_wconv.stage(("p", "y"))
+    traded = Exchange(halves(tied([branch], ddtb)[0]), mine)
+    dnormed = nt(tied([dproj], second, *grad_wconv.sends)[0], w_conv)
+    grad_wgate.keep(dnormed)
     grad_wgate.last_at_once()
-    grad_wconv.stage(("p", "y"))
+    near = grad_wconv.came
+    (dnormed,) = tied([dnormed], *grad_wgate.sends)
+    output = traded.result(jnp.stack, dnormed)
     returned = lax.ppermute(dnormed[rows:], "zc", [(i + 1, i) for i in range(count - 1)])
-    near = grad_wconv.came
-    output = from_span((hidden + branch) * valid, mine)
-    grad_wconv.stage(("y", "p"))
-    grad_wconv.last()
     dnormed = dnormed[:rows] + dgate_normed
     dnormed = dnormed + jnp.pad(returned, ((rows - EDGE, 0), (0, 0)))
     unit = unit[:rows]
     dunit = dnormed * norm_gain
     dhidden = scale[:rows] * (dunit - unit * jnp.mean(dunit * unit, axis=1, keepdims=True))
-    grad_input = from_span(tied([grad_out + dhidden], *near)[0], mine)
+    grad_input = Exchange(halves(tied([grad_out + dhidden], *near)[0]), mine).result(jnp.stack)
     grad_skip = jnp.sum(jnp.sum(skipg, axis=0).reshape(HEADS, HDIM), axis=1)
     sums = jnp.concatenate(
         [
@@ -1095,6 +1184,8 @@
     )
     (sums,) = tied([jnp.pad(sums, (0, -sums.shape[0] % 128)).reshape(-1, 128)], *near)
     sums = sum_everywhere(sums).reshape(-1)
+    grad_wconv.stage(("y", "p"))
+    grad_wconv.last()
     parts = []
     for size in (width, DI, HEADS, HEADS, HEADS):
         parts.append(sums[:size])

time: 629 us -> 614 us (0.976)
  starting transfers between devices: 103 us -> 57 us
  Pallas kernels: 99.9 us -> 122 us
  matrix products: 96.8 us -> 83.5 us
  between operations: 2.3 us -> 15.5 us
  waiting for transfers between devices: 181 us -> 188 us
    ppermute x58 -> x40, starting transfers between devices: 53.5 us -> 29.7 us  [shift(): lax.ppermute(block, axis, [(i, (i + step) % count) for i in range(count)])]
    pallas_call x3, Pallas kernels: 9.82 us -> 31.4 us  [the longest x1 12.9 us: right(): pl.pallas_call(right_kernel, grid=(cols // COLUMNS,), in_specs=[full((row...]
    ppermute x58 -> x40, waiting for transfers between devices: 148 us -> 128 us  [shift(): lax.ppermute(block, axis, [(i, (i + step) % count) for i in range(count)])]
    ppermute x1, waiting for transfers between devices: 3.81 us -> 18.5 us  [per_device(): lax.ppermute(dnormed[rows:], 'zc', [(i + 1, i) for i in range(count - 1)])]
    unnamed x163 -> x141, local copies, waits for them, and re-layouts: 5.16 us -> 16.2 us
    all_to_all x2 -> x0, starting transfers between devices: 9.76 us -> none  [line_at_once(): lax.all_to_all(jnp.broadcast_to(piece, (count,) + piece.shape), 'zc', 0, 0)]
    dot_general x3 -> x2, matrix products: 30.7 us -> 21.1 us  [nt(): lax.dot_general(a, b, (((1,), (1,)), ((), ())), precision=precision, pref...]
    slice x5 -> x7, local copies, waits for them, and re-layouts: 1.8 us -> 10.4 us  [the longest x1 5.01 us: per_device(): w_out = rest[:, DI // width * own_rows:].reshape(DI, width)]
  transfers between devices with their start and end apart: 68 -> 50, of which waited for: 27 -> 17; matrix products, arithmetic and copies ran while one was open for 34% -> 27% of each run, Pallas kernels for 13% -> 17%
where the time goes in v3:
time: 614 us; the launch traced here: 603 us
  waiting for transfers between devices  188 us (31%)
  Pallas kernels  122 us (20%)
  matrix products  83.5 us (14%)
  other arithmetic  69.3 us (11%)
  local copies, waits for them, and re-layouts  67.4 us (11%)
  starting transfers between devices  57 us (9%)
  between operations  15.5 us (3%)
    ppermute x40, waiting for transfers between devices, shift(): lax.ppermute(block, axis, [(i, (i + step) % count) for i in range(count)])  128 us
    dot_general x6, matrix products, tn(): lax.dot_general(a, b, (((0,), (0,)), ((), ())), precision=precision, pref...  39.3 us
    pallas_call x1, Pallas kernels, back(): pl.pallas_call(back_kernel, grid=(cuts,), in_specs=[at(MIXED), at(HEADS),...  33.7 us
    ppermute x4, waiting for transfers between devices, send(): self.came.append(lax.ppermute(block, 'zc', route))  33.5 us
    ppermute x40, starting transfers between devices, shift(): lax.ppermute(block, axis, [(i, (i + step) % count) for i in range(count)])  29.7 us
    dot_general x3, matrix products, nn(): return jnp.dot(a, b, precision=precision, preferred_element_type=F32)  23.1 us
    dot_general x2, matrix products, nt(): lax.dot_general(a, b, (((1,), (1,)), ((), ())), precision=precision, pref...  21.1 us
    add x12, other arithmetic, indexed(): total = part if total is None else total + part  18.7 us
  transfers between devices with their start and end apart: 50, of which 17 were waited for; matrix products, arithmetic and copies ran while one was open for 27% of the time, Pallas kernels for 17%

profile of v3, /device:TPU:8, one launch (start us, length us, event | category | flops | bytes accessed | tf_op | source)
XLA Modules:
  0.0 603.5 jit_solution(15943003027047835454)
XLA Ops:
  18.2 16.9 %collective-permute-done.3 = f32[32,2432]{1,0:T(8,128)S(1)} collective-permute-done((f32[32,2432]{1,0:T(8,128)S(1)}, f32[32,2432]{1,0:T(8,128)S(1)}, u32[]{:S(2)}, u32[]{:S(2)}) %collective-permute-start.3) | collective-permute-done | bytes 311328 | tf_op jit(solution)/shard_map/ppermute | solution.py:35
  35.2 17.6 %collective-permute-done.4 = f32[32,2432]{1,0:T(8,128)S(1)} collective-permute-done((f32[32,2432]{1,0:T(8,128)S(1)}, f32[32,2432]{1,0:T(8,128)S(1)}, u32[]{:S(2)}, u32[]{:S(2)}) %collective-permute-start.4) | collective-permute-done | bytes 311328 | tf_op jit(solution)/shard_map/ppermute | solution.py:35
  62.6 37.0 %collective-permute-done.6.refs_1_ = f32[128,2432]{1,0:T(8,128)S(1)} collective-permute-done((f32[128,2432]{1,0:T(8,128)S(1)}, f32[128,2432]{1,0:T(8,128)S(1)}, u32[]{:S(2)}, u32[]{:S(2)}) %collective-permute-start.6) | collective-permute-done | bytes 1245216 | tf_op jit(solution)/shard_map/ppermute | solution.py:35
  108.0 16.8 %collective-permute-done.8.refs_3_ = f32[64,2432]{1,0:T(8,128)S(1)} collective-permute-done((f32[64,2432]{1,0:T(8,128)}, f32[64,2432]{1,0:T(8,128)S(1)}, u32[]{:S(2)}, u32[]{:S(2)}) %collective-permute-start.8) | collective-permute-done | bytes 622624 | tf_op jit(solution)/shard_map/ppermute | solution.py:35
  124.8 6.8 %collective-permute-done.9.refs_4_ = f32[64,2432]{1,0:T(8,128)} collective-permute-done((f32[64,2432]{1,0:T(8,128)}, f32[64,2432]{1,0:T(8,128)}, u32[]{:S(2)}, u32[]{:S(2)}) %collective-permute-start.9) | collective-permute-done | bytes 622624 | tf_op jit(solution)/shard_map/ppermute | solution.py:35
  140.6 7.1 %place.1 = f32[1024,2432]{1,0:T(8,128)} custom-call(s32[32]{0:T(128)S(1)} %stack.164.where_ref, f32[128,2432]{1,0:T(8,128)S(1)} %pad_maximum_fusion.7.refs_0_, f32[128,2432]{1,0:T(8,128)S(1)} %collective-permute-done.6.refs_1_, f32[128,2432]{1,0:T(8,128)} %collective-permute-done.7.refs_2_, f32[64,2432]{1,0:T(8,128)S(1)} %collective-permute-done.8.refs_3_, ...), custom_call_target="tpu_custom_call" | custom-call | tf_op jit(solution)/shard_map/place/pallas_call | solution.py:99
  147.7 13.0 %fusion.90.proj_ref.edge_ref.halo_ref = f32[520,2432]{1,0:T(8,128)} fusion(f32[520,1024]{1,0:T(8,128)S(1)} %get-tuple-element.146, f32[1024,2432]{1,0:T(8,128)} %place.1), kind=kOutput, calls=%fused_computation.211 | convolution fusion | flops 7769948160 | bytes 17149952 | tf_op jit(solution)/shard_map/dot_general | solution.py:332
  162.5 11.6 %prepare.1 = (f32[512,2304]{1,0:T(8,128)}, f32[512,32]{1,0:T(8,128)S(1)}, f32[512,32]{1,0:T(8,128)S(1)}, f32[512,32]{1,0:T(8,128)S(1)}, f32[4,128,2048]{2,1,0:T(...) custom-call(f32[520,2432]{1,0:T(8,128)} %fusion.90.proj_ref.edge_ref.halo_ref, ...), custom_call_target="tpu_custom_call" | custom-call | tf_op jit(solution)/shard_map/prepare/pallas_call | solution.py:458
  179.1 10.6 %intra.1.inner_ref = f32[512,2048]{1,0:T(8,128)} custom-call(f32[512,2304]{1,0:T(8,128)} %get-tuple-element.117.act_ref, f32[512,32]{1,0:T(8,128)S(1)} %get-tuple-element.88.step_ref, f32[512,32]{1,0:T(8,128)S(1)} %get-tuple-element.84.logd_ref, f32[1,2048]{1,0:T(1,128)S(1)} %reshape_reshape.4.skip_ref, bf16[96,2048]{1,0:T(8,128)(2,1)S(1)} %fusion.30.spreader_ref), custom_call_target="tpu_custom_call" | custom-call | tf_op jit(solution)/shard_map/intra/pallas_call | solution.py:545
  194.2 5.1 fusion.92.gate_right_ref
  199.2 5.1 fusion.91.gate_left_ref
  210.8 5.0 slice.292
  215.9 8.8 %fusion.93.dng_ref = f32[512,2048]{1,0:T(8,128)} fusion(f32[512,1024]{1,0:T(8,128)S(1)} %maximum_multiply_fusion, f32[2048,1024]{1,0:T(8,128)S(1)} %bitcast.338), kind=kOutput, calls=%fused_computation.214 | convolution fusion | flops 6442450944 | bytes 14680064 | tf_op jit(solution)/shard_map/dot_general | solution.py:336
  224.6 28.7 %collective-permute-done.17 = f32[128,2048]{1,0:T(8,128)S(1)} collective-permute-done((f32[128,2048]{1,0:T(8,128)S(1)}, f32[128,2048]{1,0:T(8,128)S(1)}, u32[]{:S(2)}, u32[]{:S(2)}) %collective-permute-start.17) | collective-permute-done | bytes 1048608 | tf_op jit(solution)/shard_map/ppermute | solution.py:302
  253.5 17.0 %mixer.1 = (f32[512,2048]{1,0:T(8,128)}, f32[512,2048]{1,0:T(8,128)}, f32[512,2048]{1,0:T(8,128)}, f32[4,128,2048]{2,1,0:T(8,128)}, f32[8,2048]{1,0:T(8,128)S(1)}, /*index=5*/f32[8,2048]{1,0:T(8,128)S(1)}) custom-call(f32[512,2304]{1,0:T(8,128)} %get-tuple-element.117.act_ref, f32[512,32]{1,0:T(8,128)S(1)} %get-tuple-element.84.logd_ref, ...), custom_call_target="tpu_custom_call" | custom-call | tf_op jit(solution)/shard_map/mixer/pallas_call | solution.py:638
  275.2 5.1 fusion.94
  292.4 12.9 %right.1 = f32[512,1024]{1,0:T(8,128)} custom-call(f32[512,2048]{1,0:T(8,128)} %get-tuple-element.100.x_ref, f32[2048,1024]{1,0:T(8,128)} %bitcast.339, f32[512,1024]{1,0:T(8,128)} %pad_maximum_fusion.2.added_ref, f32[512,1]{1,0:T(8,128)S(1)} %fusion.68.scale_ref), custom_call_target="tpu_custom_call" | custom-call | tf_op jit(solution)/shard_map/right/pallas_call | solution.py:990
  319.1 5.4 fusion.13
  330.1 5.4 fusion.17
  335.5 18.2 %back_intra.1 = (f32[512,2048]{1,0:T(8,128)}, f32[512,256]{1,0:T(8,128)S(1)}, f32[512,32]{1,0:T(8,128)S(1)}) custom-call(f32[512,2304]{1,0:T(8,128)} %get-tuple-element.117.act_ref, f32[512,32]{1,0:T(8,128)S(1)} %get-tuple-element.88.step_ref, f32[512,32]{1,0:T(8,128)S(1)} %get-tuple-element.84.logd_ref, f32[512,2048]{1,0:T(8,128)} %get-tuple-element.108.dy_ref, ...), custom_call_target="tpu_custom_call" | custom-call | tf_op jit(solution)/shard_map/back_intra/pallas_call | solution.py:747
  370.3 11.4 %right_back.1 = f32[512,1024]{1,0:T(8,128)} custom-call(f32[512,2048]{1,0:T(8,128)} %get-tuple-element.114.x_ref, f32[1024,1024]{1,0:T(8,128)} %bitcast.343, f32[1024,1024]{1,0:T(8,128)} %bitcast.341), custom_call_target="tpu_custom_call" | custom-call | tf_op jit(solution)/shard_map/right_back/pallas_call | solution.py:1015
  388.2 33.7 %back.1 = (f32[520,2432]{1,0:T(8,128)}, f32[32,2304]{1,0:T(8,128)S(1)}, f32[8,2304]{1,0:T(8,128)S(1)}, f32[8,32]{1,0:T(8,128)S(1)}, f32[8,32]{1,0:T(8,128)S(1)}) custom-call(f32[512,2304]{1,0:T(8,128)} %get-tuple-element.117.act_ref, f32[512,32]{1,0:T(8,128)S(1)} %get-tuple-element.88.step_ref, f32[512,32]{1,0:T(8,128)S(1)} %get-tuple-element.118.slope_ref, ...), custom_call_target="tpu_custom_call" | custom-call | tf_op jit(solution)/shard_map/back/pallas_call | solution.py:925
  430.1 10.1 %maximum_add_fusion = f32[512,2432]{1,0:T(8,128)} fusion(f32[256,2432]{1,0:T(8,128)S(1)} %get-tuple-element.186, f32[256,2432]{1,0:T(8,128)S(1)} %get-tuple-element.185, f32[520,2432]{1,0:T(8,128)} %get-tuple-element.133, f32[520,256]{1,0:T(8,128)S(1)} %get-tuple-element.175, f32[520,256]{1,0:T(8,128)S(1)} %copy-done.49), kind=kOutput, calls=%fused_computation.4 | convolution fusion | flops 3887730688 | bytes 16084992 | tf_op jit(solution)/shard_map/dot_general | solution.py:342
  440.5 7.6 %all-to-all-start.1 = ((f32[4,64,1024]{2,1,0:T(8,128)}), f32[4,64,1024]{2,1,0:T(8,128)}, u32[]{:S(2)}, u32[]{:S(2)}) async-start(f32[4,64,1024]{2,1,0:T(8,128)} %pad_maximum_fusion.8), calls=%async_computation.1 | async-start | bytes 2097152 | tf_op jit(solution)/shard_map/all_to_all | solution.py:230
  452.0 9.7 %maximum_add_fusion.1 = f32[512,2432]{1,0:T(8,128)S(1)} fusion(f32[256,2432]{1,0:T(8,128)} %get-tuple-element.188, f32[256,2432]{1,0:T(8,128)} %get-tuple-element.187, f32[520,2432]{1,0:T(8,128)} %get-tuple-element.133, f32[520,256]{1,0:T(8,128)S(1)} %copy-done.47, f32[520,256]{1,0:T(8,128)S(1)} %copy-done.45), kind=kOutput, calls=%fused_computation.5 | convolution fusion | flops 3887730688 | bytes 16084992 | tf_op jit(solution)/shard_map/dot_general | solution.py:342
  463.5 7.7 %all-to-all-done.1 = f32[4,64,1024]{2,1,0:T(8,128)} async-done(((f32[4,64,1024]{2,1,0:T(8,128)}), f32[4,64,1024]{2,1,0:T(8,128)}, u32[]{:S(2)}, u32[]{:S(2)}) %all-to-all-start.1) | async-done | bytes 1048608 | tf_op jit(solution)/shard_map/all_to_all | solution.py:230
  483.8 12.3 %fusion.95 = f32[520,1024]{1,0:T(8,128)} fusion(f32[520,2432]{1,0:T(8,128)S(1)} %bitcast.346, f32[1024,2432]{1,0:T(8,128)} %place.1), kind=kOutput, calls=%fused_computation.216 | convolution fusion | flops 7769948160 | bytes 17149952 | tf_op jit(solution)/shard_map/dot_general | solution.py:336
  500.2 7.6 %all-to-all-start = ((f32[4,32,2048]{2,1,0:T(8,128)}), f32[4,32,2048]{2,1,0:T(8,128)}, u32[]{:S(2)}, u32[]{:S(2)}) async-start(f32[4,32,2048]{2,1,0:T(8,128)} %pad_maximum_fusion.9), calls=%async_computation | async-start | bytes 2097152 | tf_op jit(solution)/shard_map/all_to_all | solution.py:230
  513.8 18.5 %collective-permute-done.32 = f32[8,1024]{1,0:T(8,128)S(1)} collective-permute-done((f32[8,1024]{1,0:T(8,128)S(1)}, f32[8,1024]{1,0:T(8,128)S(1)}, u32[]{:S(2)}, u32[]{:S(2)}) %collective-permute-start.32) | collective-permute-done | bytes 32800 | tf_op jit(solution)/shard_map/ppermute | solution.py:1168
  552.4 6.7 %collective-permute-done.42 = f32[2,32,2432]{2,1,0:T(8,128)S(1)} collective-permute-done((f32[2,32,2432]{2,1,0:T(8,128)S(1)}, f32[2,32,2432]{2,1,0:T(8,128)S(1)}, u32[]{:S(2)}, u32[]{:S(2)}) %collective-permute-start.42) | collective-permute-done | bytes 622624 | tf_op jit(solution)/shard_map/ppermute | solution.py:35
  566.5 18.0 %collective-permute-done.44 = f32[32,2432]{1,0:T(8,128)} collective-permute-done((f32[32,2432]{1,0:T(8,128)}, f32[32,2432]{1,0:T(8,128)}, u32[]{:S(2)}, u32[]{:S(2)}) %collective-permute-start.44) | collective-permute-done | bytes 311328 | tf_op jit(solution)/shard_map/ppermute | solution.py:35
  584.6 5.0 collective-permute-done.45
  (367 shorter events, 185.7 us)
Async XLA Ops:
  7.2 182.5 %all-gather.3.cloned.1.call-start = ((), (), s32[]{:S(2)}) async-start(), calls=%async_computation.2 | async-start | bytes 17301504 | tf_op jit(solution)/shard_map/all_gather | solution.py:1070
  11.9 42.8 %collective-permute-start = (f32[256,1024]{1,0:T(8,128)}, f32[256,1024]{1,0:T(8,128)}, u32[]{:S(2)}, u32[]{:S(2)}) collective-permute-start(f32[256,1024]{1,0:T(8,128)} %dynamic-slice_bitcast_fusion.3), channel_id=1, source_target_pairs={{0,1},{1,0},{2,3},{3,2},{4,5},{5,4},{6,7},{7,6},{8,9},{9,8},{10,11... | collective-permute-start | bytes 3145736 | tf_op jit(solution)/shard_map/ppermute | solution.py:35
  15.2 37.5 %collective-permute-start.4 = (f32[32,2432]{1,0:T(8,128)S(1)}, f32[32,2432]{1,0:T(8,128)S(1)}, u32[]{:S(2)}, u32[]{:S(2)}) collective-permute-start(f32[32,2432]{1,0:T(8,128)S(1)} %pad_maximum_fusion.12), channel_id=1, source_target_pairs={{0,4},{2,6},{4,0},{6,2},{1,5},{3,7},{5,1},{7,3},{8,12},{10,14},{12... | collective-permute-start | bytes 933896 | tf_op jit(solution)/shard_map/ppermute | solution.py:35
  16.4 38.1 %collective-permute-start.5 = (f32[32,2432]{1,0:T(8,128)S(1)}, f32[32,2432]{1,0:T(8,128)S(1)}, u32[]{:S(2)}, u32[]{:S(2)}) collective-permute-start(f32[32,2432]{1,0:T(8,128)S(1)} %pad_maximum_fusion.12), channel_id=1, source_target_pairs={{0,6},{2,0},{4,2},{6,4},{1,7},{3,1},{5,3},{7,5},{8,14},{10,8},{12,... | collective-permute-start | bytes 933896 | tf_op jit(solution)/shard_map/ppermute | solution.py:35
  54.6 45.0 %collective-permute-start.6 = (f32[128,2432]{1,0:T(8,128)S(1)}, f32[128,2432]{1,0:T(8,128)S(1)}, u32[]{:S(2)}, u32[]{:S(2)}) collective-permute-start(f32[128,2432]{1,0:T(8,128)S(1)} %pad_maximum_fusion.7.refs_0_), channel_id=1, source_target_pairs={{0,1},{1,0},{2,3},{3,2},{4,5},{5,4},{6,7},{7,6},{8,9},{9,8},{10,11... | collective-permute-start | bytes 3735560 | tf_op jit(solution)/shard_map/ppermute | solution.py:35
  55.2 46.8 %collective-permute-start.7 = (f32[128,2432]{1,0:T(8,128)S(1)}, f32[128,2432]{1,0:T(8,128)}, u32[]{:S(2)}, u32[]{:S(2)}) collective-permute-start(f32[128,2432]{1,0:T(8,128)S(1)} %pad_maximum_fusion.7.refs_0_), channel_id=1, source_target_pairs={{0,16},{16,0},{1,17},{17,1},{2,18},{18,2},{3,19},{19,3},{4,20},{20... | collective-permute-start | bytes 3735560 | tf_op jit(solution)/shard_map/ppermute | solution.py:35
  58.2 46.2 %collective-permute-start.1 = (f32[8,1024]{1,0:T(8,128)}, f32[8,1024]{1,0:T(8,128)}, u32[]{:S(2)}, u32[]{:S(2)}) collective-permute-start(f32[8,1024]{1,0:T(8,128)} %get-tuple-element.179), channel_id=1, source_target_pairs={{1,2},{3,4},{5,6},{9,10},{11,12},{13,14},{17,18},{19,20},{21,22},{... | collective-permute-start | bytes 98312 | tf_op jit(solution)/shard_map/ppermute | solution.py:269
  59.5 45.4 %collective-permute-start.2 = (f32[8,1024]{1,0:T(8,128)}, f32[8,1024]{1,0:T(8,128)}, u32[]{:S(2)}, u32[]{:S(2)}) collective-permute-start(f32[8,1024]{1,0:T(8,128)} %get-tuple-element.178), channel_id=1, source_target_pairs={{1,3},{3,5},{5,7},{9,11},{11,13},{13,15},{17,19},{19,21},{21,23},{... | collective-permute-start | bytes 98312 | tf_op jit(solution)/shard_map/ppermute | solution.py:269
  104.0 27.7 %collective-permute-start.9 = (f32[64,2432]{1,0:T(8,128)}, f32[64,2432]{1,0:T(8,128)}, u32[]{:S(2)}, u32[]{:S(2)}) collective-permute-start(f32[64,2432]{1,0:T(8,128)} %slice.283), channel_id=1, source_target_pairs={{0,1},{1,0},{2,3},{3,2},{4,5},{5,4},{6,7},{7,6},{8,9},{9,8},{10,11... | collective-permute-start | bytes 1867784 | tf_op jit(solution)/shard_map/ppermute | solution.py:35
  104.2 33.9 %collective-permute-start.10 = (f32[128,2432]{1,0:T(8,128)S(1)}, f32[128,2432]{1,0:T(8,128)S(1)}, u32[]{:S(2)}, u32[]{:S(2)}) collective-permute-start(f32[128,2432]{1,0:T(8,128)S(1)} %pad_maximum_fusion.7.refs_0_), channel_id=1, source_target_pairs={{0,8},{8,0},{1,9},{9,1},{2,10},{10,2},{3,11},{11,3},{4,12},{12,4},... | collective-permute-start | bytes 3735560 | tf_op jit(solution)/shard_map/ppermute | solution.py:35
  104.3 33.8 %collective-permute-start.11 = (f32[128,2432]{1,0:T(8,128)S(1)}, f32[128,2432]{1,0:T(8,128)S(1)}, u32[]{:S(2)}, u32[]{:S(2)}) collective-permute-start(f32[128,2432]{1,0:T(8,128)S(1)} %collective-permute-done.6.refs_1_), channel_id=1, source_target_pairs={{0,8},{8,0},{1,9},{9,1},{2,10},{10,2},{3,11},{11,3},{4,12},{12,4},... | collective-permute-start | bytes 3735560 | tf_op jit(solution)/shard_map/ppermute | solution.py:35
  104.8 33.4 %collective-permute-start.12 = (f32[128,2432]{1,0:T(8,128)}, f32[128,2432]{1,0:T(8,128)S(1)}, u32[]{:S(2)}, u32[]{:S(2)}) collective-permute-start(f32[128,2432]{1,0:T(8,128)} %collective-permute-done.7.refs_2_), channel_id=1, source_target_pairs={{0,8},{8,0},{1,9},{9,1},{2,10},{10,2},{3,11},{11,3},{4,12},{12,4},... | collective-permute-start | bytes 3735560 | tf_op jit(solution)/shard_map/ppermute | solution.py:35
  138.1 51.5 %collective-permute-start.15 = (f32[256,1024]{1,0:T(8,128)}, f32[256,1024]{1,0:T(8,128)}, u32[]{:S(2)}, u32[]{:S(2)}) collective-permute-start(f32[256,1024]{1,0:T(8,128)} %dynamic-slice_bitcast_fusion.2), channel_id=1, source_target_pairs={{0,1},{1,0},{2,3},{3,2},{4,5},{5,4},{6,7},{7,6},{8,9},{9,8},{10,11... | collective-permute-start | bytes 3145736 | tf_op jit(solution)/shard_map/ppermute | solution.py:35
  176.9 28.6 %collective-permute-start.16 = (f32[136,2048]{1,0:T(8,128)}, f32[136,2048]{1,0:T(8,128)S(1)}, u32[]{:S(2)}, u32[]{:S(2)}) collective-permute-start(f32[136,2048]{1,0:T(8,128)} %pad_maximum_fusion.6), channel_id=1, source_target_pairs={{0,2},{2,4},{4,6},{1,3},{3,5},{5,7},{8,10},{10,12},{12,14},{9,11},... | collective-permute-start | bytes 3342344 | tf_op jit(solution)/shard_map/ppermute | solution.py:302
  207.4 46.0 %collective-permute-start.17 = (f32[128,2048]{1,0:T(8,128)S(1)}, f32[128,2048]{1,0:T(8,128)S(1)}, u32[]{:S(2)}, u32[]{:S(2)}) collective-permute-start(f32[128,2048]{1,0:T(8,128)S(1)} %multiply_add_fusion.4), channel_id=1, source_target_pairs={{0,4},{2,6},{1,5},{3,7},{8,12},{10,14},{9,13},{11,15},{16,20},{18,... | collective-permute-start | bytes 3145736 | tf_op jit(solution)/shard_map/ppermute | solution.py:302
  280.3 31.8 %collective-permute-start.19 = (f32[1024,1024]{1,0:T(8,128)}, f32[1024,1024]{1,0:T(8,128)}, u32[]{:S(2)}, u32[]{:S(2)}) collective-permute-start(f32[1024,1024]{1,0:T(8,128)} %fusion.94), channel_id=1, source_target_pairs={{0,8},{8,0},{1,9},{9,1},{2,10},{10,2},{3,11},{11,3},{4,12},{12,4},... | collective-permute-start | bytes 12582920 | tf_op jit(solution)/shard_map/ppermute | solution.py:35
  280.3 29.2 %collective-permute-start.18 = (f32[136,2048]{1,0:T(8,128)}, f32[136,2048]{1,0:T(8,128)}, u32[]{:S(2)}, u32[]{:S(2)}) collective-permute-start(f32[136,2048]{1,0:T(8,128)} %pad_maximum_fusion.5), channel_id=1, source_target_pairs={{2,0},{4,2},{6,4},{3,1},{5,3},{7,5},{10,8},{12,10},{14,12},{11,9},... | collective-permute-start | bytes 3342344 | tf_op jit(solution)/shard_map/ppermute | solution.py:302
  324.5 38.3 %collective-permute-start.22 = (f32[512,2048]{1,0:T(8,128)}, f32[512,2048]{1,0:T(8,128)}, u32[]{:S(2)}, u32[]{:S(2)}) collective-permute-start(f32[512,2048]{1,0:T(8,128)} %fusion.13), channel_id=1, source_target_pairs={{0,8},{8,0},{1,9},{9,1},{2,10},{10,2},{3,11},{11,3},{4,12},{12,4},... | collective-permute-start | bytes 12582920 | tf_op jit(solution)/shard_map/ppermute | solution.py:35
  324.5 30.0 %collective-permute-start.21 = (f32[2,2,64,1024]{3,2,0,1:T(8,128)}, f32[2,2,64,1024]{3,2,0,1:T(8,128)}, u32[]{:S(2)}, u32[]{:S(2)}) collective-permute-start(f32[2,2,64,1024]{3,2,0,1:T(8,128)} %fusion.24), channel_id=1, source_target_pairs={{0,16},{16,0},{1,17},{17,1},{2,18},{18,2},{3,19},{19,3},{4,20},{20... | collective-permute-start | bytes 3145736 | tf_op jit(solution)/shard_map/ppermute | solution.py:35
  324.5 30.1 %collective-permute-start.20 = (f32[2,2,64,1024]{3,2,1,0:T(8,128)}, f32[2,2,64,1024]{3,2,1,0:T(8,128)}, u32[]{:S(2)}, u32[]{:S(2)}) collective-permute-start(f32[2,2,64,1024]{3,2,1,0:T(8,128)} %fusion.22), channel_id=1, source_target_pairs={{0,1},{1,0},{2,3},{3,2},{4,5},{5,4},{6,7},{7,6},{8,9},{9,8},{10,11... | collective-permute-start | bytes 3145736 | tf_op jit(solution)/shard_map/ppermute | solution.py:35
  327.7 53.9 %collective-permute-start.25 = (f32[128,2048]{1,0:T(8,128)}, f32[128,2048]{1,0:T(8,128)}, u32[]{:S(2)}, u32[]{:S(2)}) collective-permute-start(f32[128,2048]{1,0:T(8,128)} %multiply_add_fusion.2), channel_id=1, source_target_pairs={{4,0},{6,2},{5,1},{7,3},{12,8},{14,10},{13,9},{15,11},{20,16},{22,... | collective-permute-start | bytes 3145736 | tf_op jit(solution)/shard_map/ppermute | solution.py:302
  367.1 58.4 %collective-permute-start.28 = (f32[2,2,32,2048]{3,2,0,1:T(8,128)}, f32[2,2,32,2048]{3,2,0,1:T(8,128)}, u32[]{:S(2)}, u32[]{:S(2)}) collective-permute-start(f32[2,2,32,2048]{3,2,0,1:T(8,128)} %fusion.23), channel_id=1, source_target_pairs={{0,16},{16,0},{1,17},{17,1},{2,18},{18,2},{3,19},{19,3},{4,20},{20... | collective-permute-start | bytes 3145736 | tf_op jit(solution)/shard_map/ppermute | solution.py:35
  369.6 58.2 %collective-permute-start.27 = (f32[2,2,32,2048]{3,2,1,0:T(8,128)}, f32[2,2,32,2048]{3,2,1,0:T(8,128)}, u32[]{:S(2)}, u32[]{:S(2)}) collective-permute-start(f32[2,2,32,2048]{3,2,1,0:T(8,128)} %fusion.21), channel_id=1, source_target_pairs={{0,1},{1,0},{2,3},{3,2},{4,5},{5,4},{6,7},{7,6},{8,9},{9,8},{10,11... | collective-permute-start | bytes 3145736 | tf_op jit(solution)/shard_map/ppermute | solution.py:35
  440.2 32.9 %collective-permute-start.29 = (f32[512,2432]{1,0:T(8,128)}, f32[512,2432]{1,0:T(8,128)}, u32[]{:S(2)}, u32[]{:S(2)}) collective-permute-start(f32[512,2432]{1,0:T(8,128)} %maximum_add_fusion), channel_id=1, source_target_pairs={{0,8},{8,0},{1,9},{9,1},{2,10},{10,2},{3,11},{11,3},{4,12},{12,4},... | collective-permute-start | bytes 14942216 | tf_op jit(solution)/shard_map/ppermute | solution.py:35
  440.5 30.7 %all-to-all-start.1 = ((f32[4,64,1024]{2,1,0:T(8,128)}), f32[4,64,1024]{2,1,0:T(8,128)}, u32[]{:S(2)}, u32[]{:S(2)}) async-start(f32[4,64,1024]{2,1,0:T(8,128)} %pad_maximum_fusion.8), calls=%async_computation.1 | async-start | bytes 2097152 | tf_op jit(solution)/shard_map/all_to_all | solution.py:230
  449.2 61.5 %collective-permute-start.26 = (f32[256,1024]{1,0:T(8,128)}, f32[256,1024]{1,0:T(8,128)}, u32[]{:S(2)}, u32[]{:S(2)}) collective-permute-start(f32[256,1024]{1,0:T(8,128)} %dynamic-slice_bitcast_fusion.1), channel_id=1, source_target_pairs={{0,1},{1,0},{2,3},{3,2},{4,5},{5,4},{6,7},{7,6},{8,9},{9,8},{10,11... | collective-permute-start | bytes 3145736 | tf_op jit(solution)/shard_map/ppermute | solution.py:35
  450.6 45.5 %collective-permute-start.30 = (f32[2,32,2048]{2,1,0:T(8,128)}, f32[2,32,2048]{2,1,0:T(8,128)}, u32[]{:S(2)}, u32[]{:S(2)}) collective-permute-start(f32[2,32,2048]{2,1,0:T(8,128)} %fusion.45), channel_id=1, source_target_pairs={{0,16},{16,0},{1,17},{17,1},{2,18},{18,2},{3,19},{19,3},{4,20},{20... | collective-permute-start | bytes 1572872 | tf_op jit(solution)/shard_map/ppermute | solution.py:35
  451.3 44.8 %collective-permute-start.31 = (f32[2,32,2048]{2,1,0:T(8,128)}, f32[2,32,2048]{2,1,0:T(8,128)S(1)}, u32[]{:S(2)}, u32[]{:S(2)}) collective-permute-start(f32[2,32,2048]{2,1,0:T(8,128)} %fusion.43), channel_id=1, source_target_pairs={{0,1},{1,0},{2,3},{3,2},{4,5},{5,4},{6,7},{7,6},{8,9},{9,8},{10,11... | collective-permute-start | bytes 1572872 | tf_op jit(solution)/shard_map/ppermute | solution.py:35
  477.2 57.2 %collective-permute-start.34 = (f32[2,2,32,2432]{3,2,0,1:T(8,128)}, f32[2,2,32,2432]{3,2,0,1:T(8,128)}, u32[]{:S(2)}, u32[]{:S(2)}) collective-permute-start(f32[2,2,32,2432]{3,2,0,1:T(8,128)} %fusion.6), channel_id=1, source_target_pairs={{0,16},{16,0},{1,17},{17,1},{2,18},{18,2},{3,19},{19,3},{4,20},{20... | collective-permute-start | bytes 3735560 | tf_op jit(solution)/shard_map/ppermute | solution.py:35
  482.4 52.0 %collective-permute-start.33 = (f32[2,2,32,2432]{3,2,1,0:T(8,128)}, f32[2,2,32,2432]{3,2,1,0:T(8,128)}, u32[]{:S(2)}, u32[]{:S(2)}) collective-permute-start(f32[2,2,32,2432]{3,2,1,0:T(8,128)} %fusion.5), channel_id=1, source_target_pairs={{0,1},{1,0},{2,3},{3,2},{4,5},{5,4},{6,7},{7,6},{8,9},{9,8},{10,11... | collective-permute-start | bytes 3735560 | tf_op jit(solution)/shard_map/ppermute | solution.py:35
  500.2 65.0 %all-to-all-start = ((f32[4,32,2048]{2,1,0:T(8,128)}), f32[4,32,2048]{2,1,0:T(8,128)}, u32[]{:S(2)}, u32[]{:S(2)}) async-start(f32[4,32,2048]{2,1,0:T(8,128)} %pad_maximum_fusion.9), calls=%async_computation | async-start | bytes 2097152 | tf_op jit(solution)/shard_map/all_to_all | solution.py:230
  548.9 44.6 %collective-permute-start.35 = (f32[256,1024]{1,0:T(8,128)}, f32[256,1024]{1,0:T(8,128)}, u32[]{:S(2)}, u32[]{:S(2)}) collective-permute-start(f32[256,1024]{1,0:T(8,128)} %dynamic-slice_bitcast_fusion), channel_id=1, source_target_pairs={{0,1},{1,0},{2,3},{3,2},{4,5},{5,4},{6,7},{7,6},{8,9},{9,8},{10,11... | collective-permute-start | bytes 3145736 | tf_op jit(solution)/shard_map/ppermute | solution.py:35
  (90 other events, 1404.2 us)
Sparse Core Ops, SparseCore 0:
  11.6 164.8 all-gather.2

commit v4 on v3

--- a/solution.py
+++ b/solution.py
@@ -21,7 +21,7 @@
 SPARE = 128 - HEADS
 WIDE = RATED + SPARE
 STRIP = 128
-BLOCK = 512
+BLOCK = 1024
 F32 = jnp.float32
 BF16 = jnp.bfloat16
 HIGH = lax.Precision.HIGH
@@ -227,7 +227,10 @@
     def last_at_once(self):
         line = jnp.concatenate([functools.reduce(jnp.add, v) for v, _ in self.parts], axis=0)
         self.sends = [line]
-        line = lax.all_to_all(line, "zc", 0, 0)
+        self.line = lax.all_to_all(line, "zc", 0, 0)
+
+    def settle(self, *others):
+        (line,) = tied([self.line], *others) if others else [self.line]
         self.came, self.kept = ([line[k] for k in range(1, line.shape[0])], line[0])
 
     def result(self):
@@ -735,7 +738,7 @@
     moved_ref[...] = sum_rows[...].T - sum_columns[:, 0:HEADS]
 
 
-BACK_UNROLL = 4
+BACK_UNROLL = 8
 
 
 def back_intra(act, step, logd, dy, spreader):
@@ -1121,6 +1124,7 @@
     second = tn(ng_keep, turn)
     grad_wout = Scatter(first, second)
     branch = right(tied([ng], second)[0], w_out, hidden, valid)
+    traded = Exchange(halves(branch), mine)
     grads.go_on(branch)
     grad_wout.keep(branch)
     grad_wout.stage(("p", "y"))
@@ -1134,7 +1138,7 @@
     grad_wgate.keep(back_parts[1])
     grad_wout.stage(("y", "p"))
     grad_wgate.stage(("p", "y"))
-    (turn,) = tied([dz], back_parts[1], *grad_wout.sends, *grad_wgate.sends)
+    (turn,) = tied([dz], back_parts[1], *grad_wout.sends, *grad_wgate.sends, traded.other)
     dgate_normed = right_back(turn, w_gates)
     grad_wout.keep(dgate_normed)
     grad_wout.last_at_once()
@@ -1149,21 +1153,21 @@
     dsmall = jnp.pad(dsmall, ((0, 0), (0, SPARE * own_rows - small.shape[0])))
     dsmall = jnp.pad(dsmall.reshape(width, SPARE), ((0, 0), (RATED, 0)))
     small_keep, small_send = (core_rows(dsmall, k) for k in (0, 1))
+    grad_wout.settle()
     grad_wgate.keep(ddtb)
     grad_wgate.stage(("y", "p"))
-    (turn,) = tied([dproj], *grad_wgate.sends)
+    (turn,) = tied([dproj], *grad_wgate.sends, grad_wout.line)
     first = tn(in_send, turn) + small_send
     (turn,) = tied([dproj], first)
     second = tn(in_keep, turn) + small_keep
     grad_wconv = Scatter(first, second)
     grad_wconv.keep(second)
     grad_wconv.stage(("p", "y"))
-    traded = Exchange(halves(tied([branch], ddtb)[0]), mine)
-    dnormed = nt(tied([dproj], second, *grad_wconv.sends)[0], w_conv)
-    grad_wgate.keep(dnormed)
+    grad_wgate.keep(second, *grad_wconv.sends)
     grad_wgate.last_at_once()
+    dnormed = nt(tied([dproj], second, *grad_wconv.sends, *grad_wgate.sends)[0], w_conv)
+    grad_wgate.settle(dnormed)
     near = grad_wconv.came
-    (dnormed,) = tied([dnormed], *grad_wgate.sends)
     output = traded.result(jnp.stack, dnormed)
     returned = lax.ppermute(dnormed[rows:], "zc", [(i + 1, i) for i in range(count - 1)])
     dnormed = dnormed[:rows] + dgate_normed

time: 614 us -> 594 us (0.967)
  waiting for transfers between devices: 188 us -> 171 us
    ppermute x1, waiting for transfers between devices: 18.5 us -> 6.79 us  [per_device(): lax.ppermute(dnormed[rows:], 'zc', [(i + 1, i) for i in range(count - 1)])]
    all_to_all x2, waiting for transfers between devices: 7.68 us -> 0.01 us  [last_at_once(): self.line = lax.all_to_all(line, 'zc', 0, 0)]
    unnamed x141 -> x135, local copies, waits for them, and re-layouts: 16.2 us -> 12.8 us
  transfers between devices with their start and end apart: 50 -> 50, of which waited for: 17 -> 18; matrix products, arithmetic and copies ran while one was open for 27% -> 28% of each run, Pallas kernels for 17% -> 18%
where the time goes in v4:
time: 594 us; the launch traced here: 584 us
  waiting for transfers between devices  171 us (29%)
  Pallas kernels  119 us (20%)
  matrix products  84.5 us (14%)
  other arithmetic  69.4 us (12%)
  local copies, waits for them, and re-layouts  66.6 us (11%)
  starting transfers between devices  57.6 us (10%)
  between operations  15.6 us (3%)
    ppermute x40, waiting for transfers between devices, shift(): lax.ppermute(block, axis, [(i, (i + step) % count) for i in range(count)])  131 us
    dot_general x6, matrix products, tn(): lax.dot_general(a, b, (((0,), (0,)), ((), ())), precision=precision, pref...  40.3 us
    ppermute x40, starting transfers between devices, shift(): lax.ppermute(block, axis, [(i, (i + step) % count) for i in range(count)])  34.7 us
    ppermute x4, waiting for transfers between devices, send(): self.came.append(lax.ppermute(block, 'zc', route))  33.2 us
    pallas_call x1, Pallas kernels, back(): pl.pallas_call(back_kernel, grid=(cuts,), in_specs=[at(MIXED), at(HEADS),...  31.2 us
    dot_general x3, matrix products, nn(): return jnp.dot(a, b, precision=precision, preferred_element_type=F32)  23.2 us
    dot_general x2, matrix products, nt(): lax.dot_general(a, b, (((1,), (1,)), ((), ())), precision=precision, pref...  21 us
    add x12, other arithmetic, indexed(): total = part if total is None else total + part  20.1 us
  transfers between devices with their start and end apart: 50, of which 18 were waited for; matrix products, arithmetic and copies ran while one was open for 28% of the time, Pallas kernels for 18%

profile of v4, /device:TPU:8, one launch (start us, length us, event | category | flops | bytes accessed | tf_op | source)
XLA Modules:
  0.0 584.1 jit_solution(5445743470091233704)
XLA Ops:
  18.2 16.9 %collective-permute-done.3 = f32[32,2432]{1,0:T(8,128)S(1)} collective-permute-done((f32[32,2432]{1,0:T(8,128)S(1)}, f32[32,2432]{1,0:T(8,128)S(1)}, u32[]{:S(2)}, u32[]{:S(2)}) %collective-permute-start.3) | collective-permute-done | bytes 311328 | tf_op jit(solution)/shard_map/ppermute | solution.py:35
  35.2 17.6 %collective-permute-done.4 = f32[32,2432]{1,0:T(8,128)S(1)} collective-permute-done((f32[32,2432]{1,0:T(8,128)S(1)}, f32[32,2432]{1,0:T(8,128)S(1)}, u32[]{:S(2)}, u32[]{:S(2)}) %collective-permute-start.4) | collective-permute-done | bytes 311328 | tf_op jit(solution)/shard_map/ppermute | solution.py:35
  62.8 36.8 %collective-permute-done.6.refs_1_ = f32[128,2432]{1,0:T(8,128)S(1)} collective-permute-done((f32[128,2432]{1,0:T(8,128)S(1)}, f32[128,2432]{1,0:T(8,128)S(1)}, u32[]{:S(2)}, u32[]{:S(2)}) %collective-permute-start.6) | collective-permute-done | bytes 1245216 | tf_op jit(solution)/shard_map/ppermute | solution.py:35
  108.0 16.8 %collective-permute-done.8.refs_3_ = f32[64,2432]{1,0:T(8,128)S(1)} collective-permute-done((f32[64,2432]{1,0:T(8,128)}, f32[64,2432]{1,0:T(8,128)S(1)}, u32[]{:S(2)}, u32[]{:S(2)}) %collective-permute-start.8) | collective-permute-done | bytes 622624 | tf_op jit(solution)/shard_map/ppermute | solution.py:35
  124.8 6.8 %collective-permute-done.9.refs_4_ = f32[64,2432]{1,0:T(8,128)} collective-permute-done((f32[64,2432]{1,0:T(8,128)}, f32[64,2432]{1,0:T(8,128)}, u32[]{:S(2)}, u32[]{:S(2)}) %collective-permute-start.9) | collective-permute-done | bytes 622624 | tf_op jit(solution)/shard_map/ppermute | solution.py:35
  140.6 7.1 %place.1 = f32[1024,2432]{1,0:T(8,128)} custom-call(s32[32]{0:T(128)S(1)} %stack.164.where_ref, f32[128,2432]{1,0:T(8,128)S(1)} %pad_maximum_fusion.7.refs_0_, f32[128,2432]{1,0:T(8,128)S(1)} %collective-permute-done.6.refs_1_, f32[128,2432]{1,0:T(8,128)} %collective-permute-done.7.refs_2_, f32[64,2432]{1,0:T(8,128)S(1)} %collective-permute-done.8.refs_3_, ...), custom_call_target="tpu_custom_call" | custom-call | tf_op jit(solution)/shard_map/place/pallas_call | solution.py:99
  147.7 13.0 %fusion.91.proj_ref.edge_ref.halo_ref = f32[520,2432]{1,0:T(8,128)} fusion(f32[520,1024]{1,0:T(8,128)S(1)} %get-tuple-element.144, f32[1024,2432]{1,0:T(8,128)} %place.1), kind=kOutput, calls=%fused_computation.209 | convolution fusion | flops 7769948160 | bytes 17149952 | tf_op jit(solution)/shard_map/dot_general | solution.py:335
  162.6 11.6 %prepare.1 = (f32[512,2304]{1,0:T(8,128)}, f32[512,32]{1,0:T(8,128)S(1)}, f32[512,32]{1,0:T(8,128)S(1)}, f32[512,32]{1,0:T(8,128)S(1)}, f32[4,128,2048]{2,1,0:T(...) custom-call(f32[520,2432]{1,0:T(8,128)} %fusion.91.proj_ref.edge_ref.halo_ref, ...), custom_call_target="tpu_custom_call" | custom-call | tf_op jit(solution)/shard_map/prepare/pallas_call | solution.py:461
  179.1 10.6 %intra.1.inner_ref = f32[512,2048]{1,0:T(8,128)} custom-call(f32[512,2304]{1,0:T(8,128)} %get-tuple-element.116.act_ref, f32[512,32]{1,0:T(8,128)S(1)} %get-tuple-element.87.step_ref, f32[512,32]{1,0:T(8,128)S(1)} %get-tuple-element.83.logd_ref, f32[1,2048]{1,0:T(1,128)S(1)} %reshape_reshape.4.skip_ref, bf16[96,2048]{1,0:T(8,128)(2,1)S(1)} %fusion.31.spreader_ref), custom_call_target="tpu_custom_call" | custom-call | tf_op jit(solution)/shard_map/intra/pallas_call | solution.py:548
  194.2 5.1 fusion.93.gate_right_ref
  199.3 5.1 fusion.92.gate_left_ref
  210.8 5.0 slice.292
  215.9 8.8 %fusion.94.dng_ref = f32[512,2048]{1,0:T(8,128)} fusion(f32[512,1024]{1,0:T(8,128)S(1)} %maximum_multiply_fusion, f32[2048,1024]{1,0:T(8,128)S(1)} %bitcast.338), kind=kOutput, calls=%fused_computation.212 | convolution fusion | flops 6442450944 | bytes 14680064 | tf_op jit(solution)/shard_map/dot_general | solution.py:339
  224.7 28.7 %collective-permute-done.17 = f32[128,2048]{1,0:T(8,128)S(1)} collective-permute-done((f32[128,2048]{1,0:T(8,128)S(1)}, f32[128,2048]{1,0:T(8,128)S(1)}, u32[]{:S(2)}, u32[]{:S(2)}) %collective-permute-start.17) | collective-permute-done | bytes 1048608 | tf_op jit(solution)/shard_map/ppermute | solution.py:305
  253.6 17.0 %mixer.1 = (f32[512,2048]{1,0:T(8,128)}, f32[512,2048]{1,0:T(8,128)}, f32[512,2048]{1,0:T(8,128)}, f32[4,128,2048]{2,1,0:T(8,128)}, f32[8,2048]{1,0:T(8,128)S(1)}, /*index=5*/f32[8,2048]{1,0:T(8,128)S(1)}) custom-call(f32[512,2304]{1,0:T(8,128)} %get-tuple-element.116.act_ref, f32[512,32]{1,0:T(8,128)S(1)} %get-tuple-element.83.logd_ref, ...), custom_call_target="tpu_custom_call" | custom-call | tf_op jit(solution)/shard_map/mixer/pallas_call | solution.py:641
  275.3 5.1 fusion.95
  292.8 12.9 %right.1 = f32[512,1024]{1,0:T(8,128)} custom-call(f32[512,2048]{1,0:T(8,128)} %get-tuple-element.99.x_ref, f32[2048,1024]{1,0:T(8,128)} %bitcast.339, f32[512,1024]{1,0:T(8,128)} %pad_maximum_fusion.2.added_ref, f32[512,1]{1,0:T(8,128)S(1)} %fusion.68.scale_ref), custom_call_target="tpu_custom_call" | custom-call | tf_op jit(solution)/shard_map/right/pallas_call | solution.py:993
  319.3 5.3 fusion.14
  333.9 5.4 fusion.18
  339.3 17.5 %back_intra.1 = (f32[512,2048]{1,0:T(8,128)}, f32[512,256]{1,0:T(8,128)S(1)}, f32[512,32]{1,0:T(8,128)S(1)}) custom-call(f32[512,2304]{1,0:T(8,128)} %get-tuple-element.116.act_ref, f32[512,32]{1,0:T(8,128)S(1)} %get-tuple-element.87.step_ref, f32[512,32]{1,0:T(8,128)S(1)} %get-tuple-element.83.logd_ref, f32[512,2048]{1,0:T(8,128)} %get-tuple-element.107.dy_ref, ...), custom_call_target="tpu_custom_call" | custom-call | tf_op jit(solution)/shard_map/back_intra/pallas_call | solution.py:750
  376.6 11.4 %right_back.1 = f32[512,1024]{1,0:T(8,128)} custom-call(f32[512,2048]{1,0:T(8,128)} %get-tuple-element.113.x_ref, f32[1024,1024]{1,0:T(8,128)} %bitcast.343, f32[1024,1024]{1,0:T(8,128)} %bitcast.341), custom_call_target="tpu_custom_call" | custom-call | tf_op jit(solution)/shard_map/right_back/pallas_call | solution.py:1018
  391.7 5.7 all-to-all-start
  400.0 31.2 %back.1 = (f32[520,2432]{1,0:T(8,128)}, f32[32,2304]{1,0:T(8,128)S(1)}, f32[8,2304]{1,0:T(8,128)S(1)}, f32[8,32]{1,0:T(8,128)S(1)}, f32[8,32]{1,0:T(8,128)S(1)}) custom-call(f32[512,2304]{1,0:T(8,128)} %get-tuple-element.116.act_ref, f32[512,32]{1,0:T(8,128)S(1)} %get-tuple-element.87.step_ref, f32[512,32]{1,0:T(8,128)S(1)} %get-tuple-element.117.slope_ref, ...), custom_call_target="tpu_custom_call" | custom-call | tf_op jit(solution)/shard_map/back/pallas_call | solution.py:928
  431.8 4.6 pad_dynamic-slice_fusion.3
  440.9 10.9 %maximum_add_fusion = f32[512,2432]{1,0:T(8,128)} fusion(f32[256,2432]{1,0:T(8,128)} %get-tuple-element.184, f32[256,2432]{1,0:T(8,128)} %get-tuple-element.183, f32[520,2432]{1,0:T(8,128)} %get-tuple-element.133, f32[520,256]{1,0:T(8,128)S(1)} %copy-done.44, f32[520,256]{1,0:T(8,128)} %copy-done.45), kind=kOutput, calls=%fused_computation.4 | convolution fusion | flops 3887730688 | bytes 16084992 | tf_op jit(solution)/shard_map/dot_general | solution.py:345
  457.6 9.9 %maximum_add_fusion.1 = f32[512,2432]{1,0:T(8,128)S(1)} fusion(f32[256,2432]{1,0:T(8,128)} %get-tuple-element.186, f32[256,2432]{1,0:T(8,128)} %get-tuple-element.185, f32[520,2432]{1,0:T(8,128)} %get-tuple-element.133, f32[520,256]{1,0:T(8,128)} %copy-done.42, f32[520,256]{1,0:T(8,128)S(1)} %copy-done.41), kind=kOutput, calls=%fused_computation.5 | convolution fusion | flops 3887730688 | bytes 16084992 | tf_op jit(solution)/shard_map/dot_general | solution.py:345
  467.9 4.6 fusion.84
  479.7 5.1 all-to-all-start.1
  485.6 12.2 %fusion.96 = f32[520,1024]{1,0:T(8,128)S(1)} fusion(f32[520,2432]{1,0:T(8,128)} %get-tuple-element.133, f32[1024,2432]{1,0:T(8,128)} %place.1), kind=kOutput, calls=%fused_computation.214 | convolution fusion | flops 7769948160 | bytes 17149952 | tf_op jit(solution)/shard_map/dot_general | solution.py:339
  503.0 6.8 %collective-permute-done.32 = f32[8,1024]{1,0:T(8,128)S(1)} collective-permute-done((f32[8,1024]{1,0:T(8,128)S(1)}, f32[8,1024]{1,0:T(8,128)S(1)}, u32[]{:S(2)}, u32[]{:S(2)}) %collective-permute-start.32) | collective-permute-done | bytes 32800 | tf_op jit(solution)/shard_map/ppermute | solution.py:1172
  547.9 17.0 %collective-permute-done.44 = f32[32,2432]{1,0:T(8,128)S(1)} collective-permute-done((f32[32,2432]{1,0:T(8,128)S(1)}, f32[32,2432]{1,0:T(8,128)S(1)}, u32[]{:S(2)}, u32[]{:S(2)}) %collective-permute-start.44) | collective-permute-done | bytes 311328 | tf_op jit(solution)/shard_map/ppermute | solution.py:35
  564.9 4.7 collective-permute-done.45
  (360 shorter events, 191.2 us)
Async XLA Ops:
  7.2 182.5 %all-gather.3.cloned.1.call-start = ((), (), s32[]{:S(2)}) async-start(), calls=%async_computation.2 | async-start | bytes 17301504 | tf_op jit(solution)/shard_map/all_gather | solution.py:1073
  11.9 42.8 %collective-permute-start = (f32[256,1024]{1,0:T(8,128)}, f32[256,1024]{1,0:T(8,128)}, u32[]{:S(2)}, u32[]{:S(2)}) collective-permute-start(f32[256,1024]{1,0:T(8,128)} %dynamic-slice_bitcast_fusion.3), channel_id=1, source_target_pairs={{0,1},{1,0},{2,3},{3,2},{4,5},{5,4},{6,7},{7,6},{8,9},{9,8},{10,11... | collective-permute-start | bytes 3145736 | tf_op jit(solution)/shard_map/ppermute | solution.py:35
  15.2 37.5 %collective-permute-start.4 = (f32[32,2432]{1,0:T(8,128)S(1)}, f32[32,2432]{1,0:T(8,128)S(1)}, u32[]{:S(2)}, u32[]{:S(2)}) collective-permute-start(f32[32,2432]{1,0:T(8,128)S(1)} %pad_maximum_fusion.12), channel_id=1, source_target_pairs={{0,4},{2,6},{4,0},{6,2},{1,5},{3,7},{5,1},{7,3},{8,12},{10,14},{12... | collective-permute-start | bytes 933896 | tf_op jit(solution)/shard_map/ppermute | solution.py:35
  16.4 38.1 %collective-permute-start.5 = (f32[32,2432]{1,0:T(8,128)S(1)}, f32[32,2432]{1,0:T(8,128)S(1)}, u32[]{:S(2)}, u32[]{:S(2)}) collective-permute-start(f32[32,2432]{1,0:T(8,128)S(1)} %pad_maximum_fusion.12), channel_id=1, source_target_pairs={{0,6},{2,0},{4,2},{6,4},{1,7},{3,1},{5,3},{7,5},{8,14},{10,8},{12,... | collective-permute-start | bytes 933896 | tf_op jit(solution)/shard_map/ppermute | solution.py:35
  54.6 45.0 %collective-permute-start.6 = (f32[128,2432]{1,0:T(8,128)S(1)}, f32[128,2432]{1,0:T(8,128)S(1)}, u32[]{:S(2)}, u32[]{:S(2)}) collective-permute-start(f32[128,2432]{1,0:T(8,128)S(1)} %pad_maximum_fusion.7.refs_0_), channel_id=1, source_target_pairs={{0,1},{1,0},{2,3},{3,2},{4,5},{5,4},{6,7},{7,6},{8,9},{9,8},{10,11... | collective-permute-start | bytes 3735560 | tf_op jit(solution)/shard_map/ppermute | solution.py:35
  55.2 46.8 %collective-permute-start.7 = (f32[128,2432]{1,0:T(8,128)S(1)}, f32[128,2432]{1,0:T(8,128)}, u32[]{:S(2)}, u32[]{:S(2)}) collective-permute-start(f32[128,2432]{1,0:T(8,128)S(1)} %pad_maximum_fusion.7.refs_0_), channel_id=1, source_target_pairs={{0,16},{16,0},{1,17},{17,1},{2,18},{18,2},{3,19},{19,3},{4,20},{20... | collective-permute-start | bytes 3735560 | tf_op jit(solution)/shard_map/ppermute | solution.py:35
  58.2 46.2 %collective-permute-start.1 = (f32[8,1024]{1,0:T(8,128)}, f32[8,1024]{1,0:T(8,128)}, u32[]{:S(2)}, u32[]{:S(2)}) collective-permute-start(f32[8,1024]{1,0:T(8,128)} %get-tuple-element.177), channel_id=1, source_target_pairs={{1,2},{3,4},{5,6},{9,10},{11,12},{13,14},{17,18},{19,20},{21,22},{... | collective-permute-start | bytes 98312 | tf_op jit(solution)/shard_map/ppermute | solution.py:272
  59.4 45.4 %collective-permute-start.2 = (f32[8,1024]{1,0:T(8,128)}, f32[8,1024]{1,0:T(8,128)}, u32[]{:S(2)}, u32[]{:S(2)}) collective-permute-start(f32[8,1024]{1,0:T(8,128)} %get-tuple-element.176), channel_id=1, source_target_pairs={{1,3},{3,5},{5,7},{9,11},{11,13},{13,15},{17,19},{19,21},{21,23},{... | collective-permute-start | bytes 98312 | tf_op jit(solution)/shard_map/ppermute | solution.py:272
  104.0 27.7 %collective-permute-start.9 = (f32[64,2432]{1,0:T(8,128)}, f32[64,2432]{1,0:T(8,128)}, u32[]{:S(2)}, u32[]{:S(2)}) collective-permute-start(f32[64,2432]{1,0:T(8,128)} %slice.283), channel_id=1, source_target_pairs={{0,1},{1,0},{2,3},{3,2},{4,5},{5,4},{6,7},{7,6},{8,9},{9,8},{10,11... | collective-permute-start | bytes 1867784 | tf_op jit(solution)/shard_map/ppermute | solution.py:35
  104.2 33.9 %collective-permute-start.10 = (f32[128,2432]{1,0:T(8,128)S(1)}, f32[128,2432]{1,0:T(8,128)S(1)}, u32[]{:S(2)}, u32[]{:S(2)}) collective-permute-start(f32[128,2432]{1,0:T(8,128)S(1)} %pad_maximum_fusion.7.refs_0_), channel_id=1, source_target_pairs={{0,8},{8,0},{1,9},{9,1},{2,10},{10,2},{3,11},{11,3},{4,12},{12,4},... | collective-permute-start | bytes 3735560 | tf_op jit(solution)/shard_map/ppermute | solution.py:35
  104.3 33.8 %collective-permute-start.11 = (f32[128,2432]{1,0:T(8,128)S(1)}, f32[128,2432]{1,0:T(8,128)S(1)}, u32[]{:S(2)}, u32[]{:S(2)}) collective-permute-start(f32[128,2432]{1,0:T(8,128)S(1)} %collective-permute-done.6.refs_1_), channel_id=1, source_target_pairs={{0,8},{8,0},{1,9},{9,1},{2,10},{10,2},{3,11},{11,3},{4,12},{12,4},... | collective-permute-start | bytes 3735560 | tf_op jit(solution)/shard_map/ppermute | solution.py:35
  104.8 33.3 %collective-permute-start.12 = (f32[128,2432]{1,0:T(8,128)}, f32[128,2432]{1,0:T(8,128)S(1)}, u32[]{:S(2)}, u32[]{:S(2)}) collective-permute-start(f32[128,2432]{1,0:T(8,128)} %collective-permute-done.7.refs_2_), channel_id=1, source_target_pairs={{0,8},{8,0},{1,9},{9,1},{2,10},{10,2},{3,11},{11,3},{4,12},{12,4},... | collective-permute-start | bytes 3735560 | tf_op jit(solution)/shard_map/ppermute | solution.py:35
  138.1 51.6 %collective-permute-start.15 = (f32[256,1024]{1,0:T(8,128)}, f32[256,1024]{1,0:T(8,128)}, u32[]{:S(2)}, u32[]{:S(2)}) collective-permute-start(f32[256,1024]{1,0:T(8,128)} %dynamic-slice_bitcast_fusion.2), channel_id=1, source_target_pairs={{0,1},{1,0},{2,3},{3,2},{4,5},{5,4},{6,7},{7,6},{8,9},{9,8},{10,11... | collective-permute-start | bytes 3145736 | tf_op jit(solution)/shard_map/ppermute | solution.py:35
  177.0 28.6 %collective-permute-start.16 = (f32[136,2048]{1,0:T(8,128)}, f32[136,2048]{1,0:T(8,128)S(1)}, u32[]{:S(2)}, u32[]{:S(2)}) collective-permute-start(f32[136,2048]{1,0:T(8,128)} %pad_maximum_fusion.6), channel_id=1, source_target_pairs={{0,2},{2,4},{4,6},{1,3},{3,5},{5,7},{8,10},{10,12},{12,14},{9,11},... | collective-permute-start | bytes 3342344 | tf_op jit(solution)/shard_map/ppermute | solution.py:305
  207.4 46.0 %collective-permute-start.17 = (f32[128,2048]{1,0:T(8,128)S(1)}, f32[128,2048]{1,0:T(8,128)S(1)}, u32[]{:S(2)}, u32[]{:S(2)}) collective-permute-start(f32[128,2048]{1,0:T(8,128)S(1)} %multiply_add_fusion.4), channel_id=1, source_target_pairs={{0,4},{2,6},{1,5},{3,7},{8,12},{10,14},{9,13},{11,15},{16,20},{18,... | collective-permute-start | bytes 3145736 | tf_op jit(solution)/shard_map/ppermute | solution.py:305
  280.4 31.8 %collective-permute-start.20 = (f32[1024,1024]{1,0:T(8,128)}, f32[1024,1024]{1,0:T(8,128)}, u32[]{:S(2)}, u32[]{:S(2)}) collective-permute-start(f32[1024,1024]{1,0:T(8,128)} %fusion.95), channel_id=1, source_target_pairs={{0,8},{8,0},{1,9},{9,1},{2,10},{10,2},{3,11},{11,3},{4,12},{12,4},... | collective-permute-start | bytes 12582920 | tf_op jit(solution)/shard_map/ppermute | solution.py:35
  280.4 29.2 %collective-permute-start.19 = (f32[136,2048]{1,0:T(8,128)}, f32[136,2048]{1,0:T(8,128)}, u32[]{:S(2)}, u32[]{:S(2)}) collective-permute-start(f32[136,2048]{1,0:T(8,128)} %pad_maximum_fusion.5), channel_id=1, source_target_pairs={{2,0},{4,2},{6,4},{3,1},{5,3},{7,5},{10,8},{12,10},{14,12},{11,9},... | collective-permute-start | bytes 3342344 | tf_op jit(solution)/shard_map/ppermute | solution.py:305
  324.6 40.8 %collective-permute-start.23 = (f32[512,2048]{1,0:T(8,128)}, f32[512,2048]{1,0:T(8,128)}, u32[]{:S(2)}, u32[]{:S(2)}) collective-permute-start(f32[512,2048]{1,0:T(8,128)} %fusion.14), channel_id=1, source_target_pairs={{0,8},{8,0},{1,9},{9,1},{2,10},{10,2},{3,11},{11,3},{4,12},{12,4},... | collective-permute-start | bytes 12582920 | tf_op jit(solution)/shard_map/ppermute | solution.py:35
  327.1 30.5 %collective-permute-start.22 = (f32[2,2,64,1024]{3,2,0,1:T(8,128)}, f32[2,2,64,1024]{3,2,0,1:T(8,128)S(1)}, u32[]{:S(2)}, u32[]{:S(2)}) collective-permute-start(f32[2,2,64,1024]{3,2,0,1:T(8,128)} %fusion.25), channel_id=1, source_target_pairs={{0,16},{16,0},{1,17},{17,1},{2,18},{18,2},{3,19},{19,3},{4,20},{20... | collective-permute-start | bytes 3145736 | tf_op jit(solution)/shard_map/ppermute | solution.py:35
  327.1 30.5 %collective-permute-start.21 = (f32[2,2,64,1024]{3,2,1,0:T(8,128)}, f32[2,2,64,1024]{3,2,1,0:T(8,128)S(1)}, u32[]{:S(2)}, u32[]{:S(2)}) collective-permute-start(f32[2,2,64,1024]{3,2,1,0:T(8,128)} %fusion.23), channel_id=1, source_target_pairs={{0,1},{1,0},{2,3},{3,2},{4,5},{5,4},{6,7},{7,6},{8,9},{9,8},{10,11... | collective-permute-start | bytes 3145736 | tf_op jit(solution)/shard_map/ppermute | solution.py:35
  330.2 45.6 %collective-permute-start.18 = (f32[256,1024]{1,0:T(8,128)}, f32[256,1024]{1,0:T(8,128)}, u32[]{:S(2)}, u32[]{:S(2)}) collective-permute-start(f32[256,1024]{1,0:T(8,128)} %dynamic-slice_bitcast_fusion.1), channel_id=1, source_target_pairs={{0,1},{1,0},{2,3},{3,2},{4,5},{5,4},{6,7},{7,6},{8,9},{9,8},{10,11... | collective-permute-start | bytes 3145736 | tf_op jit(solution)/shard_map/ppermute | solution.py:35
  331.5 65.9 %collective-permute-start.26 = (f32[128,2048]{1,0:T(8,128)}, f32[128,2048]{1,0:T(8,128)}, u32[]{:S(2)}, u32[]{:S(2)}) collective-permute-start(f32[128,2048]{1,0:T(8,128)} %multiply_add_fusion.2), channel_id=1, source_target_pairs={{4,0},{6,2},{5,1},{7,3},{12,8},{14,10},{13,9},{15,11},{20,16},{22,... | collective-permute-start | bytes 3145736 | tf_op jit(solution)/shard_map/ppermute | solution.py:305
  361.3 26.6 %collective-permute-start.24 = (f32[2,64,1024]{2,1,0:T(8,128)S(1)}, f32[2,64,1024]{2,1,0:T(8,128)S(1)}, u32[]{:S(2)}, u32[]{:S(2)}) collective-permute-start(f32[2,64,1024]{2,1,0:T(8,128)S(1)} %fusion.53), channel_id=1, source_target_pairs={{0,16},{16,0},{1,17},{17,1},{2,18},{18,2},{3,19},{19,3},{4,20},{20... | collective-permute-start | bytes 1572872 | tf_op jit(solution)/shard_map/ppermute | solution.py:35
  369.6 66.9 %collective-permute-start.28 = (f32[2,2,32,2048]{3,2,0,1:T(8,128)}, f32[2,2,32,2048]{3,2,0,1:T(8,128)}, u32[]{:S(2)}, u32[]{:S(2)}) collective-permute-start(f32[2,2,32,2048]{3,2,0,1:T(8,128)} %fusion.24), channel_id=1, source_target_pairs={{0,16},{16,0},{1,17},{17,1},{2,18},{18,2},{3,19},{19,3},{4,20},{20... | collective-permute-start | bytes 3145736 | tf_op jit(solution)/shard_map/ppermute | solution.py:35
  375.8 60.7 %collective-permute-start.27 = (f32[2,2,32,2048]{3,2,1,0:T(8,128)}, f32[2,2,32,2048]{3,2,1,0:T(8,128)}, u32[]{:S(2)}, u32[]{:S(2)}) collective-permute-start(f32[2,2,32,2048]{3,2,1,0:T(8,128)} %fusion.22), channel_id=1, source_target_pairs={{0,1},{1,0},{2,3},{3,2},{4,5},{5,4},{6,7},{7,6},{8,9},{9,8},{10,11... | collective-permute-start | bytes 3145736 | tf_op jit(solution)/shard_map/ppermute | solution.py:35
  391.7 49.2 %all-to-all-start = ((f32[4,64,1024]{2,1,0:T(8,128)}), f32[4,64,1024]{2,1,0:T(8,128)}, u32[]{:S(2)}, u32[]{:S(2)}) async-start(f32[4,64,1024]{2,1,0:T(8,128)} %pad_maximum_fusion.8), calls=%async_computation | async-start | bytes 2097152 | tf_op jit(solution)/shard_map/all_to_all | solution.py:230
  479.7 53.6 %all-to-all-start.1 = ((f32[4,32,2048]{2,1,0:T(8,128)}), f32[4,32,2048]{2,1,0:T(8,128)}, u32[]{:S(2)}, u32[]{:S(2)}) async-start(f32[4,32,2048]{2,1,0:T(8,128)} %pad_maximum_fusion.9), calls=%async_computation.1 | async-start | bytes 2097152 | tf_op jit(solution)/shard_map/all_to_all | solution.py:230
  484.8 28.9 %collective-permute-start.34 = (f32[2,2,32,2432]{3,2,0,1:T(8,128)}, f32[2,2,32,2432]{3,2,0,1:T(8,128)}, u32[]{:S(2)}, u32[]{:S(2)}) collective-permute-start(f32[2,2,32,2432]{3,2,0,1:T(8,128)} %fusion.7), channel_id=1, source_target_pairs={{0,16},{16,0},{1,17},{17,1},{2,18},{18,2},{3,19},{19,3},{4,20},{20... | collective-permute-start | bytes 3735560 | tf_op jit(solution)/shard_map/ppermute | solution.py:35
  484.9 28.9 %collective-permute-start.33 = (f32[2,2,32,2432]{3,2,1,0:T(8,128)}, f32[2,2,32,2432]{3,2,1,0:T(8,128)}, u32[]{:S(2)}, u32[]{:S(2)}) collective-permute-start(f32[2,2,32,2432]{3,2,1,0:T(8,128)} %fusion.6), channel_id=1, source_target_pairs={{0,1},{1,0},{2,3},{3,2},{4,5},{5,4},{6,7},{7,6},{8,9},{9,8},{10,11... | collective-permute-start | bytes 3735560 | tf_op jit(solution)/shard_map/ppermute | solution.py:35
  530.1 44.0 %collective-permute-start.35 = (f32[256,1024]{1,0:T(8,128)}, f32[256,1024]{1,0:T(8,128)}, u32[]{:S(2)}, u32[]{:S(2)}) collective-permute-start(f32[256,1024]{1,0:T(8,128)} %dynamic-slice_bitcast_fusion), channel_id=1, source_target_pairs={{0,1},{1,0},{2,3},{3,2},{4,5},{5,4},{6,7},{7,6},{8,9},{9,8},{10,11... | collective-permute-start | bytes 3145736 | tf_op jit(solution)/shard_map/ppermute | solution.py:35
  543.7 25.9 %collective-permute-start.45 = (f32[32,2432]{1,0:T(8,128)S(1)}, f32[32,2432]{1,0:T(8,128)S(1)}, u32[]{:S(2)}, u32[]{:S(2)}) collective-permute-start(f32[32,2432]{1,0:T(8,128)S(1)} %get-tuple-element.179), channel_id=1, source_target_pairs={{0,4},{2,6},{4,0},{6,2},{1,5},{3,7},{5,1},{7,3},{8,12},{10,14},{12... | collective-permute-start | bytes 933896 | tf_op jit(solution)/shard_map/ppermute | solution.py:35
  544.9 26.4 %collective-permute-start.46 = (f32[32,2432]{1,0:T(8,128)S(1)}, f32[32,2432]{1,0:T(8,128)S(1)}, u32[]{:S(2)}, u32[]{:S(2)}) collective-permute-start(f32[32,2432]{1,0:T(8,128)S(1)} %get-tuple-element.180), channel_id=1, source_target_pairs={{0,6},{2,0},{4,2},{6,4},{1,7},{3,1},{5,3},{7,5},{8,14},{10,8},{12,... | collective-permute-start | bytes 933896 | tf_op jit(solution)/shard_map/ppermute | solution.py:35
  (87 other events, 1378.4 us)
Sparse Core Ops, SparseCore 0:
  11.6 164.8 all-gather.2

commit v5 on v4

--- a/solution.py
+++ b/solution.py
@@ -509,7 +509,7 @@
     return jnp.concatenate([jnp.where(left, pair, zero), jnp.where(left, zero, pair)], axis=0)
 
 
-UNROLL = 8
+UNROLL = 16
 
 
 def intra_kernel(
@@ -738,7 +738,7 @@
     moved_ref[...] = sum_rows[...].T - sum_columns[:, 0:HEADS]
 
 
-BACK_UNROLL = 8
+BACK_UNROLL = 16
 
 
 def back_intra(act, step, logd, dy, spreader):

time: 594 us -> 594 us (level)
  transfers between devices with their start and end apart: 50 -> 50, of which waited for: 18 -> 19; matrix products, arithmetic and copies ran while one was open for 28% -> 28% of each run, Pallas kernels for 18% -> 17%
where the time goes in v5:
time: 594 us; the launch traced here: 584 us
  waiting for transfers between devices  173 us (29%)
  Pallas kernels  117 us (20%)
  matrix products  84.5 us (14%)
  other arithmetic  68.9 us (12%)
  local copies, waits for them, and re-layouts  66.6 us (11%)
  starting transfers between devices  59.1 us (10%)
  between operations  15.6 us (3%)
    ppermute x40, waiting for transfers between devices, shift(): lax.ppermute(block, axis, [(i, (i + step) % count) for i in range(count)])  134 us
    dot_general x6, matrix products, tn(): lax.dot_general(a, b, (((0,), (0,)), ((), ())), precision=precision, pref...  40.3 us
    ppermute x40, starting transfers between devices, shift(): lax.ppermute(block, axis, [(i, (i + step) % count) for i in range(count)])  36.1 us
    ppermute x4, waiting for transfers between devices, send(): self.came.append(lax.ppermute(block, 'zc', route))  32.6 us
    pallas_call x1, Pallas kernels, back(): pl.pallas_call(back_kernel, grid=(cuts,), in_specs=[at(MIXED), at(HEADS),...  31.2 us
    dot_general x3, matrix products, nn(): return jnp.dot(a, b, precision=precision, preferred_element_type=F32)  23.2 us
    dot_general x2, matrix products, nt(): lax.dot_general(a, b, (((1,), (1,)), ((), ())), precision=precision, pref...  21 us
    add x12, other arithmetic, indexed(): total = part if total is None else total + part  19.6 us
  transfers between devices with their start and end apart: 50, of which 19 were waited for; matrix products, arithmetic and copies ran while one was open for 28% of the time, Pallas kernels for 17%

profile of v5, /device:TPU:8, one launch (start us, length us, event | category | flops | bytes accessed | tf_op | source)
XLA Modules:
  0.0 584.5 jit_solution(14225236139130059712)
XLA Ops:
  18.2 16.9 %collective-permute-done.3 = f32[32,2432]{1,0:T(8,128)S(1)} collective-permute-done((f32[32,2432]{1,0:T(8,128)S(1)}, f32[32,2432]{1,0:T(8,128)S(1)}, u32[]{:S(2)}, u32[]{:S(2)}) %collective-permute-start.3) | collective-permute-done | bytes 311328 | tf_op jit(solution)/shard_map/ppermute | solution.py:35
  35.2 17.6 %collective-permute-done.4 = f32[32,2432]{1,0:T(8,128)S(1)} collective-permute-done((f32[32,2432]{1,0:T(8,128)S(1)}, f32[32,2432]{1,0:T(8,128)S(1)}, u32[]{:S(2)}, u32[]{:S(2)}) %collective-permute-start.4) | collective-permute-done | bytes 311328 | tf_op jit(solution)/shard_map/ppermute | solution.py:35
  62.8 36.8 %collective-permute-done.6.refs_1_ = f32[128,2432]{1,0:T(8,128)S(1)} collective-permute-done((f32[128,2432]{1,0:T(8,128)S(1)}, f32[128,2432]{1,0:T(8,128)S(1)}, u32[]{:S(2)}, u32[]{:S(2)}) %collective-permute-start.6) | collective-permute-done | bytes 1245216 | tf_op jit(solution)/shard_map/ppermute | solution.py:35
  108.0 16.8 %collective-permute-done.8.refs_3_ = f32[64,2432]{1,0:T(8,128)S(1)} collective-permute-done((f32[64,2432]{1,0:T(8,128)}, f32[64,2432]{1,0:T(8,128)S(1)}, u32[]{:S(2)}, u32[]{:S(2)}) %collective-permute-start.8) | collective-permute-done | bytes 622624 | tf_op jit(solution)/shard_map/ppermute | solution.py:35
  124.8 6.8 %collective-permute-done.9.refs_4_ = f32[64,2432]{1,0:T(8,128)} collective-permute-done((f32[64,2432]{1,0:T(8,128)}, f32[64,2432]{1,0:T(8,128)}, u32[]{:S(2)}, u32[]{:S(2)}) %collective-permute-start.9) | collective-permute-done | bytes 622624 | tf_op jit(solution)/shard_map/ppermute | solution.py:35
  140.6 7.1 %place.1 = f32[1024,2432]{1,0:T(8,128)} custom-call(s32[32]{0:T(128)S(1)} %stack.164.where_ref, f32[128,2432]{1,0:T(8,128)S(1)} %pad_maximum_fusion.7.refs_0_, f32[128,2432]{1,0:T(8,128)S(1)} %collective-permute-done.6.refs_1_, f32[128,2432]{1,0:T(8,128)} %collective-permute-done.7.refs_2_, f32[64,2432]{1,0:T(8,128)S(1)} %collective-permute-done.8.refs_3_, ...), custom_call_target="tpu_custom_call" | custom-call | tf_op jit(solution)/shard_map/place/pallas_call | solution.py:99
  147.7 13.0 %fusion.91.proj_ref.edge_ref.halo_ref = f32[520,2432]{1,0:T(8,128)} fusion(f32[520,1024]{1,0:T(8,128)S(1)} %get-tuple-element.144, f32[1024,2432]{1,0:T(8,128)} %place.1), kind=kOutput, calls=%fused_computation.209 | convolution fusion | flops 7769948160 | bytes 17149952 | tf_op jit(solution)/shard_map/dot_general | solution.py:335
  162.6 11.6 %prepare.1 = (f32[512,2304]{1,0:T(8,128)}, f32[512,32]{1,0:T(8,128)S(1)}, f32[512,32]{1,0:T(8,128)S(1)}, f32[512,32]{1,0:T(8,128)S(1)}, f32[4,128,2048]{2,1,0:T(...) custom-call(f32[520,2432]{1,0:T(8,128)} %fusion.91.proj_ref.edge_ref.halo_ref, ...), custom_call_target="tpu_custom_call" | custom-call | tf_op jit(solution)/shard_map/prepare/pallas_call | solution.py:461
  179.1 11.0 %intra.1.inner_ref = f32[512,2048]{1,0:T(8,128)} custom-call(f32[512,2304]{1,0:T(8,128)} %get-tuple-element.116.act_ref, f32[512,32]{1,0:T(8,128)S(1)} %get-tuple-element.87.step_ref, f32[512,32]{1,0:T(8,128)S(1)} %get-tuple-element.83.logd_ref, f32[1,2048]{1,0:T(1,128)S(1)} %reshape_reshape.4.skip_ref, bf16[96,2048]{1,0:T(8,128)(2,1)S(1)} %fusion.31.spreader_ref), custom_call_target="tpu_custom_call" | custom-call | tf_op jit(solution)/shard_map/intra/pallas_call | solution.py:548
  194.6 5.1 fusion.93.gate_right_ref
  199.7 5.1 fusion.92.gate_left_ref
  210.8 5.0 slice.292
  215.9 8.8 %fusion.94.dng_ref = f32[512,2048]{1,0:T(8,128)} fusion(f32[512,1024]{1,0:T(8,128)S(1)} %maximum_multiply_fusion, f32[2048,1024]{1,0:T(8,128)S(1)} %bitcast.338), kind=kOutput, calls=%fused_computation.212 | convolution fusion | flops 6442450944 | bytes 14680064 | tf_op jit(solution)/shard_map/dot_general | solution.py:339
  224.7 28.5 %collective-permute-done.17 = f32[128,2048]{1,0:T(8,128)S(1)} collective-permute-done((f32[128,2048]{1,0:T(8,128)S(1)}, f32[128,2048]{1,0:T(8,128)S(1)}, u32[]{:S(2)}, u32[]{:S(2)}) %collective-permute-start.17) | collective-permute-done | bytes 1048608 | tf_op jit(solution)/shard_map/ppermute | solution.py:305
  253.4 17.0 %mixer.1 = (f32[512,2048]{1,0:T(8,128)}, f32[512,2048]{1,0:T(8,128)}, f32[512,2048]{1,0:T(8,128)}, f32[4,128,2048]{2,1,0:T(8,128)}, f32[8,2048]{1,0:T(8,128)S(1)}, /*index=5*/f32[8,2048]{1,0:T(8,128)S(1)}) custom-call(f32[512,2304]{1,0:T(8,128)} %get-tuple-element.116.act_ref, f32[512,32]{1,0:T(8,128)S(1)} %get-tuple-element.83.logd_ref, ...), custom_call_target="tpu_custom_call" | custom-call | tf_op jit(solution)/shard_map/mixer/pallas_call | solution.py:641
  275.2 5.1 fusion.95
  292.7 13.0 %right.1 = f32[512,1024]{1,0:T(8,128)} custom-call(f32[512,2048]{1,0:T(8,128)} %get-tuple-element.99.x_ref, f32[2048,1024]{1,0:T(8,128)} %bitcast.339, f32[512,1024]{1,0:T(8,128)} %pad_maximum_fusion.2.added_ref, f32[512,1]{1,0:T(8,128)S(1)} %fusion.68.scale_ref), custom_call_target="tpu_custom_call" | custom-call | tf_op jit(solution)/shard_map/right/pallas_call | solution.py:993
  319.1 5.3 fusion.14
  333.7 5.4 fusion.18
  339.2 15.1 %back_intra.1 = (f32[512,2048]{1,0:T(8,128)}, f32[512,256]{1,0:T(8,128)S(1)}, f32[512,32]{1,0:T(8,128)S(1)}) custom-call(f32[512,2304]{1,0:T(8,128)} %get-tuple-element.116.act_ref, f32[512,32]{1,0:T(8,128)S(1)} %get-tuple-element.87.step_ref, f32[512,32]{1,0:T(8,128)S(1)} %get-tuple-element.83.logd_ref, f32[512,2048]{1,0:T(8,128)} %get-tuple-element.107.dy_ref, ...), custom_call_target="tpu_custom_call" | custom-call | tf_op jit(solution)/shard_map/back_intra/pallas_call | solution.py:750
  370.1 5.6 collective-permute-done.18
  376.9 11.4 %right_back.1 = f32[512,1024]{1,0:T(8,128)} custom-call(f32[512,2048]{1,0:T(8,128)} %get-tuple-element.113.x_ref, f32[1024,1024]{1,0:T(8,128)} %bitcast.343, f32[1024,1024]{1,0:T(8,128)} %bitcast.341), custom_call_target="tpu_custom_call" | custom-call | tf_op jit(solution)/shard_map/right_back/pallas_call | solution.py:1018
  392.0 5.7 all-to-all-start
  400.4 31.2 %back.1 = (f32[520,2432]{1,0:T(8,128)}, f32[32,2304]{1,0:T(8,128)S(1)}, f32[8,2304]{1,0:T(8,128)S(1)}, f32[8,32]{1,0:T(8,128)S(1)}, f32[8,32]{1,0:T(8,128)S(1)}) custom-call(f32[512,2304]{1,0:T(8,128)} %get-tuple-element.116.act_ref, f32[512,32]{1,0:T(8,128)S(1)} %get-tuple-element.87.step_ref, f32[512,32]{1,0:T(8,128)S(1)} %get-tuple-element.117.slope_ref, ...), custom_call_target="tpu_custom_call" | custom-call | tf_op jit(solution)/shard_map/back/pallas_call | solution.py:928
  432.2 4.6 pad_dynamic-slice_fusion.3
  441.3 10.9 %maximum_add_fusion = f32[512,2432]{1,0:T(8,128)} fusion(f32[256,2432]{1,0:T(8,128)} %get-tuple-element.184, f32[256,2432]{1,0:T(8,128)} %get-tuple-element.183, f32[520,2432]{1,0:T(8,128)} %get-tuple-element.133, f32[520,256]{1,0:T(8,128)S(1)} %copy-done.44, f32[520,256]{1,0:T(8,128)} %copy-done.45), kind=kOutput, calls=%fused_computation.4 | convolution fusion | flops 3887730688 | bytes 16084992 | tf_op jit(solution)/shard_map/dot_general | solution.py:345
  457.5 9.9 %maximum_add_fusion.1 = f32[512,2432]{1,0:T(8,128)S(1)} fusion(f32[256,2432]{1,0:T(8,128)} %get-tuple-element.186, f32[256,2432]{1,0:T(8,128)} %get-tuple-element.185, f32[520,2432]{1,0:T(8,128)} %get-tuple-element.133, f32[520,256]{1,0:T(8,128)} %copy-done.42, f32[520,256]{1,0:T(8,128)S(1)} %copy-done.41), kind=kOutput, calls=%fused_computation.5 | convolution fusion | flops 3887730688 | bytes 16084992 | tf_op jit(solution)/shard_map/dot_general | solution.py:345
  479.6 5.1 all-to-all-start.1
  486.0 12.2 %fusion.96 = f32[520,1024]{1,0:T(8,128)S(1)} fusion(f32[520,2432]{1,0:T(8,128)} %get-tuple-element.133, f32[1024,2432]{1,0:T(8,128)} %place.1), kind=kOutput, calls=%fused_computation.214 | convolution fusion | flops 7769948160 | bytes 17149952 | tf_op jit(solution)/shard_map/dot_general | solution.py:339
  503.4 6.3 %collective-permute-done.32 = f32[8,1024]{1,0:T(8,128)S(1)} collective-permute-done((f32[8,1024]{1,0:T(8,128)S(1)}, f32[8,1024]{1,0:T(8,128)S(1)}, u32[]{:S(2)}, u32[]{:S(2)}) %collective-permute-start.32) | collective-permute-done | bytes 32800 | tf_op jit(solution)/shard_map/ppermute | solution.py:1172
  548.3 17.0 %collective-permute-done.44 = f32[32,2432]{1,0:T(8,128)S(1)} collective-permute-done((f32[32,2432]{1,0:T(8,128)S(1)}, f32[32,2432]{1,0:T(8,128)S(1)}, u32[]{:S(2)}, u32[]{:S(2)}) %collective-permute-start.44) | collective-permute-done | bytes 311328 | tf_op jit(solution)/shard_map/ppermute | solution.py:35
  565.3 4.7 collective-permute-done.45
  (360 shorter events, 193.3 us)
Async XLA Ops:
  7.2 182.9 %all-gather.3.cloned.1.call-start = ((), (), s32[]{:S(2)}) async-start(), calls=%async_computation.2 | async-start | bytes 17301504 | tf_op jit(solution)/shard_map/all_gather | solution.py:1073
  11.9 42.8 %collective-permute-start = (f32[256,1024]{1,0:T(8,128)}, f32[256,1024]{1,0:T(8,128)}, u32[]{:S(2)}, u32[]{:S(2)}) collective-permute-start(f32[256,1024]{1,0:T(8,128)} %dynamic-slice_bitcast_fusion.3), channel_id=1, source_target_pairs={{0,1},{1,0},{2,3},{3,2},{4,5},{5,4},{6,7},{7,6},{8,9},{9,8},{10,11... | collective-permute-start | bytes 3145736 | tf_op jit(solution)/shard_map/ppermute | solution.py:35
  15.2 37.5 %collective-permute-start.4 = (f32[32,2432]{1,0:T(8,128)S(1)}, f32[32,2432]{1,0:T(8,128)S(1)}, u32[]{:S(2)}, u32[]{:S(2)}) collective-permute-start(f32[32,2432]{1,0:T(8,128)S(1)} %pad_maximum_fusion.12), channel_id=1, source_target_pairs={{0,4},{2,6},{4,0},{6,2},{1,5},{3,7},{5,1},{7,3},{8,12},{10,14},{12... | collective-permute-start | bytes 933896 | tf_op jit(solution)/shard_map/ppermute | solution.py:35
  16.4 38.1 %collective-permute-start.5 = (f32[32,2432]{1,0:T(8,128)S(1)}, f32[32,2432]{1,0:T(8,128)S(1)}, u32[]{:S(2)}, u32[]{:S(2)}) collective-permute-start(f32[32,2432]{1,0:T(8,128)S(1)} %pad_maximum_fusion.12), channel_id=1, source_target_pairs={{0,6},{2,0},{4,2},{6,4},{1,7},{3,1},{5,3},{7,5},{8,14},{10,8},{12,... | collective-permute-start | bytes 933896 | tf_op jit(solution)/shard_map/ppermute | solution.py:35
  54.6 45.0 %collective-permute-start.6 = (f32[128,2432]{1,0:T(8,128)S(1)}, f32[128,2432]{1,0:T(8,128)S(1)}, u32[]{:S(2)}, u32[]{:S(2)}) collective-permute-start(f32[128,2432]{1,0:T(8,128)S(1)} %pad_maximum_fusion.7.refs_0_), channel_id=1, source_target_pairs={{0,1},{1,0},{2,3},{3,2},{4,5},{5,4},{6,7},{7,6},{8,9},{9,8},{10,11... | collective-permute-start | bytes 3735560 | tf_op jit(solution)/shard_map/ppermute | solution.py:35
  55.2 46.8 %collective-permute-start.7 = (f32[128,2432]{1,0:T(8,128)S(1)}, f32[128,2432]{1,0:T(8,128)}, u32[]{:S(2)}, u32[]{:S(2)}) collective-permute-start(f32[128,2432]{1,0:T(8,128)S(1)} %pad_maximum_fusion.7.refs_0_), channel_id=1, source_target_pairs={{0,16},{16,0},{1,17},{17,1},{2,18},{18,2},{3,19},{19,3},{4,20},{20... | collective-permute-start | bytes 3735560 | tf_op jit(solution)/shard_map/ppermute | solution.py:35
  58.2 46.2 %collective-permute-start.1 = (f32[8,1024]{1,0:T(8,128)}, f32[8,1024]{1,0:T(8,128)}, u32[]{:S(2)}, u32[]{:S(2)}) collective-permute-start(f32[8,1024]{1,0:T(8,128)} %get-tuple-element.177), channel_id=1, source_target_pairs={{1,2},{3,4},{5,6},{9,10},{11,12},{13,14},{17,18},{19,20},{21,22},{... | collective-permute-start | bytes 98312 | tf_op jit(solution)/shard_map/ppermute | solution.py:272
  59.4 45.4 %collective-permute-start.2 = (f32[8,1024]{1,0:T(8,128)}, f32[8,1024]{1,0:T(8,128)}, u32[]{:S(2)}, u32[]{:S(2)}) collective-permute-start(f32[8,1024]{1,0:T(8,128)} %get-tuple-element.176), channel_id=1, source_target_pairs={{1,3},{3,5},{5,7},{9,11},{11,13},{13,15},{17,19},{19,21},{21,23},{... | collective-permute-start | bytes 98312 | tf_op jit(solution)/shard_map/ppermute | solution.py:272
  104.0 27.7 %collective-permute-start.9 = (f32[64,2432]{1,0:T(8,128)}, f32[64,2432]{1,0:T(8,128)}, u32[]{:S(2)}, u32[]{:S(2)}) collective-permute-start(f32[64,2432]{1,0:T(8,128)} %slice.283), channel_id=1, source_target_pairs={{0,1},{1,0},{2,3},{3,2},{4,5},{5,4},{6,7},{7,6},{8,9},{9,8},{10,11... | collective-permute-start | bytes 1867784 | tf_op jit(solution)/shard_map/ppermute | solution.py:35
  104.2 33.9 %collective-permute-start.10 = (f32[128,2432]{1,0:T(8,128)S(1)}, f32[128,2432]{1,0:T(8,128)S(1)}, u32[]{:S(2)}, u32[]{:S(2)}) collective-permute-start(f32[128,2432]{1,0:T(8,128)S(1)} %pad_maximum_fusion.7.refs_0_), channel_id=1, source_target_pairs={{0,8},{8,0},{1,9},{9,1},{2,10},{10,2},{3,11},{11,3},{4,12},{12,4},... | collective-permute-start | bytes 3735560 | tf_op jit(solution)/shard_map/ppermute | solution.py:35
  104.3 33.8 %collective-permute-start.11 = (f32[128,2432]{1,0:T(8,128)S(1)}, f32[128,2432]{1,0:T(8,128)S(1)}, u32[]{:S(2)}, u32[]{:S(2)}) collective-permute-start(f32[128,2432]{1,0:T(8,128)S(1)} %collective-permute-done.6.refs_1_), channel_id=1, source_target_pairs={{0,8},{8,0},{1,9},{9,1},{2,10},{10,2},{3,11},{11,3},{4,12},{12,4},... | collective-permute-start | bytes 3735560 | tf_op jit(solution)/shard_map/ppermute | solution.py:35
  104.8 33.3 %collective-permute-start.12 = (f32[128,2432]{1,0:T(8,128)}, f32[128,2432]{1,0:T(8,128)S(1)}, u32[]{:S(2)}, u32[]{:S(2)}) collective-permute-start(f32[128,2432]{1,0:T(8,128)} %collective-permute-done.7.refs_2_), channel_id=1, source_target_pairs={{0,8},{8,0},{1,9},{9,1},{2,10},{10,2},{3,11},{11,3},{4,12},{12,4},... | collective-permute-start | bytes 3735560 | tf_op jit(solution)/shard_map/ppermute | solution.py:35
  138.1 52.0 %collective-permute-start.15 = (f32[256,1024]{1,0:T(8,128)}, f32[256,1024]{1,0:T(8,128)}, u32[]{:S(2)}, u32[]{:S(2)}) collective-permute-start(f32[256,1024]{1,0:T(8,128)} %dynamic-slice_bitcast_fusion.2), channel_id=1, source_target_pairs={{0,1},{1,0},{2,3},{3,2},{4,5},{5,4},{6,7},{7,6},{8,9},{9,8},{10,11... | collective-permute-start | bytes 3145736 | tf_op jit(solution)/shard_map/ppermute | solution.py:35
  177.0 28.6 %collective-permute-start.16 = (f32[136,2048]{1,0:T(8,128)}, f32[136,2048]{1,0:T(8,128)S(1)}, u32[]{:S(2)}, u32[]{:S(2)}) collective-permute-start(f32[136,2048]{1,0:T(8,128)} %pad_maximum_fusion.6), channel_id=1, source_target_pairs={{0,2},{2,4},{4,6},{1,3},{3,5},{5,7},{8,10},{10,12},{12,14},{9,11},... | collective-permute-start | bytes 3342344 | tf_op jit(solution)/shard_map/ppermute | solution.py:305
  207.4 45.9 %collective-permute-start.17 = (f32[128,2048]{1,0:T(8,128)S(1)}, f32[128,2048]{1,0:T(8,128)S(1)}, u32[]{:S(2)}, u32[]{:S(2)}) collective-permute-start(f32[128,2048]{1,0:T(8,128)S(1)} %multiply_add_fusion.4), channel_id=1, source_target_pairs={{0,4},{2,6},{1,5},{3,7},{8,12},{10,14},{9,13},{11,15},{16,20},{18,... | collective-permute-start | bytes 3145736 | tf_op jit(solution)/shard_map/ppermute | solution.py:305
  280.3 31.8 %collective-permute-start.20 = (f32[1024,1024]{1,0:T(8,128)}, f32[1024,1024]{1,0:T(8,128)}, u32[]{:S(2)}, u32[]{:S(2)}) collective-permute-start(f32[1024,1024]{1,0:T(8,128)} %fusion.95), channel_id=1, source_target_pairs={{0,8},{8,0},{1,9},{9,1},{2,10},{10,2},{3,11},{11,3},{4,12},{12,4},... | collective-permute-start | bytes 12582920 | tf_op jit(solution)/shard_map/ppermute | solution.py:35
  280.3 29.2 %collective-permute-start.19 = (f32[136,2048]{1,0:T(8,128)}, f32[136,2048]{1,0:T(8,128)}, u32[]{:S(2)}, u32[]{:S(2)}) collective-permute-start(f32[136,2048]{1,0:T(8,128)} %pad_maximum_fusion.5), channel_id=1, source_target_pairs={{2,0},{4,2},{6,4},{3,1},{5,3},{7,5},{10,8},{12,10},{14,12},{11,9},... | collective-permute-start | bytes 3342344 | tf_op jit(solution)/shard_map/ppermute | solution.py:305
  324.4 38.8 %collective-permute-start.23 = (f32[512,2048]{1,0:T(8,128)}, f32[512,2048]{1,0:T(8,128)}, u32[]{:S(2)}, u32[]{:S(2)}) collective-permute-start(f32[512,2048]{1,0:T(8,128)} %fusion.14), channel_id=1, source_target_pairs={{0,8},{8,0},{1,9},{9,1},{2,10},{10,2},{3,11},{11,3},{4,12},{12,4},... | collective-permute-start | bytes 12582920 | tf_op jit(solution)/shard_map/ppermute | solution.py:35
  327.0 28.1 %collective-permute-start.22 = (f32[2,2,64,1024]{3,2,0,1:T(8,128)}, f32[2,2,64,1024]{3,2,0,1:T(8,128)S(1)}, u32[]{:S(2)}, u32[]{:S(2)}) collective-permute-start(f32[2,2,64,1024]{3,2,0,1:T(8,128)} %fusion.25), channel_id=1, source_target_pairs={{0,16},{16,0},{1,17},{17,1},{2,18},{18,2},{3,19},{19,3},{4,20},{20... | collective-permute-start | bytes 3145736 | tf_op jit(solution)/shard_map/ppermute | solution.py:35
  327.0 28.1 %collective-permute-start.21 = (f32[2,2,64,1024]{3,2,1,0:T(8,128)}, f32[2,2,64,1024]{3,2,1,0:T(8,128)S(1)}, u32[]{:S(2)}, u32[]{:S(2)}) collective-permute-start(f32[2,2,64,1024]{3,2,1,0:T(8,128)} %fusion.23), channel_id=1, source_target_pairs={{0,1},{1,0},{2,3},{3,2},{4,5},{5,4},{6,7},{7,6},{8,9},{9,8},{10,11... | collective-permute-start | bytes 3145736 | tf_op jit(solution)/shard_map/ppermute | solution.py:35
  330.6 45.1 %collective-permute-start.18 = (f32[256,1024]{1,0:T(8,128)}, f32[256,1024]{1,0:T(8,128)}, u32[]{:S(2)}, u32[]{:S(2)}) collective-permute-start(f32[256,1024]{1,0:T(8,128)} %dynamic-slice_bitcast_fusion.1), channel_id=1, source_target_pairs={{0,1},{1,0},{2,3},{3,2},{4,5},{5,4},{6,7},{7,6},{8,9},{9,8},{10,11... | collective-permute-start | bytes 3145736 | tf_op jit(solution)/shard_map/ppermute | solution.py:35
  331.4 66.4 %collective-permute-start.26 = (f32[128,2048]{1,0:T(8,128)}, f32[128,2048]{1,0:T(8,128)}, u32[]{:S(2)}, u32[]{:S(2)}) collective-permute-start(f32[128,2048]{1,0:T(8,128)} %multiply_add_fusion.2), channel_id=1, source_target_pairs={{4,0},{6,2},{5,1},{7,3},{12,8},{14,10},{13,9},{15,11},{20,16},{22,... | collective-permute-start | bytes 3145736 | tf_op jit(solution)/shard_map/ppermute | solution.py:305
  358.8 29.5 %collective-permute-start.24 = (f32[2,64,1024]{2,1,0:T(8,128)S(1)}, f32[2,64,1024]{2,1,0:T(8,128)S(1)}, u32[]{:S(2)}, u32[]{:S(2)}) collective-permute-start(f32[2,64,1024]{2,1,0:T(8,128)S(1)} %fusion.53), channel_id=1, source_target_pairs={{0,16},{16,0},{1,17},{17,1},{2,18},{18,2},{3,19},{19,3},{4,20},{20... | collective-permute-start | bytes 1572872 | tf_op jit(solution)/shard_map/ppermute | solution.py:35
  362.0 26.3 %collective-permute-start.25 = (f32[2,64,1024]{2,1,0:T(8,128)S(1)}, f32[2,64,1024]{2,1,0:T(8,128)S(1)}, u32[]{:S(2)}, u32[]{:S(2)}) collective-permute-start(f32[2,64,1024]{2,1,0:T(8,128)S(1)} %fusion.51), channel_id=1, source_target_pairs={{0,1},{1,0},{2,3},{3,2},{4,5},{5,4},{6,7},{7,6},{8,9},{9,8},{10,11... | collective-permute-start | bytes 1572872 | tf_op jit(solution)/shard_map/ppermute | solution.py:35
  367.6 69.3 %collective-permute-start.28 = (f32[2,2,32,2048]{3,2,0,1:T(8,128)}, f32[2,2,32,2048]{3,2,0,1:T(8,128)}, u32[]{:S(2)}, u32[]{:S(2)}) collective-permute-start(f32[2,2,32,2048]{3,2,0,1:T(8,128)} %fusion.24), channel_id=1, source_target_pairs={{0,16},{16,0},{1,17},{17,1},{2,18},{18,2},{3,19},{19,3},{4,20},{20... | collective-permute-start | bytes 3145736 | tf_op jit(solution)/shard_map/ppermute | solution.py:35
  375.7 61.2 %collective-permute-start.27 = (f32[2,2,32,2048]{3,2,1,0:T(8,128)}, f32[2,2,32,2048]{3,2,1,0:T(8,128)}, u32[]{:S(2)}, u32[]{:S(2)}) collective-permute-start(f32[2,2,32,2048]{3,2,1,0:T(8,128)} %fusion.22), channel_id=1, source_target_pairs={{0,1},{1,0},{2,3},{3,2},{4,5},{5,4},{6,7},{7,6},{8,9},{9,8},{10,11... | collective-permute-start | bytes 3145736 | tf_op jit(solution)/shard_map/ppermute | solution.py:35
  392.0 49.2 %all-to-all-start = ((f32[4,64,1024]{2,1,0:T(8,128)}), f32[4,64,1024]{2,1,0:T(8,128)}, u32[]{:S(2)}, u32[]{:S(2)}) async-start(f32[4,64,1024]{2,1,0:T(8,128)} %pad_maximum_fusion.8), calls=%async_computation | async-start | bytes 2097152 | tf_op jit(solution)/shard_map/all_to_all | solution.py:230
  479.6 53.7 %all-to-all-start.1 = ((f32[4,32,2048]{2,1,0:T(8,128)}), f32[4,32,2048]{2,1,0:T(8,128)}, u32[]{:S(2)}, u32[]{:S(2)}) async-start(f32[4,32,2048]{2,1,0:T(8,128)} %pad_maximum_fusion.9), calls=%async_computation.1 | async-start | bytes 2097152 | tf_op jit(solution)/shard_map/all_to_all | solution.py:230
  484.7 28.9 %collective-permute-start.34 = (f32[2,2,32,2432]{3,2,0,1:T(8,128)}, f32[2,2,32,2432]{3,2,0,1:T(8,128)}, u32[]{:S(2)}, u32[]{:S(2)}) collective-permute-start(f32[2,2,32,2432]{3,2,0,1:T(8,128)} %fusion.7), channel_id=1, source_target_pairs={{0,16},{16,0},{1,17},{17,1},{2,18},{18,2},{3,19},{19,3},{4,20},{20... | collective-permute-start | bytes 3735560 | tf_op jit(solution)/shard_map/ppermute | solution.py:35
  484.7 28.9 %collective-permute-start.33 = (f32[2,2,32,2432]{3,2,1,0:T(8,128)}, f32[2,2,32,2432]{3,2,1,0:T(8,128)}, u32[]{:S(2)}, u32[]{:S(2)}) collective-permute-start(f32[2,2,32,2432]{3,2,1,0:T(8,128)} %fusion.6), channel_id=1, source_target_pairs={{0,1},{1,0},{2,3},{3,2},{4,5},{5,4},{6,7},{7,6},{8,9},{9,8},{10,11... | collective-permute-start | bytes 3735560 | tf_op jit(solution)/shard_map/ppermute | solution.py:35
  530.5 44.0 %collective-permute-start.35 = (f32[256,1024]{1,0:T(8,128)}, f32[256,1024]{1,0:T(8,128)}, u32[]{:S(2)}, u32[]{:S(2)}) collective-permute-start(f32[256,1024]{1,0:T(8,128)} %dynamic-slice_bitcast_fusion), channel_id=1, source_target_pairs={{0,1},{1,0},{2,3},{3,2},{4,5},{5,4},{6,7},{7,6},{8,9},{9,8},{10,11... | collective-permute-start | bytes 3145736 | tf_op jit(solution)/shard_map/ppermute | solution.py:35
  545.3 26.4 %collective-permute-start.46 = (f32[32,2432]{1,0:T(8,128)S(1)}, f32[32,2432]{1,0:T(8,128)S(1)}, u32[]{:S(2)}, u32[]{:S(2)}) collective-permute-start(f32[32,2432]{1,0:T(8,128)S(1)} %get-tuple-element.180), channel_id=1, source_target_pairs={{0,6},{2,0},{4,2},{6,4},{1,7},{3,1},{5,3},{7,5},{8,14},{10,8},{12,... | collective-permute-start | bytes 933896 | tf_op jit(solution)/shard_map/ppermute | solution.py:35
  (87 other events, 1382.4 us)
Sparse Core Ops, SparseCore 0:
  11.6 164.8 all-gather.2
